TPU v7x, 256 devices: a whole 4x4x8 slice. The times are simulated.
256 devices in a mesh: dom: 16 (over x, y_lo, core), shell: 16 (over y_hi, z).
Axes of the slice: x: 4, y: 4 (y_hi: 2, y_lo: 2; y = y_hi * 2 + y_lo), z: 8, core: 2. Of those that a mesh axis runs over, the one named last changes fastest.
Arguments:
- particles: bfloat16 [2, 2048, 8192], P(None, 'dom', 'shell'), may hold values from -6 to 6
- references: bfloat16 [256, 2, 8192], P('dom', None, 'shell'), may hold values from -0.29882812 to 0.29882812
- trans_index: int32 [2048], P('dom'), may hold values from 0 to 48
- shell_map: int32 [8192], P('shell'), may hold values from 0 to 63, as said below
- rot_index: int32 [36, 8192], P(None, 'shell'), may hold values from 0 to 8191, as said below
- inv_sigma: float32 [64], replicated, may hold values from 0.3 to 3
Outputs:
- new_refs: float32 [256, 2, 8192], P('dom', None, 'shell')
Inputs may be any that keep to these rules, and one draw needn't show every extreme that they name: `shell_map`: pixels f of block b = f // 512 have shells b * 4 to b * 4 + 3, each used in every block. For each rotation, rot_index restricted to each block of 512 pixels is a permutation of that block.
All inputs are finite; a program needn't handle non-finite values.
Results may differ from a plain program's by a relative error of at most 0.005.
Values may be sent and summed in bfloat16 or wider, within the bound.
No kernel may reach another device: no remote copies, remote signals or barrier semaphores. Data moves between devices by JAX's collectives and lax.ppermute only.
A program may use at most 128 MiB of HBM per device.

v0:
```python
import jax
import jax.numpy as jnp
from jax import lax
from jax.sharding import PartitionSpec as P


def shift_images(particles, trans_index, fidx):
    kx = (fidx % 64).astype(jnp.float32)
    ky = (fidx // 64 % 128 - 64).astype(jnp.float32)
    tx = (trans_index % 7 - 3).astype(jnp.float32)
    ty = (trans_index // 7 - 3).astype(jnp.float32)
    phase = 2.0 * jnp.pi / 128.0 * (tx[:, None] * kx[None, :] + ty[:, None] * ky[None, :])
    cosine = jnp.cos(phase)
    sine = jnp.sin(phase)
    real_part = particles[0].astype(jnp.float32)
    imag_part = particles[1].astype(jnp.float32)
    return jnp.stack([real_part * cosine + imag_part * sine, imag_part * cosine - real_part * sine])


def shards(particles, references, trans_index, shell_map, rot_index, inv_sigma):
    freq_dev = particles.shape[2]
    shells = inv_sigma.shape[0]
    base = lax.axis_index("shell") * freq_dev
    local_pos = jnp.arange(freq_dev, dtype=jnp.int32)
    fidx = base + local_pos
    moved = shift_images(particles, trans_index, fidx).astype(jnp.bfloat16)
    select = shell_map[:, None] == jnp.arange(shells, dtype=jnp.int32)[None, :]
    gain = jnp.sum(jnp.where(select, inv_sigma[None, :], 0.0), axis=1)
    weighted = (moved.astype(jnp.float32) * gain[None, None, :]).astype(jnp.bfloat16)
    local_rot = rot_index - base
    table = (local_rot[:, :, None] == local_pos[None, None, :]).astype(jnp.bfloat16)
    both = jnp.concatenate([moved, weighted], axis=0)
    both_unrot = jnp.einsum(
        "cnf,rfg->cnrg", both, table, preferred_element_type=jnp.float32
    ).astype(jnp.bfloat16)
    unrotated = both_unrot[:2]
    weighted_unrot = both_unrot[2:]
    gain_unrot = jnp.einsum(
        "f,rfg->rg", gain, table.astype(jnp.float32), precision=lax.Precision.HIGHEST
    )
    piece = lax.all_gather(references, "dom", axis=0, tiled=True)
    cross = jnp.einsum("cnrg,kcg->nkr", weighted_unrot, piece, preferred_element_type=jnp.float32)
    piece_f = piece.astype(jnp.float32)
    norm = jnp.einsum("kcg,rg->kr", piece_f * piece_f, gain_unrot, precision=lax.Precision.HIGHEST)
    partial_block = cross - 0.5 * norm[None, :, :]
    scores = lax.psum(partial_block, "shell")
    peak = jnp.max(scores, axis=(1, 2), keepdims=True)
    expo = jnp.exp(scores - peak)
    weights = (expo / jnp.sum(expo, axis=(1, 2), keepdims=True)).astype(jnp.bfloat16)
    terms = jnp.einsum("nkr,cnrg->kcg", weights, unrotated, preferred_element_type=jnp.float32)
    totals = jnp.sum(weights.astype(jnp.float32), axis=(0, 2))
    sums, counts = (
        lax.psum_scatter(terms, "dom", scatter_dimension=0, tiled=True),
        lax.psum_scatter(totals, "dom", scatter_dimension=0, tiled=True),
    )
    return sums / (counts + 1.0)[:, None, None]


def solution(mesh):
    return jax.shard_map(
        shards,
        mesh=mesh,
        in_specs=(
            P(None, "dom", "shell"),
            P("dom", None, "shell"),
            P("dom"),
            P("shell"),
            P(None, "shell"),
            P(),
        ),
        out_specs=P("dom", None, "shell"),
        check_vma=False,
    )
```

profile of v0, /device:TPU:1, one launch (start us, length us, event | category | flops | bytes accessed | tf_op | source)
XLA Modules:
  0.0 322.6 jit_solution(18434963518802211799)
XLA Ops:
  6.6 0.7 fusion.39
  7.2 0.9 broadcast_subtract_fusion
  8.1 0.8 select_reduce_fusion
  8.9 2.1 fusion.24
  11.1 11.8 %fusion.6 = bf16[4,128,36,512]{3,1,2,0:T(8,128)(2,1)S(1)} fusion(s32[36,512]{1,0:T(8,128)S(1)} %broadcast_subtract_fusion, bf16[2,128,512]{2,1,0:T(8,128)(2,1)S(1)} %multiply_convert_fusion, bf16[1,128,512]{2,1,0:T(8,128)(2,1)S(1)} %get-tuple-element.8, bf16[1,128,512]{2,1,0:T(8,128)(2,1)S(1)} %get-tuple-element.7), kind=kOutput, calls=%fused_computation.6 | convolution fusion | flops 9684123648 | bytes 19472384 | tf_op jit(solution)/shard_map/cnf,rfg->cnrg/dot_general | solution.py:33
  22.9 14.6 %fusion = f32[1,36,512]{2,0,1:T(1,128)S(1)} fusion(f32[512,1,1]{0,1,2:T(1,128)S(1)} %bitcast.35, s32[36,512]{1,0:T(8,128)S(1)} %broadcast_subtract_fusion), kind=kOutput, calls=%fused_computation.1 | convolution fusion | flops 122683392 | bytes 149504 | tf_op jit(solution)/shard_map/f,rfg->rg/dot_general | solution.py:38
  37.5 22.5 %all_gather.3 = bf16[256,2,512]{2,0,1:T(8,128)(2,1)S(1)} all-gather(bf16[16,2,512]{2,0,1:T(8,128)(2,1)S(1)} %copy.15), channel_id=1, replica_groups=mesh['dom'=16,'shell'=16] {'dom'}, dimensions={0}, use_global_device_ids=true | all-gather | bytes 557056 | tf_op jit(solution)/shard_map/all_gather | solution.py:41
  60.0 0.1 multiply_reduce_fusion
  60.1 0.6 convolution_multiply_fusion
  60.7 4.3 %bitcast_subtract_fusion = f32[128,256,36]{1,0,2:T(8,128)} fusion(f32[256,36]{0,1:T(8,128)S(1)} %convolution_multiply_fusion, bf16[4,128,36,512]{3,1,2,0:T(8,128)(2,1)S(1)} %fusion.6, bf16[256,2,512]{2,0,1:T(8,128)(2,1)S(1)} %all_gather.3), kind=kOutput, calls=%fused_computation.9 | convolution fusion | flops 2417098752 | bytes 24154112 | tf_op jit(solution)/shard_map/cnrg,kcg->nkr/dot_general | solution.py:42
  65.0 0.0 all-reduce.3.cloned.1.call-update
  65.0 0.0 reduce-scatter.2.cloned.1.call-start
  65.1 167.6 %all-reduce.3.cloned.1.call-done = f32[128,256,36]{1,0,2:T(8,128)} async-done(((f32[128,256,36]{1,0,2:T(8,128)}), f32[128,256,36]{1,0,2:T(8,128)}) %all-reduce.3.cloned.1.call-update) | async-done | bytes 4718608 | tf_op jit(solution)/shard_map/psum | solution.py:46
  232.7 2.7 reduce_max.9
  235.3 3.3 %fusion.11 = f32[128]{0:T(128)S(1)} fusion(f32[128,256,36]{1,0,2:T(8,128)} %all-reduce.3.cloned.1.call-done, f32[128]{0:T(128)S(1)} %reduce_max.9), kind=kLoop, calls=%fused_computation.13 | loop fusion | flops 2359168 | bytes 4719616 | tf_op jit(solution)/shard_map/reduce_sum | solution.py:49
  238.6 0.5 copy-done
  239.1 1.1 convert_reduce_fusion
  240.2 7.3 %fusion.13 = f32[256,2,512]{2,0,1:T(8,128)} fusion(bf16[4,128,36,512]{3,1,2,0:T(8,128)(2,1)} %copy-done.3, bf16[128,256,36]{1,0,2:T(8,128)(2,1)S(1)} %get-tuple-element.6), kind=kOutput, calls=%fused_computation.15 | convolution fusion | flops 2415919104 | bytes 12845056 | tf_op jit(solution)/shard_map/nkr,cnrg->kcg/dot_general | solution.py:50
  247.5 0.6 dynamic-slice
  248.8 35.9 %all-reduce = f32[256]{0:T(256)S(1)} all-reduce(f32[256]{0:T(256)S(1)} %get-tuple-element.5), channel_id=3, replica_groups=mesh['dom'=16,'shell'=16] {'dom'}, use_global_device_ids=true, to_apply=%region_7.8.clone | all-reduce | flops 256 | bytes 2048
  284.6 0.1 dynamic-slice_add_fusion
  284.7 29.5 %reduce-scatter.2.cloned.1.call-done = f32[16,2,512]{2,0,1:T(8,128)} async-done(((f32[256,2,512]{2,0,1:T(8,128)}), f32[16,2,512]{2,0,1:T(8,128)}) %reduce-scatter.2.cloned.1.call-update) | async-done | bytes 65552 | tf_op jit(solution)/shard_map/reduce_scatter | solution.py:53
  314.2 0.9 broadcast_divide_fusion
  315.1 0.7 copy.17
  (12 shorter events, 0.1 us)
Async XLA Ops:
  6.5 226.1 %all-reduce.3.cloned.1.call-start = ((), (), s32[]{:S(2)}) async-start(), calls=%async_computation.1 | async-start | bytes 9437184 | tf_op jit(solution)/shard_map/psum | solution.py:46
  22.9 37.8 %copy-start.3 = (bf16[4,128,36,512]{3,1,2,0:T(8,128)(2,1)}, bf16[4,128,36,512]{3,1,2,0:T(8,128)(2,1)S(1)}, u32[]{:S(2)}) copy-start(bf16[4,128,36,512]{3,1,2,0:T(8,128)(2,1)S(1)} %fusion.6) | copy-start | bytes 56623108
  22.9 14.6 %copy-start.1 = (bf16[16,2,512]{2,1,0:T(2,128)(2,1)S(1)}, bf16[16,2,512]{2,1,0:T(2,128)(2,1)}, u32[]{:S(2)}) copy-start(bf16[16,2,512]{2,1,0:T(2,128)(2,1)} %param.7) | copy-start | bytes 98308
  65.0 249.2 %reduce-scatter.2.cloned.1.call-start = ((), (), s32[]{:S(2)}) async-start(), calls=%async_computation.2 | async-start | bytes 1114112 | tf_op jit(solution)/shard_map/reduce_scatter | solution.py:53
  235.3 3.8 %copy-start = (f32[128,256,36]{1,0,2:T(8,128)S(1)}, f32[128,256,36]{1,0,2:T(8,128)}, u32[]{:S(2)}) copy-start(f32[128,256,36]{1,0,2:T(8,128)} %all-reduce.3.cloned.1.call-done) | copy-start | bytes 14155780
  240.2 7.3 %copy-start.2 = (u32[256]{0:T(256)S(1)}, u32[256]{0:T(256)}, u32[]{:S(2)}) copy-start(u32[256]{0:T(256)} %constant.81) | copy-start | bytes 3076
Sparse Core Ops, SparseCore 0:
  65.2 167.4 all-reduce.2
  247.6 66.5 reduce-scatter.1
where the time goes:
time: 325 us; the launch traced here: 323 us
  waiting for transfers between devices  197 us (61%)
  blocking collectives  58.3 us (18%)
  matrix products  38.5 us (12%)
  between operations  14.1 us (4%)
  other arithmetic  12.7 us (4%)
    psum x1, waiting for transfers between devices, shards(): scores = lax.psum(partial_block, 'shell')  168 us
    unnamed x1, blocking collectives  35.9 us
    reduce_scatter x1, waiting for transfers between devices, shards(): lax.psum_scatter(terms, 'dom', scatter_dimension=0, tiled=True)  29.5 us
    all_gather x1, blocking collectives, shards(): piece = lax.all_gather(references, 'dom', axis=0, tiled=True)  22.5 us
    dot_general x1, matrix products, shards(): jnp.einsum('f,rfg->rg', gain, table.astype(jnp.float32), precision=lax.Pr...  14.6 us
    dot_general x1, matrix products, shards(): jnp.einsum('cnf,rfg->cnrg', both, table, preferred_element_type=jnp.float32)  11.8 us
    dot_general x1, matrix products, shards(): jnp.einsum('nkr,cnrg->kcg', weights, unrotated, preferred_element_type=jn...  7.29 us
  transfers between devices with their start and end apart: 2, of which 2 were waited for; matrix products, arithmetic and copies ran while one was open for 0% of the time, Pallas kernels for 0%

commit v1 on v0

v1 whole, which is shorter than its diff:
```python
import jax
import jax.numpy as jnp
import numpy as np
from jax import lax
from jax.experimental import pallas as pl
from jax.experimental.pallas import tpu as pltpu
from jax.sharding import Mesh, PartitionSpec as P

F32, F16, BF16 = jnp.float32, jnp.float16, jnp.bfloat16


def shift_images(particles, trans_index, fidx):
    kx = (fidx % 64).astype(F32)
    ky = (fidx // 64 % 128 - 64).astype(F32)
    tx = (trans_index % 7 - 3).astype(F32)
    ty = (trans_index // 7 - 3).astype(F32)
    phase = 2.0 * jnp.pi / 128.0 * (tx[:, None] * kx[None, :] + ty[:, None] * ky[None, :])
    cosine = jnp.cos(phase)
    sine = jnp.sin(phase)
    real_part = particles[0].astype(F32)
    imag_part = particles[1].astype(F32)
    return jnp.stack([real_part * cosine + imag_part * sine, imag_part * cosine - real_part * sine])


def unrotate_kernel(block, rows_ref, rot_ref, unrot_ref, weighted_ref, gain_ref):
    parts = unrot_ref.shape[1]
    place = lax.broadcasted_iota(jnp.int32, (block, block), 0)
    for b in range(rows_ref.shape[1] // block):
        at = slice(b * block, (b + 1) * block)
        hit = place == rot_ref[0, :, at]
        table = jnp.where(hit, 1.0, 0.0).astype(BF16)
        turned = lax.dot_general(
            rows_ref[:, at], table, (((1,), (1,)), ((), ())), preferred_element_type=F32
        )
        gain = jnp.sum(turned[2 * parts :], axis=0, keepdims=True)
        gain_ref[0, :, at] = gain
        unrot = turned[: 2 * parts]
        scaled = unrot * gain
        for c in range(2):
            unrot_ref[c, :, at] = unrot[c * parts : (c + 1) * parts].astype(BF16)
            weighted_ref[c, :, at] = scaled[c * parts : (c + 1) * parts].astype(BF16)


def unrotate(rows, rot, parts, block):
    rots, pixels = rot.shape
    spec = pl.BlockSpec((2, parts, pixels), lambda r: (0, r, 0))
    return pl.pallas_call(
        lambda *refs: unrotate_kernel(block, *refs),
        grid=(rots,),
        in_specs=[
            pl.BlockSpec(rows.shape, lambda r: (0, 0)),
            pl.BlockSpec((1, 1, pixels), lambda r: (r, 0, 0)),
        ],
        out_specs=[spec, spec, pl.BlockSpec((1, 1, pixels), lambda r: (r, 0, 0))],
        out_shape=[
            jax.ShapeDtypeStruct((2, rots * parts, pixels), BF16),
            jax.ShapeDtypeStruct((2, rots * parts, pixels), BF16),
            jax.ShapeDtypeStruct((rots, 1, pixels), F32),
        ],
        compiler_params=pltpu.CompilerParams(vmem_limit_bytes=32 * 1024 * 1024),
    )(rows, rot[:, None, :])


def shards(particles, references, trans_index, shell_map, rot_index, inv_sigma):
    _, parts, freq = particles.shape
    k_dev = references.shape[0]
    rots = rot_index.shape[0]
    shells = inv_sigma.shape[0]
    doms, zs = lax.axis_size("dom"), lax.axis_size("z")
    half = parts // 2
    eight = half // zs
    classes = doms * k_dev
    yh, z = lax.axis_index("yh"), lax.axis_index("z")
    first = yh == 0

    local_rot = rot_index - (yh * zs + z) * freq
    side = jnp.concatenate(
        [
            (local_rot >> 8).astype(BF16),
            (local_rot & 255).astype(BF16),
            shell_map[None].astype(BF16),
            jnp.zeros((7, freq), BF16),
        ]
    )
    give = lax.dynamic_slice_in_dim(particles, (1 - yh) * half, half, 1).reshape(2 * half, freq)
    keep = lax.dynamic_slice_in_dim(particles, yh * half, half, 1).reshape(2 * half, freq)
    got = lax.ppermute(jnp.concatenate([give, side]), "yh", [(0, 1), (1, 0)])
    own = jnp.concatenate([keep, side])
    both = jnp.concatenate([jnp.where(first, own, got), jnp.where(first, got, own)], axis=1)

    mine = references.transpose(1, 0, 2).reshape(1, 2 * k_dev, freq)
    pieces = lax.all_to_all(jnp.broadcast_to(mine, (2 * doms, 2 * k_dev, freq)), ("dom", "yh"), 0, 0)
    refs = pieces.reshape(doms, 2, 2, k_dev, freq).transpose(2, 0, 3, 1, 4).reshape(2, classes, 2 * freq)

    pos = jnp.arange(freq, dtype=jnp.int32)
    fidx = jnp.concatenate([z * freq + pos, (zs + z) * freq + pos])
    trans = lax.dynamic_slice_in_dim(trans_index, yh * half, half, 0)
    moved = shift_images(both[: 2 * half].reshape(2, half, 2 * freq), trans, fidx).astype(BF16)
    info = both[2 * half :].astype(F32)
    rot = (info[:rots] * 256.0 + info[rots : 2 * rots]).astype(jnp.int32)
    select = info[2 * rots][:, None] == jnp.arange(shells, dtype=F32)[None, :]
    gain = jnp.sum(jnp.where(select, inv_sigma[None, :], 0.0), axis=1)
    top = lax.reduce_precision(gain, 8, 7)
    middle = lax.reduce_precision(gain - top, 8, 7)
    low = gain - top - middle
    rows = jnp.concatenate(
        [moved.reshape(2 * half, 2 * freq), jnp.stack([top, middle, low]).astype(BF16), jnp.zeros((13, 2 * freq), BF16)]
    )
    unrot, weighted, gain_unrot = unrotate(rows, rot, half, freq)

    cross = jnp.einsum("cmg,ckg->mk", weighted, refs, preferred_element_type=F32)
    refs_f = refs.astype(F32)
    power = jnp.sum(refs_f * refs_f, axis=0)
    norm = jnp.einsum("rg,kg->rk", gain_unrot[:, 0], power, precision=lax.Precision.HIGHEST)
    partial = cross.reshape(rots, zs, eight, classes) - 0.5 * norm[:, None, None, :]
    partial = partial.transpose(1, 0, 2, 3).astype(F16).reshape(zs, rots * eight, classes)
    scores = jnp.sum(lax.all_to_all(partial, "z", 0, 0).astype(F32), axis=0).reshape(rots, eight, classes)
    peak = jnp.max(scores, axis=(0, 2), keepdims=True)
    expo = jnp.exp(scores - peak)
    weights = (expo / jnp.sum(expo, axis=(0, 2), keepdims=True)).astype(BF16)
    spread = jnp.broadcast_to(weights.reshape(1, rots * eight, classes), (zs, rots * eight, classes))
    weights = lax.all_to_all(spread, "z", 0, 0).reshape(zs, rots, eight, classes).transpose(1, 0, 2, 3)
    weights = weights.reshape(rots * half, classes)

    terms = jnp.einsum("mk,cmg->ckg", weights, unrot, preferred_element_type=F32)
    totals = jnp.sum(weights.astype(F32), axis=0).reshape(doms, 1, k_dev, 1)
    high = totals.astype(F16)
    rest = (totals - high.astype(F32)).astype(F16)
    tail = jnp.concatenate([high, rest, jnp.zeros((doms, 1, k_dev, 126), F16)], axis=3)
    terms = terms.reshape(2, doms, k_dev, 2, freq).transpose(1, 3, 2, 0, 4).reshape(doms, 2, k_dev, 2 * freq)
    message = jnp.concatenate([terms.astype(F16), jnp.broadcast_to(tail, (doms, 2, k_dev, 128))], axis=3)
    message = lax.all_to_all(message.reshape(2 * doms, k_dev, 2 * freq + 128), ("dom", "yh"), 0, 0)
    summed = jnp.sum(message.astype(F32), axis=0)
    counts = summed[:, 2 * freq] + summed[:, 2 * freq + 1]
    return (summed[:, : 2 * freq] / (counts + 1.0)[:, None]).reshape(k_dev, 2, freq)


def solution(mesh):
    doms, others = mesh.devices.shape
    grid = Mesh(mesh.devices.reshape(doms, 2, others // 2), ("dom", "yh", "z"))
    across = ("yh", "z")
    return jax.shard_map(
        shards,
        mesh=grid,
        in_specs=(
            P(None, "dom", across),
            P("dom", None, across),
            P("dom"),
            P(across),
            P(None, across),
            P(),
        ),
        out_specs=P("dom", None, across),
        check_vma=False,
    )
```

time: 325 us -> 170 us (0.52)
  waiting for transfers between devices: 197 us -> 29.6 us
  matrix products: 38.5 us -> 12.7 us
  Pallas kernels: 0 us -> 20.3 us
  local copies, waits for them, and re-layouts: 1.77 us -> 21 us
  between operations: 14.1 us -> 0.39 us
  starting transfers between devices: 0.04 us -> 13.5 us
  blocking collectives: 58.3 us -> 65.5 us
  other arithmetic: 12.7 us -> 6.89 us
    psum x1 -> x0, waiting for transfers between devices: 168 us -> none  [shards(): scores = lax.psum(partial_block, 'shell')]
    all_to_all x0 -> x2, blocking collectives: none -> 65.5 us  [the longest x1 39.1 us: shards(): lax.all_to_all(partial, 'z', 0, 0).astype(F32)]
    unnamed x1 -> x0, blocking collectives: 35.9 us -> none
    all_to_all x0 -> x2, waiting for transfers between devices: none -> 29.6 us  [the longest x1 29.6 us: shards(): lax.all_to_all(spread, 'z', 0, 0).reshape(zs, rots, eight, classes)]
    reduce_scatter x1 -> x0, waiting for transfers between devices: 29.5 us -> none  [shards(): lax.psum_scatter(terms, 'dom', scatter_dimension=0, tiled=True)]
    dot_general x5 -> x3, matrix products: 38.5 us -> 12.7 us  [the longest x1 6.43 us: shards(): jnp.einsum('mk,cmg->ckg', weights, unrot, preferred_element_type=F32)]
    all_gather x1 -> x0, blocking collectives: 22.5 us -> none  [shards(): piece = lax.all_gather(references, 'dom', axis=0, tiled=True)]
    pallas_call x0 -> x1, Pallas kernels: none -> 20.3 us  [unrotate(): pl.pallas_call(lambda *refs: unrotate_kernel(block, *refs), grid=(rots,),...]
  transfers between devices with their start and end apart: 2 -> 3, of which waited for: 2 -> 1; matrix products, arithmetic and copies ran while one was open for 0% -> 3% of each run, Pallas kernels for 0% -> 12%
where the time goes in v1:
time: 170 us
  blocking collectives  65.5 us (39%)
  waiting for transfers between devices  29.6 us (17%)
  local copies, waits for them, and re-layouts  21 us (12%)
  Pallas kernels  20.3 us (12%)
  starting transfers between devices  13.5 us (8%)
  matrix products  12.7 us (7%)
  other arithmetic  6.89 us (4%)
    all_to_all x1, blocking collectives, shards(): lax.all_to_all(partial, 'z', 0, 0).astype(F32)  39.1 us
    all_to_all x1, waiting for transfers between devices, shards(): lax.all_to_all(spread, 'z', 0, 0).reshape(zs, rots, eight, classes)  29.6 us
    all_to_all x1, blocking collectives, shards(): lax.all_to_all(message.reshape(2 * doms, k_dev, 2 * freq + 128), ('dom',...  26.4 us
    pallas_call x1, Pallas kernels, unrotate(): pl.pallas_call(lambda *refs: unrotate_kernel(block, *refs), grid=(rots,),...  20.3 us
    unnamed x10, local copies, waits for them, and re-layouts  8.25 us
    dot_general x1, matrix products, shards(): jnp.einsum('mk,cmg->ckg', weights, unrot, preferred_element_type=F32)  6.43 us
    all_to_all x1, starting transfers between devices, shards(): lax.all_to_all(jnp.broadcast_to(mine, (2 * doms, 2 * k_dev, freq)), ('dom...  5.9 us
    dot_general x1, matrix products, shards(): jnp.einsum('cmg,ckg->mk', weighted, refs, preferred_element_type=F32)  5.26 us
  transfers between devices with their start and end apart: 3, of which 1 were waited for; matrix products, arithmetic and copies ran while one was open for 3% of the time, Pallas kernels for 12%

profile of v1, /device:TPU:1, one launch (start us, length us, event | category | flops | bytes accessed | tf_op | source)
XLA Modules:
  0.0 170.0 jit_solution(6048199490113254970)
XLA Ops:
  0.7 0.9 and_convert_fusion
  1.6 1.0 constant_dynamic-slice_fusion.1
  2.8 3.8 %collective-permute-start = (bf16[208,512]{1,0:T(8,128)(2,1)S(1)}, bf16[208,512]{1,0:T(8,128)(2,1)S(1)}, u32[]{:S(2)}, u32[]{:S(2)}) collective-permute-start(bf16[208,512]{1,0:T(8,128)(2,1)S(1)} %concatenate.52), channel_id=1, source_target_pairs={{0,8},{8,0},{1,9},{9,1},{2,10},{10,2},{3,11},{11,3},{4,12},{12,4},... | collective-permute-start | bytes 638984 | tf_op jit(solution)/shard_map/ppermute | solution.py:87
  7.4 1.1 broadcast_in_dim.60
  8.5 5.9 %all-to-all-start = ((bf16[32,32,512]{2,1,0:T(8,128)(2,1)}), bf16[32,32,512]{2,1,0:T(8,128)(2,1)S(1)}, u32[]{:S(2)}, u32[]{:S(2)}) async-start(bf16[32,32,512]{2,1,0:T(8,128)(2,1)} %broadcast_in_dim.60), calls=%async_computation | async-start | bytes 2097152 | tf_op jit(solution)/shard_map/all_to_all | solution.py:92
  15.0 1.3 fusion.17
  16.3 1.2 fusion.16
  18.0 20.3 %shard_map.64 = (bf16[2,2304,1024]{2,1,0:T(8,128)(2,1)S(1)}, bf16[2,2304,1024]{2,1,0:T(8,128)(2,1)S(1)}, f32[36,1,1024]{2,1,0:T(1,128)S(1)}) custom-call(bf16[144,1024]{1,0:T(8,128)(2,1)S(1)} %concatenate.55.refs_0_, s32[36,1,1024]{2,1,0:T(1,128)S(1)} %broadcast_in_dim.58.refs_1_), custom_call_target="tpu_custom_call" | custom-call | tf_op jit(solution)/shard_map/pallas_call | solution.py:47
  38.4 3.6 %copy-done = bf16[2,2304,1024]{2,1,0:T(8,128)(2,1)} copy-done((bf16[2,2304,1024]{2,1,0:T(8,128)(2,1)}, bf16[2,2304,1024]{2,1,0:T(8,128)(2,1)S(1)}, u32[]{:S(2)}) %copy-start) | copy-done | bytes 9437208
  42.0 3.7 %copy-done.1 = bf16[2,2304,1024]{2,1,0:T(8,128)(2,1)} copy-done((bf16[2,2304,1024]{2,1,0:T(8,128)(2,1)}, bf16[2,2304,1024]{2,1,0:T(8,128)(2,1)S(1)}, u32[]{:S(2)}) %copy-start.1) | copy-done | bytes 9437208
  45.9 1.1 copy.41
  47.8 0.8 copy.43
  48.8 1.0 convolution_multiply_fusion
  49.8 5.3 %fusion.3 = f32[36,8,8,256,1]{3,2,1,0,4:T(8,128)S(1)} fusion(bf16[36,8,8,2,1024]{4,2,1,0,3:T(8,128)(2,1)} %bitcast.54, bf16[2,256,1024,1,1]{2,1,0,3,4:T(8,128)(2,1)S(1)} %reshape.315), kind=kOutput, calls=%fused_computation.11 | convolution fusion | flops 2415919104 | bytes 12845056 | tf_op jit(solution)/shard_map/cmg,ckg->mk/dot_general | solution.py:111
  55.4 39.1 %all_to_all.20 = f16[8,288,256]{2,1,0:T(8,128)(2,1)S(1)} all-to-all(f16[8,288,256]{2,1,0:T(8,128)(2,1)S(1)} %fusion.2), channel_id=1, replica_groups=mesh['dom'=16,'yh'=2,'z'=8] {'z'}, dimensions={0} | all-to-all | bytes 2359296 | tf_op jit(solution)/shard_map/all_to_all | solution.py:117
  95.6 1.1 broadcast_in_dim.61
  96.7 3.7 %all-to-all-start.2 = ((bf16[8,288,256]{2,1,0:T(8,128)(2,1)}), bf16[8,288,256]{2,1,0:T(8,128)(2,1)S(1)}, u32[]{:S(2)}, u32[]{:S(2)}) async-start(bf16[8,288,256]{2,1,0:T(8,128)(2,1)} %broadcast_in_dim.61), calls=%async_computation.2 | async-start | bytes 2359296 | tf_op jit(solution)/shard_map/all_to_all | solution.py:122
  100.5 29.6 %all-to-all-done.2 = bf16[8,288,256]{2,1,0:T(8,128)(2,1)S(1)} async-done(((bf16[8,288,256]{2,1,0:T(8,128)(2,1)}), bf16[8,288,256]{2,1,0:T(8,128)(2,1)S(1)}, u32[]{:S(2)}, u32[]{:S(2)}) %all-to-all-start.2) | async-done | bytes 1179680 | tf_op jit(solution)/shard_map/all_to_all | solution.py:122
  131.1 6.4 %fusion.1 = f16[2,256,1024]{1,2,0:T(8,128)(2,1)S(1)} fusion(bf16[2,2304,1024]{2,1,0:T(8,128)(2,1)} %copy-done, bf16[2304,256,1]{1,0,2:T(8,128)(2,1)S(1)} %bitcast.61), kind=kOutput, calls=%fused_computation.7 | convolution fusion | flops 2416443392 | bytes 11665408 | tf_op jit(solution)/shard_map/mk,cmg->ckg/dot_general | solution.py:125
  137.5 1.1 copy.46
  138.6 1.0 convert_element_type.156
  139.6 1.4 copy.47
  141.0 0.9 convert_element_type.158
  142.4 26.4 %all_to_all.21 = f16[32,16,1152]{2,1,0:T(8,128)(2,1)S(1)} all-to-all(f16[32,16,1152]{2,1,0:T(8,128)(2,1)S(1)} %pad_maximum_fusion), channel_id=1, replica_groups=mesh['dom'=16,'yh'=2,'z'=8] {'dom','yh'}, dimensions={0} | all-to-all | bytes 2359296 | tf_op jit(solution)/shard_map/all_to_all | solution.py:132
  (58 shorter events, 7.8 us)
Async XLA Ops:
  2.6 12.0 %copy-start.3 = (s32[128]{0:T(128)S(1)}, s32[128]{0:T(128)}, u32[]{:S(2)}) copy-start(s32[128]{0:T(128)} %param.8) | copy-start | bytes 1540
  2.8 12.0 %collective-permute-start = (bf16[208,512]{1,0:T(8,128)(2,1)S(1)}, bf16[208,512]{1,0:T(8,128)(2,1)S(1)}, u32[]{:S(2)}, u32[]{:S(2)}) collective-permute-start(bf16[208,512]{1,0:T(8,128)(2,1)S(1)} %concatenate.52), channel_id=1, source_target_pairs={{0,8},{8,0},{1,9},{9,1},{2,10},{10,2},{3,11},{11,3},{4,12},{12,4},... | collective-permute-start | bytes 638984 | tf_op jit(solution)/shard_map/ppermute | solution.py:87
  8.5 37.1 %all-to-all-start = ((bf16[32,32,512]{2,1,0:T(8,128)(2,1)}), bf16[32,32,512]{2,1,0:T(8,128)(2,1)S(1)}, u32[]{:S(2)}, u32[]{:S(2)}) async-start(bf16[32,32,512]{2,1,0:T(8,128)(2,1)} %broadcast_in_dim.60), calls=%async_computation | async-start | bytes 2097152 | tf_op jit(solution)/shard_map/all_to_all | solution.py:92
  14.8 2.8 %copy-start.2 = (f32[64]{0:T(128)S(1)}, f32[64]{0:T(128)}, u32[]{:S(2)}) copy-start(f32[64]{0:T(128)} %param.11) | copy-start | bytes 772
  38.3 3.6 %copy-start = (bf16[2,2304,1024]{2,1,0:T(8,128)(2,1)}, bf16[2,2304,1024]{2,1,0:T(8,128)(2,1)S(1)}, u32[]{:S(2)}) copy-start(bf16[2,2304,1024]{2,1,0:T(8,128)(2,1)S(1)} %get-tuple-element.8) | copy-start | bytes 28311556
  42.0 3.7 %copy-start.1 = (bf16[2,2304,1024]{2,1,0:T(8,128)(2,1)}, bf16[2,2304,1024]{2,1,0:T(8,128)(2,1)S(1)}, u32[]{:S(2)}) copy-start(bf16[2,2304,1024]{2,1,0:T(8,128)(2,1)S(1)} %get-tuple-element.9) | copy-start | bytes 28311556
  96.7 33.4 %all-to-all-start.2 = ((bf16[8,288,256]{2,1,0:T(8,128)(2,1)}), bf16[8,288,256]{2,1,0:T(8,128)(2,1)S(1)}, u32[]{:S(2)}, u32[]{:S(2)}) async-start(bf16[8,288,256]{2,1,0:T(8,128)(2,1)} %broadcast_in_dim.61), calls=%async_computation.2 | async-start | bytes 2359296 | tf_op jit(solution)/shard_map/all_to_all | solution.py:122

commit v2 on v0

v2 whole, which is shorter than its diff:
```python
import functools
import jax
import jax.numpy as jnp
from jax import lax
from jax.experimental import pallas as pl
from jax.experimental.pallas import tpu as pltpu
from jax.sharding import Mesh, PartitionSpec as P

F32, F16, BF16 = jnp.float32, jnp.float16, jnp.bfloat16
MIB = 1024 * 1024
GROUP = 6
SCALAR = pl.BlockSpec(memory_space=pltpu.SMEM)


def unrotate_kernel(peers, cos_ref, sin_ref, *refs):
    msgs, (unrot_ref, weighted_ref, gain_ref, rows_ref, rot_ref) = refs[:-5], refs[-5:]
    step = pl.program_id(0)
    parts = cos_ref.shape[0]
    per = parts // peers
    block = msgs[0].shape[1]

    @pl.when(step == 0)
    def _():
        for b, msg in enumerate(msgs):
            at = slice(b * block, (b + 1) * block)
            real_part, imag_part = msg[:parts].astype(F32), msg[parts : 2 * parts].astype(F32)
            cosine, sine = cos_ref[:, at], sin_ref[:, at]
            rows_ref[:parts, at] = (real_part * cosine + imag_part * sine).astype(BF16)
            rows_ref[parts : 2 * parts, at] = (imag_part * cosine - real_part * sine).astype(BF16)
            rows_ref[2 * parts :, at] = msg[2 * parts : 2 * parts + 16]
            code = msg[2 * parts + 16 :].astype(F32)
            goal = jnp.where(code > 0.0, code - 1.0, 255.0 - code)
            rot_ref[:, :, at] = goal.reshape(rot_ref.shape[0], 8, block)

    place = lax.broadcasted_iota(jnp.int32, (block, block), 1).astype(F32)
    gain_ref[...] = jnp.zeros_like(gain_ref)
    for b in range(len(msgs)):
        at = slice(b * block, (b + 1) * block)
        goal = rot_ref[step, :, at].T
        tables = [jnp.where(place == goal[:, i : i + 1], 1.0, 0.0).astype(BF16) for i in range(GROUP)]
        out = jnp.dot(rows_ref[:, at], jnp.concatenate(tables, axis=1), preferred_element_type=F32)
        turned = [out[:, i * block : (i + 1) * block] for i in range(GROUP)]
        gains = [jnp.sum(t[2 * parts :], axis=0, keepdims=True) for t in turned]
        for i in range(GROUP):
            gain_ref[0, i : i + 1, at] = gains[i]
        for c in range(2):
            plain, scaled = [], []
            for pair in range(0, GROUP, 2):
                for p in range(peers):
                    for i in (pair, pair + 1):
                        start = c * parts + p * per
                        piece = turned[i][start : start + per]
                        plain.append(piece)
                        scaled.append(piece * gains[i])
            unrot_ref[c, :, at] = jnp.concatenate(plain).astype(BF16)
            weighted_ref[c, :, at] = jnp.concatenate(scaled).astype(BF16)


def unrotate(cosine, sine, msgs, rots, peers):
    parts, pixels = cosine.shape
    steps = rots // GROUP
    spec = pl.BlockSpec((2, GROUP * parts, pixels), lambda r: (0, r, 0))
    shape = jax.ShapeDtypeStruct((2, rots * parts, pixels), BF16)
    whole = [pl.BlockSpec(a.shape, lambda r: (0, 0)) for a in (cosine, sine, *msgs)]
    return pl.pallas_call(
        functools.partial(unrotate_kernel, peers),
        grid=(steps,),
        in_specs=whole,
        out_specs=[spec, spec, pl.BlockSpec((1, 8, pixels), lambda r: (r, 0, 0))],
        out_shape=[shape, shape, jax.ShapeDtypeStruct((steps, 8, pixels), F32)],
        scratch_shapes=[pltpu.VMEM((2 * parts + 16, pixels), BF16), pltpu.VMEM((steps, 8, pixels), F32)],
        compiler_params=pltpu.CompilerParams(vmem_limit_bytes=56 * MIB),
        cost_estimate=pl.CostEstimate(
            flops=2 * rots * (2 * parts + 16) * pixels * msgs[0].shape[1],
            bytes_accessed=8 * rots * parts * pixels,
            transcendentals=0,
        ),
    )(cosine, sine, *msgs)


def score_kernel(peers, place_ref, weighted_ref, gain_ref, own_ref, other_ref, out_ref, refs_ref, norm_ref):
    step = pl.program_id(0)
    count, k2, block = own_ref.shape
    k_dev = k2 // 2
    blocks = refs_ref.shape[1] // block

    @pl.when(step == 0)
    def _():
        for b in range(blocks):
            at = slice(b * block, (b + 1) * block)
            power = 0.0
            for c in range(2):
                held = []
                for ref in (own_ref, other_ref):
                    for d in range(count // blocks):
                        held.append(ref[d * blocks + (place_ref[0] ^ b), c * k_dev : (c + 1) * k_dev])
                turned = jnp.concatenate(held).astype(F32).T
                refs_ref[c, at, :] = turned.astype(BF16)
                power = power + turned * turned
            gain = gain_ref[:, :, at].reshape(norm_ref.shape[0], block)
            part = 0.5 * jnp.dot(gain, power, preferred_element_type=F32, precision=lax.Precision.HIGHEST)
            norm_ref[...] = part if b == 0 else norm_ref[...] + part

    cross = jnp.dot(weighted_ref[0], refs_ref[0], preferred_element_type=F32)
    cross += jnp.dot(weighted_ref[1], refs_ref[1], preferred_element_type=F32)
    rows = cross.shape[0] // (GROUP * peers)
    norm = norm_ref[pl.ds(pl.multiple_of(step * 8, 8), 8), :]
    for q in range(GROUP // 2):
        for p in range(peers):
            for i in range(2):
                start = ((q * peers + p) * 2 + i) * rows
                to = (q * 2 + i) * rows
                out_ref[p, to : to + rows, :] = cross[start : start + rows] - norm[q * 2 + i : q * 2 + i + 1]


def score(place, weighted, gain, own, other, peers):
    steps, _, pixels = gain.shape
    count, k2, block = own.shape
    classes = count * k2 // (pixels // block)
    rows = weighted.shape[1] // steps
    return pl.pallas_call(
        functools.partial(score_kernel, peers),
        grid=(steps,),
        in_specs=[
            SCALAR,
            pl.BlockSpec((2, rows, pixels), lambda i: (0, i, 0)),
            pl.BlockSpec(gain.shape, lambda i: (0, 0, 0)),
            pl.BlockSpec(own.shape, lambda i: (0, 0, 0)),
            pl.BlockSpec(other.shape, lambda i: (0, 0, 0)),
        ],
        out_specs=pl.BlockSpec((peers, rows // peers, classes), lambda i: (0, i, 0)),
        out_shape=jax.ShapeDtypeStruct((peers, rows // peers * steps, classes), F32),
        scratch_shapes=[pltpu.VMEM((2, pixels, classes), BF16), pltpu.VMEM((steps * 8, classes), F32)],
        compiler_params=pltpu.CompilerParams(vmem_limit_bytes=56 * MIB),
    )(place, weighted, gain, own, other)


def sums_kernel(steps, block, k_dev, place_ref, weights_ref, unrot_ref, out_ref, acc_ref, totals_ref):
    step = pl.program_id(0)
    peers, mine, classes = weights_ref.shape
    picked = [weights_ref[p, q * 16 : (q + 1) * 16, :] for q in range(mine // 16) for p in range(peers)]
    turned = jnp.concatenate(picked).astype(F32).T.astype(BF16)
    count = jnp.dot(turned, jnp.ones((turned.shape[1], 128), BF16), preferred_element_type=F32)
    terms = [jnp.dot(turned, unrot_ref[c], preferred_element_type=F32) for c in range(2)]

    @pl.when(step == 0)
    def _():
        for c in range(2):
            acc_ref[c] = terms[c]
        totals_ref[...] = count

    @pl.when(step > 0)
    def _():
        for c in range(2):
            acc_ref[c] += terms[c]
        totals_ref[...] += count

    @pl.when(step == steps - 1)
    def _():
        blocks = acc_ref.shape[2] // block
        totals = totals_ref[...]
        high = totals.astype(BF16).astype(F32)
        lane = lax.broadcasted_iota(jnp.int32, totals.shape, 1)
        tail = jnp.where(lane == 0, high, totals - high)
        for d in range(classes // k_dev):
            ks = slice(d * k_dev, (d + 1) * k_dev)
            for b in range(blocks):
                at = d * blocks + (place_ref[0] ^ b)
                for c in range(2):
                    out_ref[at, :, c * block : (c + 1) * block] = acc_ref[c, ks, b * block : (b + 1) * block]
                out_ref[at, :, 2 * block :] = tail[ks]


def class_sums(place, weights, unrot, block, k_dev, side, steps):
    peers, total, classes = weights.shape
    pixels = unrot.shape[2]
    mine = total // steps
    half = classes // 2
    out = (half // k_dev * (pixels // block), k_dev, 2 * block + 128)
    return pl.pallas_call(
        functools.partial(sums_kernel, steps, block, k_dev),
        grid=(steps,),
        in_specs=[
            SCALAR,
            pl.BlockSpec((peers, mine, half), lambda i: (0, i, side)),
            pl.BlockSpec((2, mine * peers, pixels), lambda i: (0, i, 0)),
        ],
        out_specs=pl.BlockSpec(out, lambda i: (0, 0, 0)),
        out_shape=jax.ShapeDtypeStruct(out, F32),
        scratch_shapes=[pltpu.VMEM((2, half, pixels), F32), pltpu.VMEM((half, 128), F32)],
        compiler_params=pltpu.CompilerParams(vmem_limit_bytes=56 * MIB),
        cost_estimate=pl.CostEstimate(
            flops=4 * half * total * peers * pixels, bytes_accessed=unrot.size * 2, transcendentals=0
        ),
    )(place, weights, unrot)


def shards(particles, references, trans_index, shell_map, rot_index, inv_sigma):
    _, parts, freq = particles.shape
    k_dev = references.shape[0]
    rots = rot_index.shape[0]
    shells = inv_sigma.shape[0]
    cols, zqs = lax.axis_size("col"), lax.axis_size("zq")
    few = parts // 4
    classes = 2 * cols * k_dev
    yh, zq, zl = lax.axis_index("yh"), lax.axis_index("zq"), lax.axis_index("zl")
    half = 2 * zqs
    place = yh * 2 + zl

    base = (yh * half + zq * 2 + zl) * freq
    local_rot = rot_index - base
    code = jnp.where(local_rot < 256, local_rot + 1, 255 - local_rot).astype(BF16)
    code = jnp.pad(code.reshape(rots // GROUP, GROUP, freq), ((0, 0), (0, 8 - GROUP), (0, 0)))
    select = shell_map[:, None] == jnp.arange(shells, dtype=jnp.int32)[None, :]
    gain = jnp.sum(jnp.where(select, inv_sigma[None, :], 0.0), axis=1)
    top = lax.reduce_precision(gain, 8, 7)
    middle = lax.reduce_precision(gain - top, 8, 7)
    low = gain - top - middle
    gains = jnp.pad(jnp.stack([top, middle, low]).astype(BF16), ((0, 13), (0, 0)))
    side = jnp.concatenate([gains, code.reshape(rots // GROUP * 8, freq)])
    msgs = []
    for b in range(4):
        chunk = lax.dynamic_slice_in_dim(particles, (place ^ b) * few, few, 1).reshape(2 * few, freq)
        msg = jnp.concatenate([chunk, side])
        if b:
            msg = lax.ppermute(msg, ("yh", "zl"), [(i, i ^ b) for i in range(4)])
        msgs.append(msg)

    mine = references.transpose(1, 0, 2).reshape(1, 2 * k_dev, freq)
    mine = jnp.broadcast_to(mine, (4 * cols, 2 * k_dev, freq))
    refs = lax.all_to_all(mine, ("col", "yh", "zl"), 0, 0)

    pos = jnp.arange(freq, dtype=jnp.int32)
    spots = [place ^ b for b in range(4)]
    fidx = jnp.concatenate([(s // 2 * half + zq * 2 + s % 2) * freq + pos for s in spots])
    trans = lax.dynamic_slice_in_dim(trans_index, place * few, few, 0)
    kx = (fidx % 64).astype(F32)
    ky = (fidx // 64 % 128 - 64).astype(F32)
    tx = (trans % 7 - 3).astype(F32)
    ty = (trans // 7 - 3).astype(F32)
    phase = 2.0 * jnp.pi / 128.0 * (tx[:, None] * kx[None, :] + ty[:, None] * ky[None, :])
    unrot, weighted, gain_unrot = unrotate(jnp.cos(phase), jnp.sin(phase), msgs, rots, zqs)

    refs, weighted = lax.optimization_barrier((refs, weighted))
    refs_other = lax.ppermute(refs, "core", [(0, 1), (1, 0)])

    spot = jnp.reshape(place, (1,)).astype(jnp.int32)
    partial = score(spot, weighted, gain_unrot, refs, refs_other, zqs).astype(F16)
    own = few // zqs
    scores = jnp.sum(lax.all_to_all(partial, "zq", 0, 0).astype(F32), axis=0).reshape(rots, own, classes)
    peak = jnp.max(scores, axis=(0, 2), keepdims=True)
    expo = jnp.exp(scores - peak)
    weights = (expo / jnp.sum(expo, axis=(0, 2), keepdims=True)).astype(BF16)
    spread = jnp.broadcast_to(weights.reshape(1, rots * own, classes), (zqs, rots * own, classes))
    weights = lax.all_to_all(spread, "zq", 0, 0)

    other = class_sums(spot, weights, unrot, freq, k_dev, 1, 3).astype(F16)
    other = lax.ppermute(other, "core", [(0, 1), (1, 0)])
    message = class_sums(spot, weights, unrot, freq, k_dev, 0, 3)
    message = (message + other.astype(F32)).astype(F16)
    message = lax.all_to_all(message, ("col", "yh", "zl"), 0, 0)
    summed = jnp.sum(message.astype(F32), axis=0)
    counts = summed[:, 2 * freq] + summed[:, 2 * freq + 1]
    return (summed[:, : 2 * freq] / (counts + 1.0)[:, None]).reshape(k_dev, 2, freq)


def solution(mesh):
    doms, others = mesh.devices.shape
    grid = Mesh(mesh.devices.reshape(doms // 2, 2, 2, others // 4, 2), ("col", "core", "yh", "zq", "zl"))
    dom, across = ("col", "core"), ("yh", "zq", "zl")
    return jax.shard_map(
        shards,
        mesh=grid,
        in_specs=(
            P(None, dom, across),
            P(dom, None, across),
            P(dom),
            P(across),
            P(None, across),
            P(),
        ),
        out_specs=P(dom, None, across),
        check_vma=False,
    )
```

time: 325 us -> 159 us (0.49)
  waiting for transfers between devices: 197 us -> 16.9 us
  Pallas kernels: 0 us -> 44.4 us
  matrix products: 38.5 us -> 0 us
  starting transfers between devices: 0.04 us -> 22.1 us
  between operations: 14.1 us -> 0.27 us
  other arithmetic: 12.7 us -> 9.01 us
  blocking collectives: 58.3 us -> 61.6 us
    psum x1 -> x0, waiting for transfers between devices: 168 us -> none  [shards(): scores = lax.psum(partial_block, 'shell')]
    all_to_all x0 -> x3, blocking collectives: none -> 61.6 us  [the longest x1 23.6 us: shards(): message = lax.all_to_all(message, ('col', 'yh', 'zl'), 0, 0)]
    pallas_call x0 -> x4, Pallas kernels: none -> 44.4 us  [the longest x1 19.7 us: unrotate(): pl.pallas_call(functools.partial(unrotate_kernel, peers), grid=(steps,),...]
    dot_general x5 -> x0, matrix products: 38.5 us -> none  [the longest x1 14.6 us: shards(): jnp.einsum('f,rfg->rg', gain, table.astype(jnp.float32), precision=lax.Pr...]
    unnamed x1 -> x0, blocking collectives: 35.9 us -> none
    reduce_scatter x1 -> x0, waiting for transfers between devices: 29.5 us -> none  [shards(): lax.psum_scatter(terms, 'dom', scatter_dimension=0, tiled=True)]
    all_gather x1 -> x0, blocking collectives: 22.5 us -> none  [shards(): piece = lax.all_gather(references, 'dom', axis=0, tiled=True)]
    ppermute x0 -> x5, waiting for transfers between devices: none -> 16.9 us  [the longest x3 14.6 us: shards(): msg = lax.ppermute(msg, ('yh', 'zl'), [(i, i ^ b) for i in range(4)])]
  transfers between devices with their start and end apart: 2 -> 6, of which waited for: 2 -> 4; matrix products, arithmetic and copies ran while one was open for 0% -> 2% of each run, Pallas kernels for 0% -> 17%
where the time goes in v2:
time: 159 us
  blocking collectives  61.6 us (39%)
  Pallas kernels  44.4 us (28%)
  starting transfers between devices  22.1 us (14%)
  waiting for transfers between devices  16.9 us (11%)
  other arithmetic  9.01 us (6%)
  local copies, waits for them, and re-layouts  4.68 us (3%)
    all_to_all x1, blocking collectives, shards(): message = lax.all_to_all(message, ('col', 'yh', 'zl'), 0, 0)  23.6 us
    all_to_all x1, blocking collectives, shards(): lax.all_to_all(partial, 'zq', 0, 0).astype(F32)  21.3 us
    pallas_call x1, Pallas kernels, unrotate(): pl.pallas_call(functools.partial(unrotate_kernel, peers), grid=(steps,),...  19.7 us
    all_to_all x1, blocking collectives, shards(): weights = lax.all_to_all(spread, 'zq', 0, 0)  16.7 us
    pallas_call x2, Pallas kernels, class_sums(): pl.pallas_call(functools.partial(sums_kernel, steps, block, k_dev), grid=...  14.6 us
    ppermute x3, waiting for transfers between devices, shards(): msg = lax.ppermute(msg, ('yh', 'zl'), [(i, i ^ b) for i in range(4)])  14.6 us
    pallas_call x1, Pallas kernels, score(): pl.pallas_call(functools.partial(score_kernel, peers), grid=(steps,), in_...  10.1 us
    all_to_all x1, starting transfers between devices, shards(): refs = lax.all_to_all(mine, ('col', 'yh', 'zl'), 0, 0)  9.37 us
  transfers between devices with their start and end apart: 6, of which 4 were waited for; matrix products, arithmetic and copies ran while one was open for 2% of the time, Pallas kernels for 17%

profile of v2, /device:TPU:1, one launch (start us, length us, event | category | flops | bytes accessed | tf_op | source)
XLA Modules:
  0.0 158.9 jit_solution(736618644302643665)
XLA Ops:
  0.0 0.8 copy.12
  0.8 1.1 broadcast_in_dim.19
  1.9 9.4 %all-to-all-start = ((bf16[32,32,512]{2,1,0:T(8,128)(2,1)}), bf16[32,32,512]{2,1,0:T(8,128)(2,1)S(1)}, u32[]{:S(2)}, u32[]{:S(2)}) async-start(bf16[32,32,512]{2,1,0:T(8,128)(2,1)} %broadcast_in_dim.19), calls=%async_computation | async-start | bytes 2097152 | tf_op jit(solution)/shard_map/all_to_all | solution.py:231
  11.6 0.7 pad_maximum_fusion.4
  12.3 3.6 %collective-permute-start.2 = (bf16[128,512]{1,0:T(8,128)(2,1)S(1)}, bf16[128,512]{1,0:T(8,128)(2,1)S(1)}, u32[]{:S(2)}, u32[]{:S(2)}) collective-permute-start(bf16[128,512]{1,0:T(8,128)(2,1)S(1)} %get-tuple-element.19), channel_id=1, source_target_pairs={{0,9},{1,8},{8,1},{9,0},{2,11},{3,10},{10,3},{11,2},{4,13},{5,12},... | collective-permute-start | bytes 393224 | tf_op jit(solution)/shard_map/ppermute | solution.py:226
  16.6 1.8 %fusion = (f32[32,2048]{1,0:T(8,128)}, f32[32,2048]{1,0:T(8,128)}) fusion(f32[2048]{0:T(1024)S(1)} %get-tuple-element.26, f32[32]{0:T(128)S(1)} %get-tuple-element.31, f32[2048]{0:T(1024)S(1)} %get-tuple-element.25, f32[32]{0:T(128)S(1)} %get-tuple-element.30), kind=kLoop, calls=%fused_computation.6 | loop fusion | flops 262144 | bytes 540928 | tf_op jit(solution)/shard_map/sin | solution.py:242
  18.5 10.6 %collective-permute-done.2.refs_3_ = bf16[128,512]{1,0:T(8,128)(2,1)S(1)} collective-permute-done((bf16[128,512]{1,0:T(8,128)(2,1)S(1)}, bf16[128,512]{1,0:T(8,128)(2,1)S(1)}, u32[]{:S(2)}, u32[]{:S(2)}) %collective-permute-start.2) | collective-permute-done | bytes 131104 | tf_op jit(solution)/shard_map/ppermute | solution.py:226
  29.5 3.6 %collective-permute-done.1.refs_2_ = bf16[128,512]{1,0:T(8,128)(2,1)S(1)} collective-permute-done((bf16[128,512]{1,0:T(8,128)(2,1)S(1)}, bf16[128,512]{1,0:T(8,128)(2,1)S(1)}, u32[]{:S(2)}, u32[]{:S(2)}) %collective-permute-start.1) | collective-permute-done | bytes 131104 | tf_op jit(solution)/shard_map/ppermute | solution.py:226
  33.1 0.6 copy-done.9
  33.7 19.7 %shard_map.64 = (bf16[2,1152,2048]{2,1,0:T(8,128)(2,1)}, bf16[2,1152,2048]{2,1,0:T(8,128)(2,1)}, f32[6,8,2048]{2,1,0:T(8,128)}) custom-call(f32[32,2048]{1,0:T(8,128)} %get-tuple-element.24.cos_ref, f32[32,2048]{1,0:T(8,128)} %get-tuple-element.23.sin_ref, bf16[128,512]{1,0:T(8,128)(2,1)} %get-tuple-element.22.refs_0_, bf16[128,512]{1,0:T(8,128)(2,1)} %copy-done.8, ...), custom_call_target="tpu_custom_call" | custom-call | flops 6039797760 | bytes 18874368 | tf_op jit(solution)/shard_map/pallas_call | solution.py:65
  53.5 0.7 collective-permute-start.3
  54.2 2.3 %collective-permute-done.3.other_ref = bf16[32,32,512]{2,1,0:T(8,128)(2,1)S(1)} collective-permute-done((bf16[32,32,512]{2,1,0:T(8,128)(2,1)S(1)}, bf16[32,32,512]{2,1,0:T(8,128)(2,1)S(1)}, u32[]{:S(2)}, u32[]{:S(2)}) %collective-permute-start.3) | collective-permute-done | bytes 1048608 | tf_op jit(solution)/shard_map/ppermute | solution.py:245
  56.5 1.0 copy-done.1
  57.5 10.1 %shard_map.65 = f32[4,288,256]{2,1,0:T(8,128)} custom-call(s32[1]{0:T(128)} %bitcast.place_ref, bf16[2,1152,2048]{2,1,0:T(8,128)(2,1)} %get-tuple-element.11.weighted_ref, f32[6,8,2048]{2,1,0:T(8,128)} %get-tuple-element.12.gain_ref, bf16[32,32,512]{2,1,0:T(8,128)(2,1)} %copy-done, bf16[32,32,512]{2,1,0:T(8,128)(2,1)} %copy-done.1), custom_call_target="tpu_custom_call" | custom-call | tf_op jit(solution)/shard_map/pallas_call | solution.py:121
  67.5 1.4 convert_element_type.58
  68.9 21.3 %all_to_all.20 = f16[4,288,256]{2,1,0:T(8,128)(2,1)S(1)} all-to-all(f16[4,288,256]{2,1,0:T(8,128)(2,1)S(1)} %convert_element_type.58), channel_id=1, replica_groups=mesh['col'=8,'core'=2,'yh'=2,'zq'=4,'zl'=2] {'zq'}, dimensions={0} | all-to-all | bytes 1179648 | tf_op jit(solution)/shard_map/all_to_all | solution.py:250
  91.3 16.7 %all_to_all.21.weights_ref = bf16[4,288,256]{2,1,0:T(8,128)(2,1)} all-to-all(bf16[4,288,256]{2,1,0:T(8,128)(2,1)S(1)} %broadcast_in_dim.22), channel_id=1, replica_groups=mesh['col'=8,'core'=2,'yh'=2,'zq'=4,'zl'=2] {'zq'}, dimensions={0} | all-to-all | bytes 1179648 | tf_op jit(solution)/shard_map/all_to_all | solution.py:255
  108.0 7.3 %shard_map.67 = f32[32,16,1152]{2,1,0:T(8,128)} custom-call(s32[1]{0:T(128)} %bitcast.place_ref, bf16[4,288,256]{2,1,0:T(8,128)(2,1)} %all_to_all.21.weights_ref, bf16[2,1152,2048]{2,1,0:T(8,128)(2,1)} %get-tuple-element.14.unrot_ref), custom_call_target="tpu_custom_call" | custom-call | flops 1207959552 | bytes 9437184 | tf_op jit(solution)/shard_map/pallas_call | solution.py:180
  115.3 1.8 %convert_element_type.61 = f16[32,16,1152]{2,1,0:T(8,128)(2,1)S(1)} convert(f32[32,16,1152]{2,1,0:T(8,128)} %shard_map.67) | non-fusion elementwise | flops 589824 | bytes 3538944 | tf_op jit(solution)/shard_map/convert_element_type | solution.py:257
  117.1 7.8 %collective-permute-start.4 = (f16[32,16,1152]{2,1,0:T(8,128)(2,1)S(1)}, f16[32,16,1152]{2,1,0:T(8,128)(2,1)S(1)}, u32[]{:S(2)}, u32[]{:S(2)}) collective-permute-start(f16[32,16,1152]{2,1,0:T(8,128)(2,1)S(1)} %convert_element_type.61), channel_id=1, source_target_pairs={{0,16},{16,0},{1,17},{17,1},{2,18},{18,2},{3,19},{19,3},{4,20},{20... | collective-permute-start | bytes 3538952 | tf_op jit(solution)/shard_map/ppermute | solution.py:258
  124.9 7.3 %shard_map.66 = f32[32,16,1152]{2,1,0:T(8,128)} custom-call(s32[1]{0:T(128)} %bitcast.place_ref, bf16[4,288,256]{2,1,0:T(8,128)(2,1)} %all_to_all.21.weights_ref, bf16[2,1152,2048]{2,1,0:T(8,128)(2,1)} %get-tuple-element.14.unrot_ref), custom_call_target="tpu_custom_call" | custom-call | flops 1207959552 | bytes 9437184 | tf_op jit(solution)/shard_map/pallas_call | solution.py:180
  132.3 1.9 %add_convert_fusion = f16[32,16,1152]{2,1,0:T(8,128)(2,1)S(1)} fusion(f32[32,16,1152]{2,1,0:T(8,128)} %shard_map.66, f16[32,16,1152]{2,1,0:T(8,128)(2,1)S(1)} %collective-permute-done.4), kind=kLoop, calls=%fused_computation.1 | loop fusion | flops 1769472 | bytes 4718592 | tf_op jit(solution)/shard_map/convert_element_type | solution.py:260
  134.2 23.6 %all_to_all.22 = f16[32,16,1152]{2,1,0:T(8,128)(2,1)S(1)} all-to-all(f16[32,16,1152]{2,1,0:T(8,128)(2,1)S(1)} %add_convert_fusion), channel_id=1, replica_groups=mesh['col'=8,'core'=2,'yh'=2,'zq'=4,'zl'=2] {'col','yh','zl'}, dimensions={0} | all-to-all | bytes 2359296 | tf_op jit(solution)/shard_map/all_to_all | solution.py:261
  158.2 0.7 reshape.252
  (50 shorter events, 2.7 us)
Async XLA Ops:
  1.9 9.4 %copy-start.4 = (s32[512]{0:T(512)S(1)}, s32[512]{0:T(512)}, u32[]{:S(2)}) copy-start(s32[512]{0:T(512)} %param.9) | copy-start | bytes 6148
  1.9 9.4 %copy-start.5 = (f32[64]{0:T(128)S(1)}, f32[64]{0:T(128)}, u32[]{:S(2)}) copy-start(f32[64]{0:T(128)} %param.11) | copy-start | bytes 772
  1.9 9.5 %copy-start.3 = (s32[36,512]{1,0:T(8,128)S(1)}, s32[36,512]{1,0:T(8,128)}, u32[]{:S(2)}) copy-start(s32[36,512]{1,0:T(8,128)} %param.10) | copy-start | bytes 221188
  1.9 9.7 %copy-start.2 = (bf16[2,128,512]{2,1,0:T(8,128)(2,1)S(1)}, bf16[2,128,512]{2,1,0:T(8,128)(2,1)}, u32[]{:S(2)}) copy-start(bf16[2,128,512]{2,1,0:T(8,128)(2,1)} %param.6) | copy-start | bytes 786436
  1.9 51.6 %all-to-all-start = ((bf16[32,32,512]{2,1,0:T(8,128)(2,1)}), bf16[32,32,512]{2,1,0:T(8,128)(2,1)S(1)}, u32[]{:S(2)}, u32[]{:S(2)}) async-start(bf16[32,32,512]{2,1,0:T(8,128)(2,1)} %broadcast_in_dim.19), calls=%async_computation | async-start | bytes 2097152 | tf_op jit(solution)/shard_map/all_to_all | solution.py:231
  11.3 5.2 %copy-start.6 = (s32[128]{0:T(128)S(1)}, s32[128]{0:T(128)}, u32[]{:S(2)}) copy-start(s32[128]{0:T(128)} %param.8) | copy-start | bytes 1540
  12.3 16.8 %collective-permute-start.2 = (bf16[128,512]{1,0:T(8,128)(2,1)S(1)}, bf16[128,512]{1,0:T(8,128)(2,1)S(1)}, u32[]{:S(2)}, u32[]{:S(2)}) collective-permute-start(bf16[128,512]{1,0:T(8,128)(2,1)S(1)} %get-tuple-element.19), channel_id=1, source_target_pairs={{0,9},{1,8},{8,1},{9,0},{2,11},{3,10},{10,3},{11,2},{4,13},{5,12},... | collective-permute-start | bytes 393224 | tf_op jit(solution)/shard_map/ppermute | solution.py:226
  16.0 13.5 %collective-permute-start = (bf16[128,512]{1,0:T(8,128)(2,1)S(1)}, bf16[128,512]{1,0:T(8,128)(2,1)S(1)}, u32[]{:S(2)}, u32[]{:S(2)}) collective-permute-start(bf16[128,512]{1,0:T(8,128)(2,1)S(1)} %get-tuple-element.20), channel_id=1, source_target_pairs={{0,1},{1,0},{8,9},{9,8},{2,3},{3,2},{10,11},{11,10},{4,5},{5,4},{1... | collective-permute-start | bytes 393224 | tf_op jit(solution)/shard_map/ppermute | solution.py:226
  16.3 16.8 %collective-permute-start.1 = (bf16[128,512]{1,0:T(8,128)(2,1)S(1)}, bf16[128,512]{1,0:T(8,128)(2,1)S(1)}, u32[]{:S(2)}, u32[]{:S(2)}) collective-permute-start(bf16[128,512]{1,0:T(8,128)(2,1)S(1)} %get-tuple-element.21), channel_id=1, source_target_pairs={{0,8},{1,9},{8,0},{9,1},{2,10},{3,11},{10,2},{11,3},{4,12},{5,13},... | collective-permute-start | bytes 393224 | tf_op jit(solution)/shard_map/ppermute | solution.py:226
  29.1 4.0 %copy-start.7 = (bf16[128,512]{1,0:T(8,128)(2,1)}, bf16[128,512]{1,0:T(8,128)(2,1)S(1)}, u32[]{:S(2)}) copy-start(bf16[128,512]{1,0:T(8,128)(2,1)S(1)} %collective-permute-done.2.refs_3_) | copy-start | bytes 393220
  29.5 3.6 %copy-start.8 = (bf16[128,512]{1,0:T(8,128)(2,1)}, bf16[128,512]{1,0:T(8,128)(2,1)S(1)}, u32[]{:S(2)}) copy-start(bf16[128,512]{1,0:T(8,128)(2,1)S(1)} %collective-permute-done.refs_1_) | copy-start | bytes 393220
  33.1 0.7 copy-start.9
  53.5 3.0 %copy-start = (bf16[32,32,512]{2,1,0:T(8,128)(2,1)}, bf16[32,32,512]{2,1,0:T(8,128)(2,1)S(1)}, u32[]{:S(2)}) copy-start(bf16[32,32,512]{2,1,0:T(8,128)(2,1)S(1)} %all-to-all-done.own_ref) | copy-start | bytes 3145732
  53.5 3.0 %collective-permute-start.3 = (bf16[32,32,512]{2,1,0:T(8,128)(2,1)S(1)}, bf16[32,32,512]{2,1,0:T(8,128)(2,1)S(1)}, u32[]{:S(2)}, u32[]{:S(2)}) collective-permute-start(bf16[32,32,512]{2,1,0:T(8,128)(2,1)S(1)} %all-to-all-done.own_ref), channel_id=1, source_target_pairs={{0,16},{16,0},{1,17},{17,1},{2,18},{18,2},{3,19},{19,3},{4,20},{20... | collective-permute-start | bytes 3145736 | tf_op jit(solution)/shard_map/ppermute | solution.py:245
  56.5 1.0 copy-start.1
  117.1 15.1 %collective-permute-start.4 = (f16[32,16,1152]{2,1,0:T(8,128)(2,1)S(1)}, f16[32,16,1152]{2,1,0:T(8,128)(2,1)S(1)}, u32[]{:S(2)}, u32[]{:S(2)}) collective-permute-start(f16[32,16,1152]{2,1,0:T(8,128)(2,1)S(1)} %convert_element_type.61), channel_id=1, source_target_pairs={{0,16},{16,0},{1,17},{17,1},{2,18},{18,2},{3,19},{19,3},{4,20},{20... | collective-permute-start | bytes 3538952 | tf_op jit(solution)/shard_map/ppermute | solution.py:258

commit v3 on v2

--- a/solution.py
+++ b/solution.py
@@ -78,7 +78,7 @@
     )(cosine, sine, *msgs)
 
 
-def score_kernel(peers, place_ref, weighted_ref, gain_ref, own_ref, other_ref, out_ref, refs_ref, norm_ref):
+def score_kernel(peers, per_step, place_ref, weighted_ref, gain_ref, own_ref, other_ref, out_ref, refs_ref, norm_ref):
     step = pl.program_id(0)
     count, k2, block = own_ref.shape
     k_dev = k2 // 2
@@ -103,23 +103,25 @@
 
     cross = jnp.dot(weighted_ref[0], refs_ref[0], preferred_element_type=F32)
     cross += jnp.dot(weighted_ref[1], refs_ref[1], preferred_element_type=F32)
-    rows = cross.shape[0] // (GROUP * peers)
-    norm = norm_ref[pl.ds(pl.multiple_of(step * 8, 8), 8), :]
-    for q in range(GROUP // 2):
-        for p in range(peers):
-            for i in range(2):
-                start = ((q * peers + p) * 2 + i) * rows
-                to = (q * 2 + i) * rows
-                out_ref[p, to : to + rows, :] = cross[start : start + rows] - norm[q * 2 + i : q * 2 + i + 1]
-
-
-def score(place, weighted, gain, own, other, peers):
-    steps, _, pixels = gain.shape
+    rows = cross.shape[0] // (per_step * GROUP * peers)
+    for g in range(per_step):
+        norm = norm_ref[pl.ds(pl.multiple_of((step * per_step + g) * 8, 8), 8), :]
+        for q in range(GROUP // 2):
+            for p in range(peers):
+                for i in range(2):
+                    start = (((g * (GROUP // 2) + q) * peers + p) * 2 + i) * rows
+                    to = (g * GROUP + q * 2 + i) * rows
+                    out_ref[p, to : to + rows, :] = cross[start : start + rows] - norm[q * 2 + i : q * 2 + i + 1]
+
+
+def score(place, weighted, gain, own, other, peers, per_step):
+    groups, _, pixels = gain.shape
+    steps = groups // per_step
     count, k2, block = own.shape
     classes = count * k2 // (pixels // block)
     rows = weighted.shape[1] // steps
     return pl.pallas_call(
-        functools.partial(score_kernel, peers),
+        functools.partial(score_kernel, peers, per_step),
         grid=(steps,),
         in_specs=[
             SCALAR,
@@ -130,12 +132,12 @@
         ],
         out_specs=pl.BlockSpec((peers, rows // peers, classes), lambda i: (0, i, 0)),
         out_shape=jax.ShapeDtypeStruct((peers, rows // peers * steps, classes), F32),
-        scratch_shapes=[pltpu.VMEM((2, pixels, classes), BF16), pltpu.VMEM((steps * 8, classes), F32)],
-        compiler_params=pltpu.CompilerParams(vmem_limit_bytes=56 * MIB),
+        scratch_shapes=[pltpu.VMEM((2, pixels, classes), BF16), pltpu.VMEM((groups * 8, classes), F32)],
+        compiler_params=pltpu.CompilerParams(vmem_limit_bytes=54 * MIB),
     )(place, weighted, gain, own, other)
 
 
-def sums_kernel(steps, block, k_dev, place_ref, weights_ref, unrot_ref, out_ref, acc_ref, totals_ref):
+def sums_kernel(steps, block, k_dev, place_ref, weights_ref, unrot_ref, own_ref, other_ref, acc_ref, totals_ref):
     step = pl.program_id(0)
     peers, mine, classes = weights_ref.shape
     picked = [weights_ref[p, q * 16 : (q + 1) * 16, :] for q in range(mine // 16) for p in range(peers)]
@@ -162,16 +164,18 @@
         high = totals.astype(BF16).astype(F32)
         lane = lax.broadcasted_iota(jnp.int32, totals.shape, 1)
         tail = jnp.where(lane == 0, high, totals - high)
-        for d in range(classes // k_dev):
+        cols = classes // k_dev // 2
+        for d in range(2 * cols):
             ks = slice(d * k_dev, (d + 1) * k_dev)
+            out_ref = own_ref if d < cols else other_ref
             for b in range(blocks):
-                at = d * blocks + (place_ref[0] ^ b)
+                at = d % cols * blocks + (place_ref[0] ^ b)
                 for c in range(2):
                     out_ref[at, :, c * block : (c + 1) * block] = acc_ref[c, ks, b * block : (b + 1) * block]
                 out_ref[at, :, 2 * block :] = tail[ks]
 
 
-def class_sums(place, weights, unrot, block, k_dev, side, steps):
+def class_sums(place, weights, unrot, block, k_dev, steps):
     peers, total, classes = weights.shape
     pixels = unrot.shape[2]
     mine = total // steps
@@ -182,15 +186,15 @@
         grid=(steps,),
         in_specs=[
             SCALAR,
-            pl.BlockSpec((peers, mine, half), lambda i: (0, i, side)),
+            pl.BlockSpec((peers, mine, classes), lambda i: (0, i, 0)),
             pl.BlockSpec((2, mine * peers, pixels), lambda i: (0, i, 0)),
         ],
-        out_specs=pl.BlockSpec(out, lambda i: (0, 0, 0)),
-        out_shape=jax.ShapeDtypeStruct(out, F32),
-        scratch_shapes=[pltpu.VMEM((2, half, pixels), F32), pltpu.VMEM((half, 128), F32)],
-        compiler_params=pltpu.CompilerParams(vmem_limit_bytes=56 * MIB),
+        out_specs=[pl.BlockSpec(out, lambda i: (0, 0, 0))] * 2,
+        out_shape=[jax.ShapeDtypeStruct(out, F32)] * 2,
+        scratch_shapes=[pltpu.VMEM((2, classes, pixels), F32), pltpu.VMEM((classes, 128), F32)],
+        compiler_params=pltpu.CompilerParams(vmem_limit_bytes=40 * MIB),
         cost_estimate=pl.CostEstimate(
-            flops=4 * half * total * peers * pixels, bytes_accessed=unrot.size * 2, transcendentals=0
+            flops=4 * classes * total * peers * pixels, bytes_accessed=unrot.size * 2, transcendentals=0
         ),
     )(place, weights, unrot)
 
@@ -226,10 +230,6 @@
             msg = lax.ppermute(msg, ("yh", "zl"), [(i, i ^ b) for i in range(4)])
         msgs.append(msg)
 
-    mine = references.transpose(1, 0, 2).reshape(1, 2 * k_dev, freq)
-    mine = jnp.broadcast_to(mine, (4 * cols, 2 * k_dev, freq))
-    refs = lax.all_to_all(mine, ("col", "yh", "zl"), 0, 0)
-
     pos = jnp.arange(freq, dtype=jnp.int32)
     spots = [place ^ b for b in range(4)]
     fidx = jnp.concatenate([(s // 2 * half + zq * 2 + s % 2) * freq + pos for s in spots])
@@ -239,13 +239,20 @@
     tx = (trans % 7 - 3).astype(F32)
     ty = (trans // 7 - 3).astype(F32)
     phase = 2.0 * jnp.pi / 128.0 * (tx[:, None] * kx[None, :] + ty[:, None] * ky[None, :])
-    unrot, weighted, gain_unrot = unrotate(jnp.cos(phase), jnp.sin(phase), msgs, rots, zqs)
+    cosine, sine = jnp.cos(phase), jnp.sin(phase)
+
+    mine = references.transpose(1, 0, 2).reshape(1, 2 * k_dev, freq)
+    mine, msgs, cosine, sine = lax.optimization_barrier((mine, msgs, cosine, sine))
+    mine = jnp.broadcast_to(mine, (4 * cols, 2 * k_dev, freq))
+    refs = lax.all_to_all(mine, ("col", "yh", "zl"), 0, 0)
+
+    unrot, weighted, gain_unrot = unrotate(cosine, sine, msgs, rots, zqs)
 
     refs, weighted = lax.optimization_barrier((refs, weighted))
     refs_other = lax.ppermute(refs, "core", [(0, 1), (1, 0)])
 
     spot = jnp.reshape(place, (1,)).astype(jnp.int32)
-    partial = score(spot, weighted, gain_unrot, refs, refs_other, zqs).astype(F16)
+    partial = score(spot, weighted, gain_unrot, refs, refs_other, zqs, 2).astype(F16)
     own = few // zqs
     scores = jnp.sum(lax.all_to_all(partial, "zq", 0, 0).astype(F32), axis=0).reshape(rots, own, classes)
     peak = jnp.max(scores, axis=(0, 2), keepdims=True)
@@ -254,9 +261,8 @@
     spread = jnp.broadcast_to(weights.reshape(1, rots * own, classes), (zqs, rots * own, classes))
     weights = lax.all_to_all(spread, "zq", 0, 0)
 
-    other = class_sums(spot, weights, unrot, freq, k_dev, 1, 3).astype(F16)
-    other = lax.ppermute(other, "core", [(0, 1), (1, 0)])
-    message = class_sums(spot, weights, unrot, freq, k_dev, 0, 3)
+    message, other = class_sums(spot, weights, unrot, freq, k_dev, 3)
+    other = lax.ppermute(other.astype(F16), "core", [(0, 1), (1, 0)])
     message = (message + other.astype(F32)).astype(F16)
     message = lax.all_to_all(message, ("col", "yh", "zl"), 0, 0)
     summed = jnp.sum(message.astype(F32), axis=0)

time: 159 us -> 144 us (0.906)
  Pallas kernels: 44.4 us -> 36.5 us
  waiting for transfers between devices: 16.9 us -> 10.3 us
  blocking collectives: 61.6 us -> 64 us
  other arithmetic: 9.01 us -> 7.39 us
    ppermute x3, waiting for transfers between devices: 14.6 us -> 5.57 us  [shards(): msg = lax.ppermute(msg, ('yh', 'zl'), [(i, i ^ b) for i in range(4)])]
    pallas_call x2 -> x1, Pallas kernels: 14.6 us -> 7.58 us  [class_sums(): pl.pallas_call(functools.partial(sums_kernel, steps, block, k_dev), grid=...]
    all_to_all x1, blocking collectives: 23.6 us -> 26.3 us  [shards(): message = lax.all_to_all(message, ('col', 'yh', 'zl'), 0, 0)]
    all_to_all x1, starting transfers between devices: 9.37 us -> 6.79 us  [shards(): refs = lax.all_to_all(mine, ('col', 'yh', 'zl'), 0, 0)]
    ppermute x1, waiting for transfers between devices: 0.01 us -> 2.47 us  [shards(): other = lax.ppermute(other.astype(F16), 'core', [(0, 1), (1, 0)])]
    convert_element_type x2, other arithmetic: 3.16 us -> 1.49 us  [the longest x1 1.36 us: shards(): score(spot, weighted, gain_unrot, refs, refs_other, zqs, 2).astype(F16)]
  transfers between devices with their start and end apart: 6 -> 6, of which waited for: 4 -> 5; matrix products, arithmetic and copies ran while one was open for 2% -> 1% of each run, Pallas kernels for 17% -> 14%
where the time goes in v3:
time: 144 us
  blocking collectives  64 us (44%)
  Pallas kernels  36.5 us (25%)
  starting transfers between devices  21.2 us (15%)
  waiting for transfers between devices  10.3 us (7%)
  other arithmetic  7.39 us (5%)
  local copies, waits for them, and re-layouts  4.2 us (3%)
    all_to_all x1, blocking collectives, shards(): message = lax.all_to_all(message, ('col', 'yh', 'zl'), 0, 0)  26.3 us
    all_to_all x1, blocking collectives, shards(): lax.all_to_all(partial, 'zq', 0, 0).astype(F32)  21.3 us
    pallas_call x1, Pallas kernels, unrotate(): pl.pallas_call(functools.partial(unrotate_kernel, peers), grid=(steps,),...  19.8 us
    all_to_all x1, blocking collectives, shards(): weights = lax.all_to_all(spread, 'zq', 0, 0)  16.3 us
    pallas_call x1, Pallas kernels, score(): pl.pallas_call(functools.partial(score_kernel, peers, per_step), grid=(st...  9.17 us
    ppermute x1, starting transfers between devices, shards(): other = lax.ppermute(other.astype(F16), 'core', [(0, 1), (1, 0)])  8.06 us
    pallas_call x1, Pallas kernels, class_sums(): pl.pallas_call(functools.partial(sums_kernel, steps, block, k_dev), grid=...  7.58 us
    all_to_all x1, starting transfers between devices, shards(): refs = lax.all_to_all(mine, ('col', 'yh', 'zl'), 0, 0)  6.79 us
  transfers between devices with their start and end apart: 6, of which 5 were waited for; matrix products, arithmetic and copies ran while one was open for 1% of the time, Pallas kernels for 14%

profile of v3, /device:TPU:1, one launch (start us, length us, event | category | flops | bytes accessed | tf_op | source)
XLA Modules:
  0.0 143.8 jit_solution(2235805815341800081)
XLA Ops:
  0.0 0.8 select_reduce_fusion
  0.8 0.9 select_convert_fusion
  1.8 1.0 constant_dynamic-slice_fusion
  2.8 0.7 pad_maximum_fusion.4
  3.5 5.1 %collective-permute-start.2 = (bf16[128,512]{1,0:T(8,128)(2,1)S(1)}, bf16[128,512]{1,0:T(8,128)(2,1)S(1)}, u32[]{:S(2)}, u32[]{:S(2)}) collective-permute-start(bf16[128,512]{1,0:T(8,128)(2,1)S(1)} %get-tuple-element.37), channel_id=1, source_target_pairs={{0,9},{1,8},{8,1},{9,0},{2,11},{3,10},{10,3},{11,2},{4,13},{5,12},... | collective-permute-start | bytes 393224 | tf_op jit(solution)/shard_map/ppermute | solution.py:230
  9.0 1.9 %fusion = (f32[32,2048]{1,0:T(8,128)}, f32[32,2048]{1,0:T(8,128)}) fusion(f32[2048]{0:T(1024)S(1)} %get-tuple-element.44, f32[32]{0:T(128)S(1)} %get-tuple-element.49, f32[2048]{0:T(1024)S(1)} %get-tuple-element.43, f32[32]{0:T(128)S(1)} %get-tuple-element.48), kind=kLoop, calls=%fused_computation.6 | loop fusion | flops 262144 | bytes 540928 | tf_op jit(solution)/shard_map/sin | solution.py:242
  11.0 3.2 %collective-permute-done.refs_1_ = bf16[128,512]{1,0:T(8,128)(2,1)S(1)} collective-permute-done((bf16[128,512]{1,0:T(8,128)(2,1)S(1)}, bf16[128,512]{1,0:T(8,128)(2,1)S(1)}, u32[]{:S(2)}, u32[]{:S(2)}) %collective-permute-start) | collective-permute-done | bytes 131104 | tf_op jit(solution)/shard_map/ppermute | solution.py:230
  14.1 2.3 %collective-permute-done.1.refs_2_ = bf16[128,512]{1,0:T(8,128)(2,1)S(1)} collective-permute-done((bf16[128,512]{1,0:T(8,128)(2,1)S(1)}, bf16[128,512]{1,0:T(8,128)(2,1)S(1)}, u32[]{:S(2)}, u32[]{:S(2)}) %collective-permute-start.1) | collective-permute-done | bytes 131104 | tf_op jit(solution)/shard_map/ppermute | solution.py:230
  16.5 1.1 broadcast_in_dim.21
  17.6 6.8 %all-to-all-start = ((bf16[32,32,512]{2,1,0:T(8,128)(2,1)}), bf16[32,32,512]{2,1,0:T(8,128)(2,1)S(1)}, u32[]{:S(2)}, u32[]{:S(2)}) async-start(bf16[32,32,512]{2,1,0:T(8,128)(2,1)} %broadcast_in_dim.21), calls=%async_computation | async-start | bytes 2097152 | tf_op jit(solution)/shard_map/all_to_all | solution.py:247
  24.4 19.8 %shard_map.64 = (bf16[2,1152,2048]{2,1,0:T(8,128)(2,1)}, bf16[2,1152,2048]{2,1,0:T(8,128)(2,1)}, f32[6,8,2048]{2,1,0:T(8,128)}) custom-call(f32[32,2048]{1,0:T(8,128)} %get-tuple-element.20.cos_ref, f32[32,2048]{1,0:T(8,128)} %get-tuple-element.21.sin_ref, bf16[128,512]{1,0:T(8,128)(2,1)} %get-tuple-element.22.refs_0_, bf16[128,512]{1,0:T(8,128)(2,1)} %copy-done.5, ...), custom_call_target="tpu_custom_call" | custom-call | flops 6039797760 | bytes 18874368 | tf_op jit(solution)/shard_map/pallas_call | solution.py:65
  44.2 1.0 collective-permute-start.3
  45.1 2.3 %collective-permute-done.3.other_ref = bf16[32,32,512]{2,1,0:T(8,128)(2,1)S(1)} collective-permute-done((bf16[32,32,512]{2,1,0:T(8,128)(2,1)S(1)}, bf16[32,32,512]{2,1,0:T(8,128)(2,1)S(1)}, u32[]{:S(2)}, u32[]{:S(2)}) %collective-permute-start.3) | collective-permute-done | bytes 1048608 | tf_op jit(solution)/shard_map/ppermute | solution.py:252
  47.4 1.0 copy-done.1
  48.4 9.2 %shard_map.65 = f32[4,288,256]{2,1,0:T(8,128)} custom-call(s32[1]{0:T(128)} %bitcast.place_ref, bf16[2,1152,2048]{2,1,0:T(8,128)(2,1)} %get-tuple-element.27.weighted_ref, f32[6,8,2048]{2,1,0:T(8,128)} %get-tuple-element.28.gain_ref, bf16[32,32,512]{2,1,0:T(8,128)(2,1)} %copy-done, bf16[32,32,512]{2,1,0:T(8,128)(2,1)} %copy-done.1), custom_call_target="tpu_custom_call" | custom-call | tf_op jit(solution)/shard_map/pallas_call | solution.py:123
  57.6 1.4 convert_element_type.58
  58.9 21.3 %all_to_all.20 = f16[4,288,256]{2,1,0:T(8,128)(2,1)S(1)} all-to-all(f16[4,288,256]{2,1,0:T(8,128)(2,1)S(1)} %convert_element_type.58), channel_id=1, replica_groups=mesh['col'=8,'core'=2,'yh'=2,'zq'=4,'zl'=2] {'zq'}, dimensions={0} | all-to-all | bytes 1179648 | tf_op jit(solution)/shard_map/all_to_all | solution.py:257
  81.4 16.3 %all_to_all.21.weights_ref = bf16[4,288,256]{2,1,0:T(8,128)(2,1)S(1)} all-to-all(bf16[4,288,256]{2,1,0:T(8,128)(2,1)S(1)} %broadcast_in_dim.22), channel_id=1, replica_groups=mesh['col'=8,'core'=2,'yh'=2,'zq'=4,'zl'=2] {'zq'}, dimensions={0} | all-to-all | bytes 1179648 | tf_op jit(solution)/shard_map/all_to_all | solution.py:262
  97.7 7.6 %shard_map.66 = (f32[32,16,1152]{2,1,0:T(8,128)S(1)}, f32[32,16,1152]{2,1,0:T(8,128)S(1)}) custom-call(s32[1]{0:T(128)} %bitcast.place_ref, bf16[4,288,256]{2,1,0:T(8,128)(2,1)S(1)} %all_to_all.21.weights_ref, bf16[2,1152,2048]{2,1,0:T(8,128)(2,1)} %get-tuple-element.30.unrot_ref), custom_call_target="tpu_custom_call" | custom-call | flops 2415919104 | bytes 9437184 | tf_op jit(solution)/shard_map/pallas_call | solution.py:184
  105.4 8.1 %collective-permute-start.4 = (f16[32,16,1152]{2,1,0:T(8,128)(2,1)S(1)}, f16[32,16,1152]{2,1,0:T(8,128)(2,1)S(1)}, u32[]{:S(2)}, u32[]{:S(2)}) collective-permute-start(f16[32,16,1152]{2,1,0:T(8,128)(2,1)S(1)} %convert_element_type.61), channel_id=1, source_target_pairs={{0,16},{16,0},{1,17},{17,1},{2,18},{18,2},{3,19},{19,3},{4,20},{20... | collective-permute-start | bytes 3538952 | tf_op jit(solution)/shard_map/ppermute | solution.py:265
  113.5 2.5 %collective-permute-done.4 = f16[32,16,1152]{2,1,0:T(8,128)(2,1)S(1)} collective-permute-done((f16[32,16,1152]{2,1,0:T(8,128)(2,1)S(1)}, f16[32,16,1152]{2,1,0:T(8,128)(2,1)S(1)}, u32[]{:S(2)}, u32[]{:S(2)}) %collective-permute-start.4) | collective-permute-done | bytes 1179680 | tf_op jit(solution)/shard_map/ppermute | solution.py:265
  116.0 0.4 add_convert_fusion
  116.4 26.3 %all_to_all.22 = f16[32,16,1152]{2,1,0:T(8,128)(2,1)S(1)} all-to-all(f16[32,16,1152]{2,1,0:T(8,128)(2,1)S(1)} %add_convert_fusion), channel_id=1, replica_groups=mesh['col'=8,'core'=2,'yh'=2,'zq'=4,'zl'=2] {'col','yh','zl'}, dimensions={0} | all-to-all | bytes 2359296 | tf_op jit(solution)/shard_map/all_to_all | solution.py:267
  143.1 0.7 reshape.254
  (43 shorter events, 2.2 us)
Async XLA Ops:
  0.0 8.9 %copy-start.3 = (s32[128]{0:T(128)S(1)}, s32[128]{0:T(128)}, u32[]{:S(2)}) copy-start(s32[128]{0:T(128)} %param.8) | copy-start | bytes 1540
  1.7 9.2 %copy-start.2 = (bf16[16,2,512]{2,1,0:T(2,128)(2,1)S(1)}, bf16[16,2,512]{2,1,0:T(2,128)(2,1)}, u32[]{:S(2)}) copy-start(bf16[16,2,512]{2,1,0:T(2,128)(2,1)} %param.7) | copy-start | bytes 98308
  3.5 7.5 %collective-permute-start.2 = (bf16[128,512]{1,0:T(8,128)(2,1)S(1)}, bf16[128,512]{1,0:T(8,128)(2,1)S(1)}, u32[]{:S(2)}, u32[]{:S(2)}) collective-permute-start(bf16[128,512]{1,0:T(8,128)(2,1)S(1)} %get-tuple-element.37), channel_id=1, source_target_pairs={{0,9},{1,8},{8,1},{9,0},{2,11},{3,10},{10,3},{11,2},{4,13},{5,12},... | collective-permute-start | bytes 393224 | tf_op jit(solution)/shard_map/ppermute | solution.py:230
  8.6 5.5 %collective-permute-start = (bf16[128,512]{1,0:T(8,128)(2,1)S(1)}, bf16[128,512]{1,0:T(8,128)(2,1)S(1)}, u32[]{:S(2)}, u32[]{:S(2)}) collective-permute-start(bf16[128,512]{1,0:T(8,128)(2,1)S(1)} %get-tuple-element.38), channel_id=1, source_target_pairs={{0,1},{1,0},{8,9},{9,8},{2,3},{3,2},{10,11},{11,10},{4,5},{5,4},{1... | collective-permute-start | bytes 393224 | tf_op jit(solution)/shard_map/ppermute | solution.py:230
  8.6 7.9 %collective-permute-start.1 = (bf16[128,512]{1,0:T(8,128)(2,1)S(1)}, bf16[128,512]{1,0:T(8,128)(2,1)S(1)}, u32[]{:S(2)}, u32[]{:S(2)}) collective-permute-start(bf16[128,512]{1,0:T(8,128)(2,1)S(1)} %get-tuple-element.39), channel_id=1, source_target_pairs={{0,8},{1,9},{8,0},{9,1},{2,10},{3,11},{10,2},{11,3},{4,12},{5,13},... | collective-permute-start | bytes 393224 | tf_op jit(solution)/shard_map/ppermute | solution.py:230
  11.0 6.6 %copy-start.4 = (bf16[128,512]{1,0:T(8,128)(2,1)}, bf16[128,512]{1,0:T(8,128)(2,1)S(1)}, u32[]{:S(2)}) copy-start(bf16[128,512]{1,0:T(8,128)(2,1)S(1)} %collective-permute-done.2.refs_3_) | copy-start | bytes 393220
  14.1 3.5 %copy-start.5 = (bf16[128,512]{1,0:T(8,128)(2,1)}, bf16[128,512]{1,0:T(8,128)(2,1)S(1)}, u32[]{:S(2)}) copy-start(bf16[128,512]{1,0:T(8,128)(2,1)S(1)} %collective-permute-done.refs_1_) | copy-start | bytes 393220
  16.5 1.1 copy-start.6
  17.6 26.6 %all-to-all-start = ((bf16[32,32,512]{2,1,0:T(8,128)(2,1)}), bf16[32,32,512]{2,1,0:T(8,128)(2,1)S(1)}, u32[]{:S(2)}, u32[]{:S(2)}) async-start(bf16[32,32,512]{2,1,0:T(8,128)(2,1)} %broadcast_in_dim.21), calls=%async_computation | async-start | bytes 2097152 | tf_op jit(solution)/shard_map/all_to_all | solution.py:247
  44.2 3.3 %copy-start = (bf16[32,32,512]{2,1,0:T(8,128)(2,1)}, bf16[32,32,512]{2,1,0:T(8,128)(2,1)S(1)}, u32[]{:S(2)}) copy-start(bf16[32,32,512]{2,1,0:T(8,128)(2,1)S(1)} %all-to-all-done.own_ref) | copy-start | bytes 3145732
  44.2 3.2 %collective-permute-start.3 = (bf16[32,32,512]{2,1,0:T(8,128)(2,1)S(1)}, bf16[32,32,512]{2,1,0:T(8,128)(2,1)S(1)}, u32[]{:S(2)}, u32[]{:S(2)}) collective-permute-start(bf16[32,32,512]{2,1,0:T(8,128)(2,1)S(1)} %all-to-all-done.own_ref), channel_id=1, source_target_pairs={{0,16},{16,0},{1,17},{17,1},{2,18},{18,2},{3,19},{19,3},{4,20},{20... | collective-permute-start | bytes 3145736 | tf_op jit(solution)/shard_map/ppermute | solution.py:252
  47.4 1.0 copy-start.1
  105.4 10.5 %collective-permute-start.4 = (f16[32,16,1152]{2,1,0:T(8,128)(2,1)S(1)}, f16[32,16,1152]{2,1,0:T(8,128)(2,1)S(1)}, u32[]{:S(2)}, u32[]{:S(2)}) collective-permute-start(f16[32,16,1152]{2,1,0:T(8,128)(2,1)S(1)} %convert_element_type.61), channel_id=1, source_target_pairs={{0,16},{16,0},{1,17},{17,1},{2,18},{18,2},{3,19},{19,3},{4,20},{20... | collective-permute-start | bytes 3538952 | tf_op jit(solution)/shard_map/ppermute | solution.py:265

commit v4 on v3

--- a/solution.py
+++ b/solution.py
@@ -29,15 +29,16 @@
             rows_ref[parts : 2 * parts, at] = (imag_part * cosine - real_part * sine).astype(BF16)
             rows_ref[2 * parts :, at] = msg[2 * parts : 2 * parts + 16]
             code = msg[2 * parts + 16 :].astype(F32)
-            goal = jnp.where(code > 0.0, code - 1.0, 255.0 - code)
+            goal = jnp.where(code > 0.0, code - 257.0, -1.0 - code)
             rot_ref[:, :, at] = goal.reshape(rot_ref.shape[0], 8, block)
 
-    place = lax.broadcasted_iota(jnp.int32, (block, block), 1).astype(F32)
+    place = (lax.broadcasted_iota(jnp.int32, (block, block), 1).astype(F32) - 256.0).astype(BF16)
+    one, zero = jnp.ones((), BF16), jnp.zeros((), BF16)
     gain_ref[...] = jnp.zeros_like(gain_ref)
     for b in range(len(msgs)):
         at = slice(b * block, (b + 1) * block)
-        goal = rot_ref[step, :, at].T
-        tables = [jnp.where(place == goal[:, i : i + 1], 1.0, 0.0).astype(BF16) for i in range(GROUP)]
+        goal = rot_ref[step, :, at].T.astype(BF16)
+        tables = [jnp.where(place == goal[:, i : i + 1], one, zero) for i in range(GROUP)]
         out = jnp.dot(rows_ref[:, at], jnp.concatenate(tables, axis=1), preferred_element_type=F32)
         turned = [out[:, i * block : (i + 1) * block] for i in range(GROUP)]
         gains = [jnp.sum(t[2 * parts :], axis=0, keepdims=True) for t in turned]
@@ -78,7 +79,7 @@
     )(cosine, sine, *msgs)
 
 
-def score_kernel(peers, per_step, place_ref, weighted_ref, gain_ref, own_ref, other_ref, out_ref, refs_ref, norm_ref):
+def score_kernel(peers, per_step, place_ref, w0_ref, w1_ref, w2_ref, w3_ref, gain_ref, own_ref, other_ref, out_ref, refs_ref, norm_ref):
     step = pl.program_id(0)
     count, k2, block = own_ref.shape
     k_dev = k2 // 2
@@ -101,8 +102,11 @@
             part = 0.5 * jnp.dot(gain, power, preferred_element_type=F32, precision=lax.Precision.HIGHEST)
             norm_ref[...] = part if b == 0 else norm_ref[...] + part
 
-    cross = jnp.dot(weighted_ref[0], refs_ref[0], preferred_element_type=F32)
-    cross += jnp.dot(weighted_ref[1], refs_ref[1], preferred_element_type=F32)
+    cross = 0.0
+    for j, ref in enumerate((w0_ref, w1_ref, w2_ref, w3_ref)):
+        width = ref.shape[2]
+        held = refs_ref[j // 2, j % 2 * width : (j % 2 + 1) * width, :]
+        cross += jnp.dot(ref[0], held, preferred_element_type=F32)
     rows = cross.shape[0] // (per_step * GROUP * peers)
     for g in range(per_step):
         norm = norm_ref[pl.ds(pl.multiple_of((step * per_step + g) * 8, 8), 8), :]
@@ -112,6 +116,14 @@
                     start = (((g * (GROUP // 2) + q) * peers + p) * 2 + i) * rows
                     to = (g * GROUP + q * 2 + i) * rows
                     out_ref[p, to : to + rows, :] = cross[start : start + rows] - norm[q * 2 + i : q * 2 + i + 1]
+
+
+def streams(rows, pixels):
+    return [
+        pl.BlockSpec((1, rows, pixels // 2), functools.partial(lambda c, h, i: (c, i, h), c, h))
+        for c in range(2)
+        for h in range(2)
+    ]
 
 
 def score(place, weighted, gain, own, other, peers, per_step):
@@ -125,7 +137,7 @@
         grid=(steps,),
         in_specs=[
             SCALAR,
-            pl.BlockSpec((2, rows, pixels), lambda i: (0, i, 0)),
+            *streams(rows, pixels),
             pl.BlockSpec(gain.shape, lambda i: (0, 0, 0)),
             pl.BlockSpec(own.shape, lambda i: (0, 0, 0)),
             pl.BlockSpec(other.shape, lambda i: (0, 0, 0)),
@@ -133,29 +145,26 @@
         out_specs=pl.BlockSpec((peers, rows // peers, classes), lambda i: (0, i, 0)),
         out_shape=jax.ShapeDtypeStruct((peers, rows // peers * steps, classes), F32),
         scratch_shapes=[pltpu.VMEM((2, pixels, classes), BF16), pltpu.VMEM((groups * 8, classes), F32)],
-        compiler_params=pltpu.CompilerParams(vmem_limit_bytes=54 * MIB),
-    )(place, weighted, gain, own, other)
-
-
-def sums_kernel(steps, block, k_dev, place_ref, weights_ref, unrot_ref, own_ref, other_ref, acc_ref, totals_ref):
+        compiler_params=pltpu.CompilerParams(vmem_limit_bytes=50 * MIB),
+    )(place, *[weighted] * 4, gain, own, other)
+
+
+def sums_kernel(steps, block, k_dev, place_ref, weights_ref, u0_ref, u1_ref, u2_ref, u3_ref, own_ref, other_ref, acc_ref, totals_ref):
     step = pl.program_id(0)
     peers, mine, classes = weights_ref.shape
     picked = [weights_ref[p, q * 16 : (q + 1) * 16, :] for q in range(mine // 16) for p in range(peers)]
     turned = jnp.concatenate(picked).astype(F32).T.astype(BF16)
     count = jnp.dot(turned, jnp.ones((turned.shape[1], 128), BF16), preferred_element_type=F32)
-    terms = [jnp.dot(turned, unrot_ref[c], preferred_element_type=F32) for c in range(2)]
 
     @pl.when(step == 0)
     def _():
-        for c in range(2):
-            acc_ref[c] = terms[c]
-        totals_ref[...] = count
-
-    @pl.when(step > 0)
-    def _():
-        for c in range(2):
-            acc_ref[c] += terms[c]
-        totals_ref[...] += count
+        acc_ref[...] = jnp.zeros_like(acc_ref)
+        totals_ref[...] = jnp.zeros_like(totals_ref)
+
+    totals_ref[...] += count
+    for j, ref in enumerate((u0_ref, u1_ref, u2_ref, u3_ref)):
+        width = ref.shape[2]
+        acc_ref[j // 2, :, j % 2 * width : (j % 2 + 1) * width] += jnp.dot(turned, ref[0], preferred_element_type=F32)
 
     @pl.when(step == steps - 1)
     def _():
@@ -187,7 +196,7 @@
         in_specs=[
             SCALAR,
             pl.BlockSpec((peers, mine, classes), lambda i: (0, i, 0)),
-            pl.BlockSpec((2, mine * peers, pixels), lambda i: (0, i, 0)),
+            *streams(mine * peers, pixels),
         ],
         out_specs=[pl.BlockSpec(out, lambda i: (0, 0, 0))] * 2,
         out_shape=[jax.ShapeDtypeStruct(out, F32)] * 2,
@@ -196,7 +205,7 @@
         cost_estimate=pl.CostEstimate(
             flops=4 * classes * total * peers * pixels, bytes_accessed=unrot.size * 2, transcendentals=0
         ),
-    )(place, weights, unrot)
+    )(place, weights, *[unrot] * 4)
 
 
 def shards(particles, references, trans_index, shell_map, rot_index, inv_sigma):
@@ -242,8 +251,8 @@
     cosine, sine = jnp.cos(phase), jnp.sin(phase)
 
     mine = references.transpose(1, 0, 2).reshape(1, 2 * k_dev, freq)
+    mine = jnp.broadcast_to(mine, (4 * cols, 2 * k_dev, freq))
     mine, msgs, cosine, sine = lax.optimization_barrier((mine, msgs, cosine, sine))
-    mine = jnp.broadcast_to(mine, (4 * cols, 2 * k_dev, freq))
     refs = lax.all_to_all(mine, ("col", "yh", "zl"), 0, 0)
 
     unrot, weighted, gain_unrot = unrotate(cosine, sine, msgs, rots, zqs)

time: 144 us -> 140 us (0.972)
  Pallas kernels: 36.5 us -> 33.5 us
    pallas_call x1, Pallas kernels: 9.17 us -> 7.43 us  [score(): pl.pallas_call(functools.partial(score_kernel, peers, per_step), grid=(st...]
  transfers between devices with their start and end apart: 6 -> 6, of which waited for: 5 -> 5; matrix products, arithmetic and copies ran while one was open for 1% -> 1% of each run, Pallas kernels for 14% -> 13%
where the time goes in v4:
time: 140 us; the launch traced here: 139 us
  blocking collectives  63.6 us (45%)
  Pallas kernels  33.5 us (24%)
  starting transfers between devices  21.1 us (15%)
  waiting for transfers between devices  10.4 us (7%)
  other arithmetic  6.1 us (4%)
  local copies, waits for them, and re-layouts  4.22 us (3%)
    all_to_all x1, blocking collectives, shards(): message = lax.all_to_all(message, ('col', 'yh', 'zl'), 0, 0)  25.9 us
    all_to_all x1, blocking collectives, shards(): lax.all_to_all(partial, 'zq', 0, 0).astype(F32)  21.3 us
    pallas_call x1, Pallas kernels, unrotate(): pl.pallas_call(functools.partial(unrotate_kernel, peers), grid=(steps,),...  18.7 us
    all_to_all x1, blocking collectives, shards(): weights = lax.all_to_all(spread, 'zq', 0, 0)  16.4 us
    ppermute x1, starting transfers between devices, shards(): other = lax.ppermute(other.astype(F16), 'core', [(0, 1), (1, 0)])  8.03 us
    pallas_call x1, Pallas kernels, score(): pl.pallas_call(functools.partial(score_kernel, peers, per_step), grid=(st...  7.43 us
    pallas_call x1, Pallas kernels, class_sums(): pl.pallas_call(functools.partial(sums_kernel, steps, block, k_dev), grid=...  7.43 us
    all_to_all x1, starting transfers between devices, shards(): refs = lax.all_to_all(mine, ('col', 'yh', 'zl'), 0, 0)  6.79 us
  transfers between devices with their start and end apart: 6, of which 5 were waited for; matrix products, arithmetic and copies ran while one was open for 1% of the time, Pallas kernels for 13%

profile of v4, /device:TPU:1, one launch (start us, length us, event | category | flops | bytes accessed | tf_op | source)
XLA Modules:
  0.0 139.2 jit_solution(17349293529852803002)
XLA Ops:
  0.0 0.8 select_reduce_fusion
  0.8 0.9 select_convert_fusion
  1.8 1.0 constant_dynamic-slice_fusion
  2.8 0.7 pad_maximum_fusion.4
  3.5 5.1 %collective-permute-start.2 = (bf16[128,512]{1,0:T(8,128)(2,1)S(1)}, bf16[128,512]{1,0:T(8,128)(2,1)S(1)}, u32[]{:S(2)}, u32[]{:S(2)}) collective-permute-start(bf16[128,512]{1,0:T(8,128)(2,1)S(1)} %get-tuple-element.37), channel_id=1, source_target_pairs={{0,9},{1,8},{8,1},{9,0},{2,11},{3,10},{10,3},{11,2},{4,13},{5,12},... | collective-permute-start | bytes 393224 | tf_op jit(solution)/shard_map/ppermute | solution.py:239
  8.6 0.3 collective-permute-start.1
  9.0 1.8 %fusion = (f32[32,2048]{1,0:T(8,128)}, f32[32,2048]{1,0:T(8,128)}) fusion(f32[2048]{0:T(1024)S(1)} %get-tuple-element.44, f32[32]{0:T(128)S(1)} %get-tuple-element.49, f32[2048]{0:T(1024)S(1)} %get-tuple-element.43, f32[32]{0:T(128)S(1)} %get-tuple-element.48), kind=kLoop, calls=%fused_computation.6 | loop fusion | flops 262144 | bytes 540928 | tf_op jit(solution)/shard_map/sin | solution.py:251
  11.0 3.2 %collective-permute-done.refs_1_ = bf16[128,512]{1,0:T(8,128)(2,1)S(1)} collective-permute-done((bf16[128,512]{1,0:T(8,128)(2,1)S(1)}, bf16[128,512]{1,0:T(8,128)(2,1)S(1)}, u32[]{:S(2)}, u32[]{:S(2)}) %collective-permute-start) | collective-permute-done | bytes 131104 | tf_op jit(solution)/shard_map/ppermute | solution.py:239
  14.1 2.3 %collective-permute-done.1.refs_2_ = bf16[128,512]{1,0:T(8,128)(2,1)S(1)} collective-permute-done((bf16[128,512]{1,0:T(8,128)(2,1)S(1)}, bf16[128,512]{1,0:T(8,128)(2,1)S(1)}, u32[]{:S(2)}, u32[]{:S(2)}) %collective-permute-start.1) | collective-permute-done | bytes 131104 | tf_op jit(solution)/shard_map/ppermute | solution.py:239
  16.5 1.1 broadcast_in_dim.19
  17.6 6.8 %all-to-all-start = ((bf16[32,32,512]{2,1,0:T(8,128)(2,1)}), bf16[32,32,512]{2,1,0:T(8,128)(2,1)S(1)}, u32[]{:S(2)}, u32[]{:S(2)}) async-start(bf16[32,32,512]{2,1,0:T(8,128)(2,1)} %broadcast_in_dim.19), calls=%async_computation | async-start | bytes 2097152 | tf_op jit(solution)/shard_map/all_to_all | solution.py:256
  24.4 18.7 %shard_map.64 = (bf16[2,1152,2048]{2,1,0:T(8,128)(2,1)}, bf16[2,1152,2048]{2,1,0:T(8,128)(2,1)}, f32[6,8,2048]{2,1,0:T(8,128)}) custom-call(f32[32,2048]{1,0:T(8,128)} %get-tuple-element.20.cos_ref, f32[32,2048]{1,0:T(8,128)} %get-tuple-element.21.sin_ref, bf16[128,512]{1,0:T(8,128)(2,1)} %get-tuple-element.22.refs_0_, bf16[128,512]{1,0:T(8,128)(2,1)} %copy-done.4, ...), custom_call_target="tpu_custom_call" | custom-call | flops 6039797760 | bytes 18874368 | tf_op jit(solution)/shard_map/pallas_call | solution.py:66
  43.1 0.9 collective-permute-start.3
  44.0 2.3 %collective-permute-done.3.other_ref = bf16[32,32,512]{2,1,0:T(8,128)(2,1)S(1)} collective-permute-done((bf16[32,32,512]{2,1,0:T(8,128)(2,1)S(1)}, bf16[32,32,512]{2,1,0:T(8,128)(2,1)S(1)}, u32[]{:S(2)}, u32[]{:S(2)}) %collective-permute-start.3) | collective-permute-done | bytes 1048608 | tf_op jit(solution)/shard_map/ppermute | solution.py:261
  46.3 1.0 copy-done
  47.3 7.4 %shard_map.65 = f32[4,288,256]{2,1,0:T(8,128)S(1)} custom-call(s32[1]{0:T(128)} %bitcast.place_ref, bf16[2,1152,2048]{2,1,0:T(8,128)(2,1)} %get-tuple-element.27.w0_ref.w1_ref.w2_ref.w3_ref, bf16[2,1152,2048]{2,1,0:T(8,128)(2,1)} %get-tuple-element.27.w0_ref.w1_ref.w2_ref.w3_ref, bf16[2,1152,2048]{2,1,0:T(8,128)(2,1)} %get-tuple-element.27.w0_ref.w1_ref.w2_ref.w3_ref, ...), custom_call_target="tpu_custom_call" | custom-call | tf_op jit(solution)/shard_map/pallas_call | solution.py:135
  54.9 21.3 %all_to_all.20 = f16[4,288,256]{2,1,0:T(8,128)(2,1)S(1)} all-to-all(f16[4,288,256]{2,1,0:T(8,128)(2,1)S(1)} %convert_element_type.58), channel_id=1, replica_groups=mesh['col'=8,'core'=2,'yh'=2,'zq'=4,'zl'=2] {'zq'}, dimensions={0} | all-to-all | bytes 1179648 | tf_op jit(solution)/shard_map/all_to_all | solution.py:266
  77.3 16.4 %all_to_all.21.weights_ref = bf16[4,288,256]{2,1,0:T(8,128)(2,1)S(1)} all-to-all(bf16[4,288,256]{2,1,0:T(8,128)(2,1)S(1)} %broadcast_in_dim.22), channel_id=1, replica_groups=mesh['col'=8,'core'=2,'yh'=2,'zq'=4,'zl'=2] {'zq'}, dimensions={0} | all-to-all | bytes 1179648 | tf_op jit(solution)/shard_map/all_to_all | solution.py:271
  93.7 7.4 %shard_map.66 = (f32[32,16,1152]{2,1,0:T(8,128)S(1)}, f32[32,16,1152]{2,1,0:T(8,128)S(1)}) custom-call(s32[1]{0:T(128)} %bitcast.place_ref, bf16[4,288,256]{2,1,0:T(8,128)(2,1)S(1)} %all_to_all.21.weights_ref, bf16[2,1152,2048]{2,1,0:T(8,128)(2,1)} %get-tuple-element.30.u0_ref.u1_ref.u2_ref.u3_ref, ...), custom_call_target="tpu_custom_call" | custom-call | flops 2415919104 | bytes 9437184 | tf_op jit(solution)/shard_map/pallas_call | solution.py:193
  101.2 8.0 %collective-permute-start.4 = (f16[32,16,1152]{2,1,0:T(8,128)(2,1)S(1)}, f16[32,16,1152]{2,1,0:T(8,128)(2,1)S(1)}, u32[]{:S(2)}, u32[]{:S(2)}) collective-permute-start(f16[32,16,1152]{2,1,0:T(8,128)(2,1)S(1)} %convert_element_type.61), channel_id=1, source_target_pairs={{0,16},{16,0},{1,17},{17,1},{2,18},{18,2},{3,19},{19,3},{4,20},{20... | collective-permute-start | bytes 3538952 | tf_op jit(solution)/shard_map/ppermute | solution.py:274
  109.3 2.5 %collective-permute-done.4 = f16[32,16,1152]{2,1,0:T(8,128)(2,1)S(1)} collective-permute-done((f16[32,16,1152]{2,1,0:T(8,128)(2,1)S(1)}, f16[32,16,1152]{2,1,0:T(8,128)(2,1)S(1)}, u32[]{:S(2)}, u32[]{:S(2)}) %collective-permute-start.4) | collective-permute-done | bytes 1179680 | tf_op jit(solution)/shard_map/ppermute | solution.py:274
  111.7 0.4 add_convert_fusion
  112.1 25.9 %all_to_all.22 = f16[32,16,1152]{2,1,0:T(8,128)(2,1)S(1)} all-to-all(f16[32,16,1152]{2,1,0:T(8,128)(2,1)S(1)} %add_convert_fusion), channel_id=1, replica_groups=mesh['col'=8,'core'=2,'yh'=2,'zq'=4,'zl'=2] {'col','yh','zl'}, dimensions={0} | all-to-all | bytes 2359296 | tf_op jit(solution)/shard_map/all_to_all | solution.py:276
  138.5 0.7 reshape.252
  (41 shorter events, 2.0 us)
Async XLA Ops:
  0.0 8.9 %copy-start.2 = (s32[128]{0:T(128)S(1)}, s32[128]{0:T(128)}, u32[]{:S(2)}) copy-start(s32[128]{0:T(128)} %param.8) | copy-start | bytes 1540
  1.7 9.1 %copy-start.1 = (bf16[16,2,512]{2,1,0:T(2,128)(2,1)S(1)}, bf16[16,2,512]{2,1,0:T(2,128)(2,1)}, u32[]{:S(2)}) copy-start(bf16[16,2,512]{2,1,0:T(2,128)(2,1)} %param.7) | copy-start | bytes 98308
  3.5 7.5 %collective-permute-start.2 = (bf16[128,512]{1,0:T(8,128)(2,1)S(1)}, bf16[128,512]{1,0:T(8,128)(2,1)S(1)}, u32[]{:S(2)}, u32[]{:S(2)}) collective-permute-start(bf16[128,512]{1,0:T(8,128)(2,1)S(1)} %get-tuple-element.37), channel_id=1, source_target_pairs={{0,9},{1,8},{8,1},{9,0},{2,11},{3,10},{10,3},{11,2},{4,13},{5,12},... | collective-permute-start | bytes 393224 | tf_op jit(solution)/shard_map/ppermute | solution.py:239
  8.6 5.5 %collective-permute-start = (bf16[128,512]{1,0:T(8,128)(2,1)S(1)}, bf16[128,512]{1,0:T(8,128)(2,1)S(1)}, u32[]{:S(2)}, u32[]{:S(2)}) collective-permute-start(bf16[128,512]{1,0:T(8,128)(2,1)S(1)} %get-tuple-element.38), channel_id=1, source_target_pairs={{0,1},{1,0},{8,9},{9,8},{2,3},{3,2},{10,11},{11,10},{4,5},{5,4},{1... | collective-permute-start | bytes 393224 | tf_op jit(solution)/shard_map/ppermute | solution.py:239
  8.6 7.9 %collective-permute-start.1 = (bf16[128,512]{1,0:T(8,128)(2,1)S(1)}, bf16[128,512]{1,0:T(8,128)(2,1)S(1)}, u32[]{:S(2)}, u32[]{:S(2)}) collective-permute-start(bf16[128,512]{1,0:T(8,128)(2,1)S(1)} %get-tuple-element.39), channel_id=1, source_target_pairs={{0,8},{1,9},{8,0},{9,1},{2,10},{3,11},{10,2},{11,3},{4,12},{5,13},... | collective-permute-start | bytes 393224 | tf_op jit(solution)/shard_map/ppermute | solution.py:239
  11.0 6.6 %copy-start.3 = (bf16[128,512]{1,0:T(8,128)(2,1)}, bf16[128,512]{1,0:T(8,128)(2,1)S(1)}, u32[]{:S(2)}) copy-start(bf16[128,512]{1,0:T(8,128)(2,1)S(1)} %collective-permute-done.2.refs_3_) | copy-start | bytes 393220
  14.1 3.5 %copy-start.4 = (bf16[128,512]{1,0:T(8,128)(2,1)}, bf16[128,512]{1,0:T(8,128)(2,1)S(1)}, u32[]{:S(2)}) copy-start(bf16[128,512]{1,0:T(8,128)(2,1)S(1)} %collective-permute-done.refs_1_) | copy-start | bytes 393220
  16.5 1.1 copy-start.5
  17.6 25.5 %all-to-all-start = ((bf16[32,32,512]{2,1,0:T(8,128)(2,1)}), bf16[32,32,512]{2,1,0:T(8,128)(2,1)S(1)}, u32[]{:S(2)}, u32[]{:S(2)}) async-start(bf16[32,32,512]{2,1,0:T(8,128)(2,1)} %broadcast_in_dim.19), calls=%async_computation | async-start | bytes 2097152 | tf_op jit(solution)/shard_map/all_to_all | solution.py:256
  43.1 3.2 %collective-permute-start.3 = (bf16[32,32,512]{2,1,0:T(8,128)(2,1)S(1)}, bf16[32,32,512]{2,1,0:T(8,128)(2,1)S(1)}, u32[]{:S(2)}, u32[]{:S(2)}) collective-permute-start(bf16[32,32,512]{2,1,0:T(8,128)(2,1)S(1)} %all-to-all-done.own_ref), channel_id=1, source_target_pairs={{0,16},{16,0},{1,17},{17,1},{2,18},{18,2},{3,19},{19,3},{4,20},{20... | collective-permute-start | bytes 3145736 | tf_op jit(solution)/shard_map/ppermute | solution.py:261
  46.3 1.0 copy-start
  101.2 10.5 %collective-permute-start.4 = (f16[32,16,1152]{2,1,0:T(8,128)(2,1)S(1)}, f16[32,16,1152]{2,1,0:T(8,128)(2,1)S(1)}, u32[]{:S(2)}, u32[]{:S(2)}) collective-permute-start(f16[32,16,1152]{2,1,0:T(8,128)(2,1)S(1)} %convert_element_type.61), channel_id=1, source_target_pairs={{0,16},{16,0},{1,17},{17,1},{2,18},{18,2},{3,19},{19,3},{4,20},{20... | collective-permute-start | bytes 3538952 | tf_op jit(solution)/shard_map/ppermute | solution.py:274

commit v5 on v4

--- a/solution.py
+++ b/solution.py
@@ -10,6 +10,48 @@
 MIB = 1024 * 1024
 GROUP = 6
 SCALAR = pl.BlockSpec(memory_space=pltpu.SMEM)
+
+
+def prepare_kernel(spot_ref, sigma_ref, particles_ref, rot_ref, shell_ref, mine_ref, *refs):
+    msgs, spread_ref = refs[:-1], refs[-1]
+    few, freq = particles_ref.shape[1] // 4, rot_ref.shape[1]
+    shell = shell_ref[...]
+    gain = jnp.zeros((1, freq), F32)
+    for s in range(sigma_ref.shape[0]):
+        gain = jnp.where(shell == s, sigma_ref[s], gain)
+    top = gain.astype(BF16).astype(F32)
+    middle = (gain - top).astype(BF16).astype(F32)
+    low = gain - top - middle
+    gains = jnp.concatenate([top, middle, low, jnp.zeros((13, freq), F32)]).astype(BF16)
+    local = rot_ref[...] - spot_ref[1]
+    code = jnp.where(local < 256, local + 1, 255 - local).astype(F32)
+    gap = jnp.zeros((8 - GROUP, freq), F32)
+    rows = []
+    for g in range(rot_ref.shape[0] // GROUP):
+        rows += [code[g * GROUP : (g + 1) * GROUP], gap]
+    code = jnp.concatenate(rows).astype(BF16)
+    for b, msg in enumerate(msgs):
+        start = pl.multiple_of((spot_ref[0] ^ b) * few, few)
+        for c in range(2):
+            msg[c * few : (c + 1) * few, :] = particles_ref[c, pl.ds(start, few), :]
+        msg[2 * few : 2 * few + 16, :] = gains
+        msg[2 * few + 16 :, :] = code
+    for j in range(spread_ref.shape[0]):
+        spread_ref[j] = mine_ref[...]
+
+
+def prepare(spot, inv_sigma, particles, rot_index, shell_map, mine, count):
+    _, parts, freq = particles.shape
+    rows = parts // 2 + 16 + rot_index.shape[0] // GROUP * 8
+    whole = pl.BlockSpec(memory_space=pltpu.VMEM)
+    return pl.pallas_call(
+        prepare_kernel,
+        in_specs=[SCALAR, SCALAR, whole, whole, whole, whole],
+        out_specs=[whole] * 5,
+        out_shape=[jax.ShapeDtypeStruct((rows, freq), BF16)] * 4
+        + [jax.ShapeDtypeStruct((count,) + mine.shape, BF16)],
+        compiler_params=pltpu.CompilerParams(vmem_limit_bytes=16 * MIB),
+    )(spot, inv_sigma, particles, rot_index, shell_map[None], mine)
 
 
 def unrotate_kernel(peers, cos_ref, sin_ref, *refs):
@@ -212,7 +254,6 @@
     _, parts, freq = particles.shape
     k_dev = references.shape[0]
     rots = rot_index.shape[0]
-    shells = inv_sigma.shape[0]
     cols, zqs = lax.axis_size("col"), lax.axis_size("zq")
     few = parts // 4
     classes = 2 * cols * k_dev
@@ -221,23 +262,11 @@
     place = yh * 2 + zl
 
     base = (yh * half + zq * 2 + zl) * freq
-    local_rot = rot_index - base
-    code = jnp.where(local_rot < 256, local_rot + 1, 255 - local_rot).astype(BF16)
-    code = jnp.pad(code.reshape(rots // GROUP, GROUP, freq), ((0, 0), (0, 8 - GROUP), (0, 0)))
-    select = shell_map[:, None] == jnp.arange(shells, dtype=jnp.int32)[None, :]
-    gain = jnp.sum(jnp.where(select, inv_sigma[None, :], 0.0), axis=1)
-    top = lax.reduce_precision(gain, 8, 7)
-    middle = lax.reduce_precision(gain - top, 8, 7)
-    low = gain - top - middle
-    gains = jnp.pad(jnp.stack([top, middle, low]).astype(BF16), ((0, 13), (0, 0)))
-    side = jnp.concatenate([gains, code.reshape(rots // GROUP * 8, freq)])
-    msgs = []
-    for b in range(4):
-        chunk = lax.dynamic_slice_in_dim(particles, (place ^ b) * few, few, 1).reshape(2 * few, freq)
-        msg = jnp.concatenate([chunk, side])
-        if b:
-            msg = lax.ppermute(msg, ("yh", "zl"), [(i, i ^ b) for i in range(4)])
-        msgs.append(msg)
+    spot = jnp.stack([place, base]).astype(jnp.int32)
+    mine = references.transpose(1, 0, 2).reshape(2 * k_dev, freq)
+    *msgs, mine = prepare(spot, inv_sigma, particles, rot_index, shell_map, mine, 4 * cols)
+    for b in range(1, 4):
+        msgs[b] = lax.ppermute(msgs[b], ("yh", "zl"), [(i, i ^ b) for i in range(4)])
 
     pos = jnp.arange(freq, dtype=jnp.int32)
     spots = [place ^ b for b in range(4)]
@@ -250,8 +279,6 @@
     phase = 2.0 * jnp.pi / 128.0 * (tx[:, None] * kx[None, :] + ty[:, None] * ky[None, :])
     cosine, sine = jnp.cos(phase), jnp.sin(phase)
 
-    mine = references.transpose(1, 0, 2).reshape(1, 2 * k_dev, freq)
-    mine = jnp.broadcast_to(mine, (4 * cols, 2 * k_dev, freq))
     mine, msgs, cosine, sine = lax.optimization_barrier((mine, msgs, cosine, sine))
     refs = lax.all_to_all(mine, ("col", "yh", "zl"), 0, 0)
 
@@ -260,8 +287,7 @@
     refs, weighted = lax.optimization_barrier((refs, weighted))
     refs_other = lax.ppermute(refs, "core", [(0, 1), (1, 0)])
 
-    spot = jnp.reshape(place, (1,)).astype(jnp.int32)
-    partial = score(spot, weighted, gain_unrot, refs, refs_other, zqs, 2).astype(F16)
+    partial = score(spot, weighted, gain_unrot, refs, refs_other, zqs, 3).astype(F16)
     own = few // zqs
     scores = jnp.sum(lax.all_to_all(partial, "zq", 0, 0).astype(F32), axis=0).reshape(rots, own, classes)
     peak = jnp.max(scores, axis=(0, 2), keepdims=True)
@@ -270,7 +296,7 @@
     spread = jnp.broadcast_to(weights.reshape(1, rots * own, classes), (zqs, rots * own, classes))
     weights = lax.all_to_all(spread, "zq", 0, 0)
 
-    message, other = class_sums(spot, weights, unrot, freq, k_dev, 3)
+    message, other = class_sums(spot, weights, unrot, freq, k_dev, 2)
     other = lax.ppermute(other.astype(F16), "core", [(0, 1), (1, 0)])
     message = (message + other.astype(F32)).astype(F16)
     message = lax.all_to_all(message, ("col", "yh", "zl"), 0, 0)

time: 140 us -> 141 us (level)
  local copies, waits for them, and re-layouts: 4.22 us -> 6.68 us
  waiting for transfers between devices: 10.4 us -> 8.31 us
  other arithmetic: 6.1 us -> 4.43 us
    unnamed x13 -> x18, local copies, waits for them, and re-layouts: 1.02 us -> 4.83 us
    ppermute x3, waiting for transfers between devices: 5.6 us -> 3.54 us  [shards(): lax.ppermute(msgs[b], ('yh', 'zl'), [(i, i ^ b) for i in range(4)])]
    pallas_call x0 -> x1, Pallas kernels: none -> 1.64 us  [prepare(): pl.pallas_call(prepare_kernel, in_specs=[SCALAR, SCALAR, whole, whole, wh...]
  transfers between devices with their start and end apart: 6 -> 6, of which waited for: 5 -> 4; matrix products, arithmetic and copies ran while one was open for 1% -> 2% of each run, Pallas kernels for 13% -> 13%
where the time goes in v5:
time: 141 us; the launch traced here: 140 us
  blocking collectives  64.3 us (46%)
  Pallas kernels  34.5 us (24%)
  starting transfers between devices  21.9 us (16%)
  waiting for transfers between devices  8.31 us (6%)
  local copies, waits for them, and re-layouts  6.68 us (5%)
  other arithmetic  4.43 us (3%)
    all_to_all x1, blocking collectives, shards(): message = lax.all_to_all(message, ('col', 'yh', 'zl'), 0, 0)  26.2 us
    all_to_all x1, blocking collectives, shards(): lax.all_to_all(partial, 'zq', 0, 0).astype(F32)  21.8 us
    pallas_call x1, Pallas kernels, unrotate(): pl.pallas_call(functools.partial(unrotate_kernel, peers), grid=(steps,),...  18.7 us
    all_to_all x1, blocking collectives, shards(): weights = lax.all_to_all(spread, 'zq', 0, 0)  16.4 us
    ppermute x1, starting transfers between devices, shards(): other = lax.ppermute(other.astype(F16), 'core', [(0, 1), (1, 0)])  8.04 us
    pallas_call x1, Pallas kernels, class_sums(): pl.pallas_call(functools.partial(sums_kernel, steps, block, k_dev), grid=...  7.24 us
    pallas_call x1, Pallas kernels, score(): pl.pallas_call(functools.partial(score_kernel, peers, per_step), grid=(st...  6.96 us
    all_to_all x1, starting transfers between devices, shards(): refs = lax.all_to_all(mine, ('col', 'yh', 'zl'), 0, 0)  6.63 us
  transfers between devices with their start and end apart: 6, of which 4 were waited for; matrix products, arithmetic and copies ran while one was open for 2% of the time, Pallas kernels for 13%

profile of v5, /device:TPU:1, one launch (start us, length us, event | category | flops | bytes accessed | tf_op | source)
XLA Modules:
  0.0 140.3 jit_solution(14064753233520175662)
XLA Ops:
  0.0 0.8 copy.12
  0.8 0.9 copy-done.1
  1.8 0.9 copy-done.2
  2.7 0.7 copy-done.3
  4.0 1.6 %shard_map.64 = (bf16[128,512]{1,0:T(8,128)(2,1)S(1)}, bf16[128,512]{1,0:T(8,128)(2,1)S(1)}, bf16[128,512]{1,0:T(8,128)(2,1)S(1)}, bf16[128,512]{1,0:T(8,128)(2,1)S(1)}, bf16[32,32,512]{2,1,0:T(8,128)(2,1)}) custom-call(s32[2]{0:T(128)S(1)} %pad_add_fusion.1.spot_ref.place_ref, f32[64]{0:T(128)S(1)} %copy-done.4, bf16[2,128,512]{2,1,0:T(8,128)(2,1)S(1)} %copy-done.1, ...), custom_call_target="tpu_custom_call" | custom-call | tf_op jit(solution)/shard_map/pallas_call | solution.py:47
  6.3 2.5 %collective-permute-start = (bf16[128,512]{1,0:T(8,128)(2,1)S(1)}, bf16[128,512]{1,0:T(8,128)(2,1)S(1)}, u32[]{:S(2)}, u32[]{:S(2)}) collective-permute-start(bf16[128,512]{1,0:T(8,128)(2,1)S(1)} %get-tuple-element.26), channel_id=1, source_target_pairs={{0,1},{1,0},{8,9},{9,8},{2,3},{3,2},{10,11},{11,10},{4,5},{5,4},{1... | collective-permute-start | bytes 393224 | tf_op jit(solution)/shard_map/ppermute | solution.py:269
  8.8 2.9 %collective-permute-start.1 = (bf16[128,512]{1,0:T(8,128)(2,1)S(1)}, bf16[128,512]{1,0:T(8,128)(2,1)S(1)}, u32[]{:S(2)}, u32[]{:S(2)}) collective-permute-start(bf16[128,512]{1,0:T(8,128)(2,1)S(1)} %get-tuple-element.27), channel_id=1, source_target_pairs={{0,8},{1,9},{8,0},{9,1},{2,10},{3,11},{10,2},{11,3},{4,12},{5,13},... | collective-permute-start | bytes 393224 | tf_op jit(solution)/shard_map/ppermute | solution.py:269
  11.7 0.7 fusion.12
  12.5 1.9 %fusion = (f32[32,2048]{1,0:T(8,128)}, f32[32,2048]{1,0:T(8,128)}) fusion(f32[2048]{0:T(1024)S(1)} %get-tuple-element.46, f32[32]{0:T(128)S(1)} %get-tuple-element.48, f32[2048]{0:T(1024)S(1)} %get-tuple-element.45, f32[32]{0:T(128)S(1)} %get-tuple-element.47), kind=kLoop, calls=%fused_computation.6 | loop fusion | flops 262144 | bytes 540928 | tf_op jit(solution)/shard_map/sin | solution.py:280
  14.4 2.2 %collective-permute-done.1.refs_2_ = bf16[128,512]{1,0:T(8,128)(2,1)S(1)} collective-permute-done((bf16[128,512]{1,0:T(8,128)(2,1)S(1)}, bf16[128,512]{1,0:T(8,128)(2,1)S(1)}, u32[]{:S(2)}, u32[]{:S(2)}) %collective-permute-start.1) | collective-permute-done | bytes 131104 | tf_op jit(solution)/shard_map/ppermute | solution.py:269
  16.6 1.3 collective-permute-done.2.refs_3_
  17.9 6.6 %all-to-all-start = ((bf16[32,32,512]{2,1,0:T(8,128)(2,1)}), bf16[32,32,512]{2,1,0:T(8,128)(2,1)S(1)}, u32[]{:S(2)}, u32[]{:S(2)}) async-start(bf16[32,32,512]{2,1,0:T(8,128)(2,1)} %get-tuple-element.29), calls=%async_computation | async-start | bytes 2097152 | tf_op jit(solution)/shard_map/all_to_all | solution.py:283
  24.6 18.7 %shard_map.65 = (bf16[2,1152,2048]{2,1,0:T(8,128)(2,1)}, bf16[2,1152,2048]{2,1,0:T(8,128)(2,1)}, f32[6,8,2048]{2,1,0:T(8,128)}) custom-call(f32[32,2048]{1,0:T(8,128)} %get-tuple-element.30.cos_ref, f32[32,2048]{1,0:T(8,128)} %get-tuple-element.31.sin_ref, bf16[128,512]{1,0:T(8,128)(2,1)} %copy-done.5, bf16[128,512]{1,0:T(8,128)(2,1)} %copy-done.6, ...), custom_call_target="tpu_custom_call" | custom-call | flops 6039797760 | bytes 18874368 | tf_op jit(solution)/shard_map/pallas_call | solution.py:108
  43.3 1.9 %collective-permute-start.3 = (bf16[32,32,512]{2,1,0:T(8,128)(2,1)S(1)}, bf16[32,32,512]{2,1,0:T(8,128)(2,1)S(1)}, u32[]{:S(2)}, u32[]{:S(2)}) collective-permute-start(bf16[32,32,512]{2,1,0:T(8,128)(2,1)S(1)} %all-to-all-done.own_ref), channel_id=1, source_target_pairs={{0,16},{16,0},{1,17},{17,1},{2,18},{18,2},{3,19},{19,3},{4,20},{20... | collective-permute-start | bytes 3145736 | tf_op jit(solution)/shard_map/ppermute | solution.py:288
  45.1 2.3 %collective-permute-done.3.other_ref = bf16[32,32,512]{2,1,0:T(8,128)(2,1)S(1)} collective-permute-done((bf16[32,32,512]{2,1,0:T(8,128)(2,1)S(1)}, bf16[32,32,512]{2,1,0:T(8,128)(2,1)S(1)}, u32[]{:S(2)}, u32[]{:S(2)}) %collective-permute-start.3) | collective-permute-done | bytes 1048608 | tf_op jit(solution)/shard_map/ppermute | solution.py:288
  47.4 1.0 copy-done
  48.4 7.0 %shard_map.66 = f32[4,288,256]{2,1,0:T(8,128)S(1)} custom-call(s32[2]{0:T(128)S(1)} %pad_add_fusion.1.spot_ref.place_ref, bf16[2,1152,2048]{2,1,0:T(8,128)(2,1)} %get-tuple-element.37.w0_ref.w1_ref.w2_ref.w3_ref, bf16[2,1152,2048]{2,1,0:T(8,128)(2,1)} %get-tuple-element.37.w0_ref.w1_ref.w2_ref.w3_ref, ...), custom_call_target="tpu_custom_call" | custom-call | tf_op jit(solution)/shard_map/pallas_call | solution.py:177
  55.5 21.8 %all_to_all.20 = f16[4,288,256]{2,1,0:T(8,128)(2,1)S(1)} all-to-all(f16[4,288,256]{2,1,0:T(8,128)(2,1)S(1)} %convert_element_type.49), channel_id=1, replica_groups=mesh['col'=8,'core'=2,'yh'=2,'zq'=4,'zl'=2] {'zq'}, dimensions={0} | all-to-all | bytes 1179648 | tf_op jit(solution)/shard_map/all_to_all | solution.py:292
  78.4 16.4 %all_to_all.21.weights_ref = bf16[4,288,256]{2,1,0:T(8,128)(2,1)S(1)} all-to-all(bf16[4,288,256]{2,1,0:T(8,128)(2,1)S(1)} %broadcast_in_dim.5), channel_id=1, replica_groups=mesh['col'=8,'core'=2,'yh'=2,'zq'=4,'zl'=2] {'zq'}, dimensions={0} | all-to-all | bytes 1179648 | tf_op jit(solution)/shard_map/all_to_all | solution.py:297
  94.7 7.2 %shard_map.67 = (f32[32,16,1152]{2,1,0:T(8,128)S(1)}, f32[32,16,1152]{2,1,0:T(8,128)S(1)}) custom-call(s32[2]{0:T(128)S(1)} %pad_add_fusion.1.spot_ref.place_ref, bf16[4,288,256]{2,1,0:T(8,128)(2,1)S(1)} %all_to_all.21.weights_ref, bf16[2,1152,2048]{2,1,0:T(8,128)(2,1)} %get-tuple-element.40.u0_ref.u1_ref.u2_ref.u3_ref, ...), custom_call_target="tpu_custom_call" | custom-call | flops 2415919104 | bytes 9437184 | tf_op jit(solution)/shard_map/pallas_call | solution.py:235
  102.1 8.0 %collective-permute-start.4 = (f16[32,16,1152]{2,1,0:T(8,128)(2,1)S(1)}, f16[32,16,1152]{2,1,0:T(8,128)(2,1)S(1)}, u32[]{:S(2)}, u32[]{:S(2)}) collective-permute-start(f16[32,16,1152]{2,1,0:T(8,128)(2,1)S(1)} %convert_element_type.52), channel_id=1, source_target_pairs={{0,16},{16,0},{1,17},{17,1},{2,18},{18,2},{3,19},{19,3},{4,20},{20... | collective-permute-start | bytes 3538952 | tf_op jit(solution)/shard_map/ppermute | solution.py:300
  110.2 2.5 %collective-permute-done.4 = f16[32,16,1152]{2,1,0:T(8,128)(2,1)S(1)} collective-permute-done((f16[32,16,1152]{2,1,0:T(8,128)(2,1)S(1)}, f16[32,16,1152]{2,1,0:T(8,128)(2,1)S(1)}, u32[]{:S(2)}, u32[]{:S(2)}) %collective-permute-start.4) | collective-permute-done | bytes 1179680 | tf_op jit(solution)/shard_map/ppermute | solution.py:300
  113.0 26.2 %all_to_all.22 = f16[32,16,1152]{2,1,0:T(8,128)(2,1)S(1)} all-to-all(f16[32,16,1152]{2,1,0:T(8,128)(2,1)S(1)} %add_convert_fusion), channel_id=1, replica_groups=mesh['col'=8,'core'=2,'yh'=2,'zq'=4,'zl'=2] {'col','yh','zl'}, dimensions={0} | all-to-all | bytes 2359296 | tf_op jit(solution)/shard_map/all_to_all | solution.py:302
  139.7 0.7 reshape.200
  (40 shorter events, 3.5 us)
Async XLA Ops:
  0.8 0.9 copy-start.1
  1.8 0.9 copy-start.2
  2.7 0.7 copy-start.3
  3.4 0.7 copy-start.4
  5.7 0.7 copy-start.5
  6.3 8.1 %collective-permute-start = (bf16[128,512]{1,0:T(8,128)(2,1)S(1)}, bf16[128,512]{1,0:T(8,128)(2,1)S(1)}, u32[]{:S(2)}, u32[]{:S(2)}) collective-permute-start(bf16[128,512]{1,0:T(8,128)(2,1)S(1)} %get-tuple-element.26), channel_id=1, source_target_pairs={{0,1},{1,0},{8,9},{9,8},{2,3},{3,2},{10,11},{11,10},{4,5},{5,4},{1... | collective-permute-start | bytes 393224 | tf_op jit(solution)/shard_map/ppermute | solution.py:269
  8.8 7.8 %collective-permute-start.1 = (bf16[128,512]{1,0:T(8,128)(2,1)S(1)}, bf16[128,512]{1,0:T(8,128)(2,1)S(1)}, u32[]{:S(2)}, u32[]{:S(2)}) collective-permute-start(bf16[128,512]{1,0:T(8,128)(2,1)S(1)} %get-tuple-element.27), channel_id=1, source_target_pairs={{0,8},{1,9},{8,0},{9,1},{2,10},{3,11},{10,2},{11,3},{4,12},{5,13},... | collective-permute-start | bytes 393224 | tf_op jit(solution)/shard_map/ppermute | solution.py:269
  11.7 6.2 %collective-permute-start.2 = (bf16[128,512]{1,0:T(8,128)(2,1)S(1)}, bf16[128,512]{1,0:T(8,128)(2,1)S(1)}, u32[]{:S(2)}, u32[]{:S(2)}) collective-permute-start(bf16[128,512]{1,0:T(8,128)(2,1)S(1)} %get-tuple-element.28), channel_id=1, source_target_pairs={{0,9},{1,8},{8,1},{9,0},{2,11},{3,10},{10,3},{11,2},{4,13},{5,12},... | collective-permute-start | bytes 393224 | tf_op jit(solution)/shard_map/ppermute | solution.py:269
  14.4 10.2 %copy-start.6 = (bf16[128,512]{1,0:T(8,128)(2,1)}, bf16[128,512]{1,0:T(8,128)(2,1)S(1)}, u32[]{:S(2)}) copy-start(bf16[128,512]{1,0:T(8,128)(2,1)S(1)} %collective-permute-done.refs_1_) | copy-start | bytes 393220
  16.6 8.0 %copy-start.7 = (bf16[128,512]{1,0:T(8,128)(2,1)}, bf16[128,512]{1,0:T(8,128)(2,1)S(1)}, u32[]{:S(2)}) copy-start(bf16[128,512]{1,0:T(8,128)(2,1)S(1)} %collective-permute-done.1.refs_2_) | copy-start | bytes 393220
  17.9 6.7 %copy-start.8 = (bf16[128,512]{1,0:T(8,128)(2,1)}, bf16[128,512]{1,0:T(8,128)(2,1)S(1)}, u32[]{:S(2)}) copy-start(bf16[128,512]{1,0:T(8,128)(2,1)S(1)} %collective-permute-done.2.refs_3_) | copy-start | bytes 393220
  17.9 25.4 %all-to-all-start = ((bf16[32,32,512]{2,1,0:T(8,128)(2,1)}), bf16[32,32,512]{2,1,0:T(8,128)(2,1)S(1)}, u32[]{:S(2)}, u32[]{:S(2)}) async-start(bf16[32,32,512]{2,1,0:T(8,128)(2,1)} %get-tuple-element.29), calls=%async_computation | async-start | bytes 2097152 | tf_op jit(solution)/shard_map/all_to_all | solution.py:283
  43.3 4.1 %collective-permute-start.3 = (bf16[32,32,512]{2,1,0:T(8,128)(2,1)S(1)}, bf16[32,32,512]{2,1,0:T(8,128)(2,1)S(1)}, u32[]{:S(2)}, u32[]{:S(2)}) collective-permute-start(bf16[32,32,512]{2,1,0:T(8,128)(2,1)S(1)} %all-to-all-done.own_ref), channel_id=1, source_target_pairs={{0,16},{16,0},{1,17},{17,1},{2,18},{18,2},{3,19},{19,3},{4,20},{20... | collective-permute-start | bytes 3145736 | tf_op jit(solution)/shard_map/ppermute | solution.py:288
  47.4 1.0 copy-start
  102.1 10.5 %collective-permute-start.4 = (f16[32,16,1152]{2,1,0:T(8,128)(2,1)S(1)}, f16[32,16,1152]{2,1,0:T(8,128)(2,1)S(1)}, u32[]{:S(2)}, u32[]{:S(2)}) collective-permute-start(f16[32,16,1152]{2,1,0:T(8,128)(2,1)S(1)} %convert_element_type.52), channel_id=1, source_target_pairs={{0,16},{16,0},{1,17},{17,1},{2,18},{18,2},{3,19},{19,3},{4,20},{20... | collective-permute-start | bytes 3538952 | tf_op jit(solution)/shard_map/ppermute | solution.py:300

commit v6 on v5

--- a/solution.py
+++ b/solution.py
@@ -43,15 +43,20 @@
 def prepare(spot, inv_sigma, particles, rot_index, shell_map, mine, count):
     _, parts, freq = particles.shape
     rows = parts // 2 + 16 + rot_index.shape[0] // GROUP * 8
-    whole = pl.BlockSpec(memory_space=pltpu.VMEM)
+    args = (particles, rot_index, shell_map[None], mine)
+    outs = [(rows, freq)] * 4 + [(count,) + mine.shape]
+
+    def block(shape):
+        return pl.BlockSpec(shape, lambda i: (0,) * len(shape))
+
     return pl.pallas_call(
         prepare_kernel,
-        in_specs=[SCALAR, SCALAR, whole, whole, whole, whole],
-        out_specs=[whole] * 5,
-        out_shape=[jax.ShapeDtypeStruct((rows, freq), BF16)] * 4
-        + [jax.ShapeDtypeStruct((count,) + mine.shape, BF16)],
-        compiler_params=pltpu.CompilerParams(vmem_limit_bytes=16 * MIB),
-    )(spot, inv_sigma, particles, rot_index, shell_map[None], mine)
+        grid=(1,),
+        in_specs=[SCALAR, SCALAR] + [block(a.shape) for a in args],
+        out_specs=[block(shape) for shape in outs],
+        out_shape=[jax.ShapeDtypeStruct(shape, BF16) for shape in outs],
+        compiler_params=pltpu.CompilerParams(vmem_limit_bytes=60 * MIB),
+    )(spot, inv_sigma, *args)
 
 
 def unrotate_kernel(peers, cos_ref, sin_ref, *refs):

time: 141 us -> 139 us (0.986)
  local copies, waits for them, and re-layouts: 6.68 us -> 3.47 us
    unnamed x18 -> x10, local copies, waits for them, and re-layouts: 4.83 us -> 1.01 us
where the time goes in v6:
time: 139 us
  blocking collectives  64.3 us (46%)
  Pallas kernels  35.2 us (25%)
  starting transfers between devices  21.9 us (16%)
  waiting for transfers between devices  8.56 us (6%)
  other arithmetic  4.95 us (4%)
  local copies, waits for them, and re-layouts  3.47 us (2%)
    all_to_all x1, blocking collectives, shards(): message = lax.all_to_all(message, ('col', 'yh', 'zl'), 0, 0)  26.2 us
    all_to_all x1, blocking collectives, shards(): lax.all_to_all(partial, 'zq', 0, 0).astype(F32)  21.8 us
    pallas_call x1, Pallas kernels, unrotate(): pl.pallas_call(functools.partial(unrotate_kernel, peers), grid=(steps,),...  18.7 us
    all_to_all x1, blocking collectives, shards(): weights = lax.all_to_all(spread, 'zq', 0, 0)  16.4 us
    ppermute x1, starting transfers between devices, shards(): other = lax.ppermute(other.astype(F16), 'core', [(0, 1), (1, 0)])  8.04 us
    pallas_call x1, Pallas kernels, class_sums(): pl.pallas_call(functools.partial(sums_kernel, steps, block, k_dev), grid=...  7.24 us
    pallas_call x1, Pallas kernels, score(): pl.pallas_call(functools.partial(score_kernel, peers, per_step), grid=(st...  6.95 us
    all_to_all x1, starting transfers between devices, shards(): refs = lax.all_to_all(mine, ('col', 'yh', 'zl'), 0, 0)  6.63 us
  transfers between devices with their start and end apart: 6, of which 4 were waited for; matrix products, arithmetic and copies ran while one was open for 2% of the time, Pallas kernels for 13%

profile of v6, /device:TPU:1, one launch (start us, length us, event | category | flops | bytes accessed | tf_op | source)
XLA Modules:
  0.0 138.6 jit_solution(17319229995570260535)
XLA Ops:
  0.0 1.4 copy.12
  1.4 0.6 pad_add_fusion.1.spot_ref.place_ref
  2.0 2.3 %shard_map.64 = (bf16[128,512]{1,0:T(8,128)(2,1)}, bf16[128,512]{1,0:T(8,128)(2,1)}, bf16[128,512]{1,0:T(8,128)(2,1)}, bf16[128,512]{1,0:T(8,128)(2,1)}, bf16[32,32,512]{2,1,0:T(8,128)(2,1)}) custom-call(s32[2]{0:T(128)} %pad_add_fusion.1.spot_ref.place_ref, f32[64]{0:T(128)} %sigma_ref.1, bf16[2,128,512]{2,1,0:T(8,128)(2,1)} %particles_ref.1, ...), custom_call_target="tpu_custom_call" | custom-call | tf_op jit(solution)/shard_map/pallas_call | solution.py:52
  4.4 2.5 %collective-permute-start = (bf16[128,512]{1,0:T(8,128)(2,1)}, bf16[128,512]{1,0:T(8,128)(2,1)S(1)}, u32[]{:S(2)}, u32[]{:S(2)}) collective-permute-start(bf16[128,512]{1,0:T(8,128)(2,1)} %get-tuple-element.26), channel_id=1, source_target_pairs={{0,1},{1,0},{8,9},{9,8},{2,3},{3,2},{10,11},{11,10},{4,5},{5,4},{1... | collective-permute-start | bytes 393224 | tf_op jit(solution)/shard_map/ppermute | solution.py:274
  6.8 2.9 %collective-permute-start.1 = (bf16[128,512]{1,0:T(8,128)(2,1)}, bf16[128,512]{1,0:T(8,128)(2,1)S(1)}, u32[]{:S(2)}, u32[]{:S(2)}) collective-permute-start(bf16[128,512]{1,0:T(8,128)(2,1)} %get-tuple-element.27), channel_id=1, source_target_pairs={{0,8},{1,9},{8,0},{9,1},{2,10},{3,11},{10,2},{11,3},{4,12},{5,13},... | collective-permute-start | bytes 393224 | tf_op jit(solution)/shard_map/ppermute | solution.py:274
  9.7 0.7 fusion.12
  10.5 1.8 %fusion = (f32[32,2048]{1,0:T(8,128)}, f32[32,2048]{1,0:T(8,128)}) fusion(f32[2048]{0:T(1024)S(1)} %get-tuple-element.46, f32[32]{0:T(128)S(1)} %get-tuple-element.48, f32[2048]{0:T(1024)S(1)} %get-tuple-element.45, f32[32]{0:T(128)S(1)} %get-tuple-element.47), kind=kLoop, calls=%fused_computation.6 | loop fusion | flops 262144 | bytes 540928 | tf_op jit(solution)/shard_map/sin | solution.py:285
  12.4 2.6 %collective-permute-done.1.refs_2_ = bf16[128,512]{1,0:T(8,128)(2,1)S(1)} collective-permute-done((bf16[128,512]{1,0:T(8,128)(2,1)}, bf16[128,512]{1,0:T(8,128)(2,1)S(1)}, u32[]{:S(2)}, u32[]{:S(2)}) %collective-permute-start.1) | collective-permute-done | bytes 131104 | tf_op jit(solution)/shard_map/ppermute | solution.py:274
  14.9 1.2 collective-permute-done.2.refs_3_
  16.2 6.6 %all-to-all-start = ((bf16[32,32,512]{2,1,0:T(8,128)(2,1)}), bf16[32,32,512]{2,1,0:T(8,128)(2,1)S(1)}, u32[]{:S(2)}, u32[]{:S(2)}) async-start(bf16[32,32,512]{2,1,0:T(8,128)(2,1)} %get-tuple-element.29), calls=%async_computation | async-start | bytes 2097152 | tf_op jit(solution)/shard_map/all_to_all | solution.py:288
  22.9 18.7 %shard_map.65 = (bf16[2,1152,2048]{2,1,0:T(8,128)(2,1)}, bf16[2,1152,2048]{2,1,0:T(8,128)(2,1)}, f32[6,8,2048]{2,1,0:T(8,128)}) custom-call(f32[32,2048]{1,0:T(8,128)} %get-tuple-element.30.cos_ref, f32[32,2048]{1,0:T(8,128)} %get-tuple-element.31.sin_ref, bf16[128,512]{1,0:T(8,128)(2,1)} %get-tuple-element.32.refs_0_, bf16[128,512]{1,0:T(8,128)(2,1)} %copy-done.2, ...), custom_call_target="tpu_custom_call" | custom-call | flops 6039797760 | bytes 18874368 | tf_op jit(solution)/shard_map/pallas_call | solution.py:113
  41.6 1.9 %collective-permute-start.3 = (bf16[32,32,512]{2,1,0:T(8,128)(2,1)S(1)}, bf16[32,32,512]{2,1,0:T(8,128)(2,1)S(1)}, u32[]{:S(2)}, u32[]{:S(2)}) collective-permute-start(bf16[32,32,512]{2,1,0:T(8,128)(2,1)S(1)} %all-to-all-done.own_ref), channel_id=1, source_target_pairs={{0,16},{16,0},{1,17},{17,1},{2,18},{18,2},{3,19},{19,3},{4,20},{20... | collective-permute-start | bytes 3145736 | tf_op jit(solution)/shard_map/ppermute | solution.py:293
  43.4 2.3 %collective-permute-done.3.other_ref = bf16[32,32,512]{2,1,0:T(8,128)(2,1)S(1)} collective-permute-done((bf16[32,32,512]{2,1,0:T(8,128)(2,1)S(1)}, bf16[32,32,512]{2,1,0:T(8,128)(2,1)S(1)}, u32[]{:S(2)}, u32[]{:S(2)}) %collective-permute-start.3) | collective-permute-done | bytes 1048608 | tf_op jit(solution)/shard_map/ppermute | solution.py:293
  45.7 1.0 copy-done
  46.7 6.9 %shard_map.66 = f32[4,288,256]{2,1,0:T(8,128)S(1)} custom-call(s32[2]{0:T(128)S(1)} %copy-done.1, bf16[2,1152,2048]{2,1,0:T(8,128)(2,1)} %get-tuple-element.37.w0_ref.w1_ref.w2_ref.w3_ref, bf16[2,1152,2048]{2,1,0:T(8,128)(2,1)} %get-tuple-element.37.w0_ref.w1_ref.w2_ref.w3_ref, bf16[2,1152,2048]{2,1,0:T(8,128)(2,1)} %get-tuple-element.37.w0_ref.w1_ref.w2_ref.w3_ref, ...), custom_call_target="tpu_custom_call" | custom-call | tf_op jit(solution)/shard_map/pallas_call | solution.py:182
  53.8 21.8 %all_to_all.20 = f16[4,288,256]{2,1,0:T(8,128)(2,1)S(1)} all-to-all(f16[4,288,256]{2,1,0:T(8,128)(2,1)S(1)} %convert_element_type.49), channel_id=1, replica_groups=mesh['col'=8,'core'=2,'yh'=2,'zq'=4,'zl'=2] {'zq'}, dimensions={0} | all-to-all | bytes 1179648 | tf_op jit(solution)/shard_map/all_to_all | solution.py:297
  76.0 0.2 fusion.2
  76.6 16.4 %all_to_all.21.weights_ref = bf16[4,288,256]{2,1,0:T(8,128)(2,1)S(1)} all-to-all(bf16[4,288,256]{2,1,0:T(8,128)(2,1)S(1)} %broadcast_in_dim.5), channel_id=1, replica_groups=mesh['col'=8,'core'=2,'yh'=2,'zq'=4,'zl'=2] {'zq'}, dimensions={0} | all-to-all | bytes 1179648 | tf_op jit(solution)/shard_map/all_to_all | solution.py:302
  93.0 7.2 %shard_map.67 = (f32[32,16,1152]{2,1,0:T(8,128)S(1)}, f32[32,16,1152]{2,1,0:T(8,128)S(1)}) custom-call(s32[2]{0:T(128)S(1)} %copy-done.1, bf16[4,288,256]{2,1,0:T(8,128)(2,1)S(1)} %all_to_all.21.weights_ref, bf16[2,1152,2048]{2,1,0:T(8,128)(2,1)} %get-tuple-element.40.u0_ref.u1_ref.u2_ref.u3_ref, ...), custom_call_target="tpu_custom_call" | custom-call | flops 2415919104 | bytes 9437184 | tf_op jit(solution)/shard_map/pallas_call | solution.py:240
  100.4 8.0 %collective-permute-start.4 = (f16[32,16,1152]{2,1,0:T(8,128)(2,1)S(1)}, f16[32,16,1152]{2,1,0:T(8,128)(2,1)S(1)}, u32[]{:S(2)}, u32[]{:S(2)}) collective-permute-start(f16[32,16,1152]{2,1,0:T(8,128)(2,1)S(1)} %convert_element_type.52), channel_id=1, source_target_pairs={{0,16},{16,0},{1,17},{17,1},{2,18},{18,2},{3,19},{19,3},{4,20},{20... | collective-permute-start | bytes 3538952 | tf_op jit(solution)/shard_map/ppermute | solution.py:305
  108.4 2.5 %collective-permute-done.4 = f16[32,16,1152]{2,1,0:T(8,128)(2,1)S(1)} collective-permute-done((f16[32,16,1152]{2,1,0:T(8,128)(2,1)S(1)}, f16[32,16,1152]{2,1,0:T(8,128)(2,1)S(1)}, u32[]{:S(2)}, u32[]{:S(2)}) %collective-permute-start.4) | collective-permute-done | bytes 1179680 | tf_op jit(solution)/shard_map/ppermute | solution.py:305
  110.9 0.4 add_convert_fusion
  111.3 26.2 %all_to_all.22 = f16[32,16,1152]{2,1,0:T(8,128)(2,1)S(1)} all-to-all(f16[32,16,1152]{2,1,0:T(8,128)(2,1)S(1)} %add_convert_fusion), channel_id=1, replica_groups=mesh['col'=8,'core'=2,'yh'=2,'zq'=4,'zl'=2] {'col','yh','zl'}, dimensions={0} | all-to-all | bytes 2359296 | tf_op jit(solution)/shard_map/all_to_all | solution.py:307
  137.9 0.7 reshape.200
  (32 shorter events, 1.5 us)
Async XLA Ops:
  4.4 8.0 %collective-permute-start = (bf16[128,512]{1,0:T(8,128)(2,1)}, bf16[128,512]{1,0:T(8,128)(2,1)S(1)}, u32[]{:S(2)}, u32[]{:S(2)}) collective-permute-start(bf16[128,512]{1,0:T(8,128)(2,1)} %get-tuple-element.26), channel_id=1, source_target_pairs={{0,1},{1,0},{8,9},{9,8},{2,3},{3,2},{10,11},{11,10},{4,5},{5,4},{1... | collective-permute-start | bytes 393224 | tf_op jit(solution)/shard_map/ppermute | solution.py:274
  6.8 8.1 %collective-permute-start.1 = (bf16[128,512]{1,0:T(8,128)(2,1)}, bf16[128,512]{1,0:T(8,128)(2,1)S(1)}, u32[]{:S(2)}, u32[]{:S(2)}) collective-permute-start(bf16[128,512]{1,0:T(8,128)(2,1)} %get-tuple-element.27), channel_id=1, source_target_pairs={{0,8},{1,9},{8,0},{9,1},{2,10},{3,11},{10,2},{11,3},{4,12},{5,13},... | collective-permute-start | bytes 393224 | tf_op jit(solution)/shard_map/ppermute | solution.py:274
  9.7 6.4 %collective-permute-start.2 = (bf16[128,512]{1,0:T(8,128)(2,1)}, bf16[128,512]{1,0:T(8,128)(2,1)S(1)}, u32[]{:S(2)}, u32[]{:S(2)}) collective-permute-start(bf16[128,512]{1,0:T(8,128)(2,1)} %get-tuple-element.28), channel_id=1, source_target_pairs={{0,9},{1,8},{8,1},{9,0},{2,11},{3,10},{10,3},{11,2},{4,13},{5,12},... | collective-permute-start | bytes 393224 | tf_op jit(solution)/shard_map/ppermute | solution.py:274
  12.4 10.4 %copy-start.2 = (bf16[128,512]{1,0:T(8,128)(2,1)}, bf16[128,512]{1,0:T(8,128)(2,1)S(1)}, u32[]{:S(2)}) copy-start(bf16[128,512]{1,0:T(8,128)(2,1)S(1)} %collective-permute-done.refs_1_) | copy-start | bytes 393220
  14.9 7.9 %copy-start.3 = (bf16[128,512]{1,0:T(8,128)(2,1)}, bf16[128,512]{1,0:T(8,128)(2,1)S(1)}, u32[]{:S(2)}) copy-start(bf16[128,512]{1,0:T(8,128)(2,1)S(1)} %collective-permute-done.1.refs_2_) | copy-start | bytes 393220
  16.2 6.7 %copy-start.4 = (bf16[128,512]{1,0:T(8,128)(2,1)}, bf16[128,512]{1,0:T(8,128)(2,1)S(1)}, u32[]{:S(2)}) copy-start(bf16[128,512]{1,0:T(8,128)(2,1)S(1)} %collective-permute-done.2.refs_3_) | copy-start | bytes 393220
  16.2 25.4 %all-to-all-start = ((bf16[32,32,512]{2,1,0:T(8,128)(2,1)}), bf16[32,32,512]{2,1,0:T(8,128)(2,1)S(1)}, u32[]{:S(2)}, u32[]{:S(2)}) async-start(bf16[32,32,512]{2,1,0:T(8,128)(2,1)} %get-tuple-element.29), calls=%async_computation | async-start | bytes 2097152 | tf_op jit(solution)/shard_map/all_to_all | solution.py:288
  22.8 22.9 %copy-start.1 = (s32[2]{0:T(128)S(1)}, s32[2]{0:T(128)}, u32[]{:S(2)}) copy-start(s32[2]{0:T(128)} %pad_add_fusion.1.spot_ref.place_ref) | copy-start | bytes 28
  41.6 4.1 %collective-permute-start.3 = (bf16[32,32,512]{2,1,0:T(8,128)(2,1)S(1)}, bf16[32,32,512]{2,1,0:T(8,128)(2,1)S(1)}, u32[]{:S(2)}, u32[]{:S(2)}) collective-permute-start(bf16[32,32,512]{2,1,0:T(8,128)(2,1)S(1)} %all-to-all-done.own_ref), channel_id=1, source_target_pairs={{0,16},{16,0},{1,17},{17,1},{2,18},{18,2},{3,19},{19,3},{4,20},{20... | collective-permute-start | bytes 3145736 | tf_op jit(solution)/shard_map/ppermute | solution.py:293
  45.7 1.0 copy-start
  100.4 10.5 %collective-permute-start.4 = (f16[32,16,1152]{2,1,0:T(8,128)(2,1)S(1)}, f16[32,16,1152]{2,1,0:T(8,128)(2,1)S(1)}, u32[]{:S(2)}, u32[]{:S(2)}) collective-permute-start(f16[32,16,1152]{2,1,0:T(8,128)(2,1)S(1)} %convert_element_type.52), channel_id=1, source_target_pairs={{0,16},{16,0},{1,17},{17,1},{2,18},{18,2},{3,19},{19,3},{4,20},{20... | collective-permute-start | bytes 3538952 | tf_op jit(solution)/shard_map/ppermute | solution.py:305

commit v7 on v6

--- a/solution.py
+++ b/solution.py
@@ -12,9 +12,12 @@
 SCALAR = pl.BlockSpec(memory_space=pltpu.SMEM)
 
 
-def prepare_kernel(spot_ref, sigma_ref, particles_ref, rot_ref, shell_ref, mine_ref, *refs):
+def prepare_kernel(sigma_ref, particles_ref, rot_ref, shell_ref, mine_ref, *refs):
     msgs, spread_ref = refs[:-1], refs[-1]
     few, freq = particles_ref.shape[1] // 4, rot_ref.shape[1]
+    place = lax.axis_index("yh") * 2 + lax.axis_index("zl")
+    zqs = lax.axis_size("zq")
+    base = (lax.axis_index("yh") * 2 * zqs + lax.axis_index("zq") * 2 + lax.axis_index("zl")) * freq
     shell = shell_ref[...]
     gain = jnp.zeros((1, freq), F32)
     for s in range(sigma_ref.shape[0]):
@@ -23,7 +26,7 @@
     middle = (gain - top).astype(BF16).astype(F32)
     low = gain - top - middle
     gains = jnp.concatenate([top, middle, low, jnp.zeros((13, freq), F32)]).astype(BF16)
-    local = rot_ref[...] - spot_ref[1]
+    local = rot_ref[...] - base
     code = jnp.where(local < 256, local + 1, 255 - local).astype(F32)
     gap = jnp.zeros((8 - GROUP, freq), F32)
     rows = []
@@ -31,20 +34,22 @@
         rows += [code[g * GROUP : (g + 1) * GROUP], gap]
     code = jnp.concatenate(rows).astype(BF16)
     for b, msg in enumerate(msgs):
-        start = pl.multiple_of((spot_ref[0] ^ b) * few, few)
+        start = pl.multiple_of((place ^ b) * few, few)
         for c in range(2):
             msg[c * few : (c + 1) * few, :] = particles_ref[c, pl.ds(start, few), :]
         msg[2 * few : 2 * few + 16, :] = gains
         msg[2 * few + 16 :, :] = code
+    mine = mine_ref[...].astype(F32)
+    mine = jnp.concatenate([mine[:, c] for c in range(2)]).astype(BF16)
     for j in range(spread_ref.shape[0]):
-        spread_ref[j] = mine_ref[...]
-
-
-def prepare(spot, inv_sigma, particles, rot_index, shell_map, mine, count):
+        spread_ref[j] = mine
+
+
+def prepare(inv_sigma, particles, rot_index, shell_map, references, count):
     _, parts, freq = particles.shape
     rows = parts // 2 + 16 + rot_index.shape[0] // GROUP * 8
-    args = (particles, rot_index, shell_map[None], mine)
-    outs = [(rows, freq)] * 4 + [(count,) + mine.shape]
+    args = (particles, rot_index, shell_map[None], references)
+    outs = [(rows, freq)] * 4 + [(count, references.shape[0] * 2, freq)]
 
     def block(shape):
         return pl.BlockSpec(shape, lambda i: (0,) * len(shape))
@@ -52,11 +57,11 @@
     return pl.pallas_call(
         prepare_kernel,
         grid=(1,),
-        in_specs=[SCALAR, SCALAR] + [block(a.shape) for a in args],
+        in_specs=[SCALAR] + [block(a.shape) for a in args],
         out_specs=[block(shape) for shape in outs],
         out_shape=[jax.ShapeDtypeStruct(shape, BF16) for shape in outs],
         compiler_params=pltpu.CompilerParams(vmem_limit_bytes=60 * MIB),
-    )(spot, inv_sigma, *args)
+    )(inv_sigma, *args)
 
 
 def unrotate_kernel(peers, cos_ref, sin_ref, *refs):
@@ -266,10 +271,7 @@
     half = 2 * zqs
     place = yh * 2 + zl
 
-    base = (yh * half + zq * 2 + zl) * freq
-    spot = jnp.stack([place, base]).astype(jnp.int32)
-    mine = references.transpose(1, 0, 2).reshape(2 * k_dev, freq)
-    *msgs, mine = prepare(spot, inv_sigma, particles, rot_index, shell_map, mine, 4 * cols)
+    *msgs, mine = prepare(inv_sigma, particles, rot_index, shell_map, references, 4 * cols)
     for b in range(1, 4):
         msgs[b] = lax.ppermute(msgs[b], ("yh", "zl"), [(i, i ^ b) for i in range(4)])
 
@@ -292,6 +294,7 @@
     refs, weighted = lax.optimization_barrier((refs, weighted))
     refs_other = lax.ppermute(refs, "core", [(0, 1), (1, 0)])
 
+    spot = jnp.reshape(place, (1,)).astype(jnp.int32)
     partial = score(spot, weighted, gain_unrot, refs, refs_other, zqs, 3).astype(F16)
     own = few // zqs
     scores = jnp.sum(lax.all_to_all(partial, "zq", 0, 0).astype(F32), axis=0).reshape(rots, own, classes)

time: 139 us -> 137 us (0.986)
  transfers between devices with their start and end apart: 6 -> 6, of which waited for: 4 -> 4; matrix products, arithmetic and copies ran while one was open for 2% -> 2% of each run, Pallas kernels for 13% -> 14%
where the time goes in v7:
time: 137 us
  blocking collectives  64.4 us (47%)
  Pallas kernels  35.1 us (26%)
  starting transfers between devices  21.9 us (16%)
  waiting for transfers between devices  8.56 us (6%)
  other arithmetic  4.31 us (3%)
  local copies, waits for them, and re-layouts  2.09 us (2%)
    all_to_all x1, blocking collectives, shards(): message = lax.all_to_all(message, ('col', 'yh', 'zl'), 0, 0)  26.2 us
    all_to_all x1, blocking collectives, shards(): lax.all_to_all(partial, 'zq', 0, 0).astype(F32)  21.8 us
    pallas_call x1, Pallas kernels, unrotate(): pl.pallas_call(functools.partial(unrotate_kernel, peers), grid=(steps,),...  18.7 us
    all_to_all x1, blocking collectives, shards(): weights = lax.all_to_all(spread, 'zq', 0, 0)  16.4 us
    ppermute x1, starting transfers between devices, shards(): other = lax.ppermute(other.astype(F16), 'core', [(0, 1), (1, 0)])  8.02 us
    pallas_call x1, Pallas kernels, class_sums(): pl.pallas_call(functools.partial(sums_kernel, steps, block, k_dev), grid=...  7.23 us
    pallas_call x1, Pallas kernels, score(): pl.pallas_call(functools.partial(score_kernel, peers, per_step), grid=(st...  6.88 us
    all_to_all x1, starting transfers between devices, shards(): refs = lax.all_to_all(mine, ('col', 'yh', 'zl'), 0, 0)  6.63 us
  transfers between devices with their start and end apart: 6, of which 4 were waited for; matrix products, arithmetic and copies ran while one was open for 2% of the time, Pallas kernels for 14%

profile of v7, /device:TPU:1, one launch (start us, length us, event | category | flops | bytes accessed | tf_op | source)
XLA Modules:
  0.0 136.5 jit_solution(13876585259095789315)
XLA Ops:
  0.0 2.3 %shard_map.64 = (bf16[128,512]{1,0:T(8,128)(2,1)}, bf16[128,512]{1,0:T(8,128)(2,1)}, bf16[128,512]{1,0:T(8,128)(2,1)}, bf16[128,512]{1,0:T(8,128)(2,1)}, bf16[32,32,512]{2,1,0:T(8,128)(2,1)}) custom-call(f32[64]{0:T(128)} %sigma_ref.1, bf16[2,128,512]{2,1,0:T(8,128)(2,1)} %particles_ref.1, s32[36,512]{1,0:T(8,128)} %rot_ref.1, s32[1,512]{1,0:T(1,128)} %bitcast.2, ...), custom_call_target="tpu_custom_call" | custom-call | tf_op jit(solution)/shard_map/pallas_call | solution.py:57
  2.3 2.5 %collective-permute-start = (bf16[128,512]{1,0:T(8,128)(2,1)}, bf16[128,512]{1,0:T(8,128)(2,1)S(1)}, u32[]{:S(2)}, u32[]{:S(2)}) collective-permute-start(bf16[128,512]{1,0:T(8,128)(2,1)} %get-tuple-element.26), channel_id=1, source_target_pairs={{0,1},{1,0},{8,9},{9,8},{2,3},{3,2},{10,11},{11,10},{4,5},{5,4},{1... | collective-permute-start | bytes 393224 | tf_op jit(solution)/shard_map/ppermute | solution.py:276
  4.8 2.9 %collective-permute-start.1 = (bf16[128,512]{1,0:T(8,128)(2,1)}, bf16[128,512]{1,0:T(8,128)(2,1)S(1)}, u32[]{:S(2)}, u32[]{:S(2)}) collective-permute-start(bf16[128,512]{1,0:T(8,128)(2,1)} %get-tuple-element.27), channel_id=1, source_target_pairs={{0,8},{1,9},{8,0},{9,1},{2,10},{3,11},{10,2},{11,3},{4,12},{5,13},... | collective-permute-start | bytes 393224 | tf_op jit(solution)/shard_map/ppermute | solution.py:276
  7.7 0.7 fusion.12
  8.5 1.8 %fusion = (f32[32,2048]{1,0:T(8,128)}, f32[32,2048]{1,0:T(8,128)}) fusion(f32[2048]{0:T(1024)S(1)} %get-tuple-element.46, f32[32]{0:T(128)S(1)} %get-tuple-element.48, f32[2048]{0:T(1024)S(1)} %get-tuple-element.45, f32[32]{0:T(128)S(1)} %get-tuple-element.47), kind=kLoop, calls=%fused_computation.6 | loop fusion | flops 262144 | bytes 540928 | tf_op jit(solution)/shard_map/sin | solution.py:287
  10.3 2.6 %collective-permute-done.1.refs_2_ = bf16[128,512]{1,0:T(8,128)(2,1)S(1)} collective-permute-done((bf16[128,512]{1,0:T(8,128)(2,1)}, bf16[128,512]{1,0:T(8,128)(2,1)S(1)}, u32[]{:S(2)}, u32[]{:S(2)}) %collective-permute-start.1) | collective-permute-done | bytes 131104 | tf_op jit(solution)/shard_map/ppermute | solution.py:276
  12.9 1.2 collective-permute-done.2.refs_3_
  14.1 6.6 %all-to-all-start = ((bf16[32,32,512]{2,1,0:T(8,128)(2,1)}), bf16[32,32,512]{2,1,0:T(8,128)(2,1)S(1)}, u32[]{:S(2)}, u32[]{:S(2)}) async-start(bf16[32,32,512]{2,1,0:T(8,128)(2,1)} %get-tuple-element.29), calls=%async_computation | async-start | bytes 2097152 | tf_op jit(solution)/shard_map/all_to_all | solution.py:290
  20.8 18.7 %shard_map.65 = (bf16[2,1152,2048]{2,1,0:T(8,128)(2,1)}, bf16[2,1152,2048]{2,1,0:T(8,128)(2,1)}, f32[6,8,2048]{2,1,0:T(8,128)}) custom-call(f32[32,2048]{1,0:T(8,128)} %get-tuple-element.30.cos_ref, f32[32,2048]{1,0:T(8,128)} %get-tuple-element.31.sin_ref, bf16[128,512]{1,0:T(8,128)(2,1)} %get-tuple-element.32.refs_0_, bf16[128,512]{1,0:T(8,128)(2,1)} %copy-done.1, ...), custom_call_target="tpu_custom_call" | custom-call | flops 6039797760 | bytes 18874368 | tf_op jit(solution)/shard_map/pallas_call | solution.py:118
  39.5 1.9 %collective-permute-start.3 = (bf16[32,32,512]{2,1,0:T(8,128)(2,1)S(1)}, bf16[32,32,512]{2,1,0:T(8,128)(2,1)S(1)}, u32[]{:S(2)}, u32[]{:S(2)}) collective-permute-start(bf16[32,32,512]{2,1,0:T(8,128)(2,1)S(1)} %all-to-all-done.own_ref), channel_id=1, source_target_pairs={{0,16},{16,0},{1,17},{17,1},{2,18},{18,2},{3,19},{19,3},{4,20},{20... | collective-permute-start | bytes 3145736 | tf_op jit(solution)/shard_map/ppermute | solution.py:295
  41.4 2.3 %collective-permute-done.3.other_ref = bf16[32,32,512]{2,1,0:T(8,128)(2,1)S(1)} collective-permute-done((bf16[32,32,512]{2,1,0:T(8,128)(2,1)S(1)}, bf16[32,32,512]{2,1,0:T(8,128)(2,1)S(1)}, u32[]{:S(2)}, u32[]{:S(2)}) %collective-permute-start.3) | collective-permute-done | bytes 1048608 | tf_op jit(solution)/shard_map/ppermute | solution.py:295
  43.7 1.0 copy-done
  44.7 6.9 %shard_map.66 = f32[4,288,256]{2,1,0:T(8,128)S(1)} custom-call(s32[1]{0:T(128)} %bitcast.place_ref, bf16[2,1152,2048]{2,1,0:T(8,128)(2,1)} %get-tuple-element.37.w0_ref.w1_ref.w2_ref.w3_ref, bf16[2,1152,2048]{2,1,0:T(8,128)(2,1)} %get-tuple-element.37.w0_ref.w1_ref.w2_ref.w3_ref, bf16[2,1152,2048]{2,1,0:T(8,128)(2,1)} %get-tuple-element.37.w0_ref.w1_ref.w2_ref.w3_ref, ...), custom_call_target="tpu_custom_call" | custom-call | tf_op jit(solution)/shard_map/pallas_call | solution.py:187
  51.6 21.8 %all_to_all.20 = f16[4,288,256]{2,1,0:T(8,128)(2,1)S(1)} all-to-all(f16[4,288,256]{2,1,0:T(8,128)(2,1)S(1)} %convert_element_type.49), channel_id=1, replica_groups=mesh['col'=8,'core'=2,'yh'=2,'zq'=4,'zl'=2] {'zq'}, dimensions={0} | all-to-all | bytes 1179648 | tf_op jit(solution)/shard_map/all_to_all | solution.py:300
  73.9 0.2 fusion.2
  74.5 16.4 %all_to_all.21.weights_ref = bf16[4,288,256]{2,1,0:T(8,128)(2,1)S(1)} all-to-all(bf16[4,288,256]{2,1,0:T(8,128)(2,1)S(1)} %broadcast_in_dim.5), channel_id=1, replica_groups=mesh['col'=8,'core'=2,'yh'=2,'zq'=4,'zl'=2] {'zq'}, dimensions={0} | all-to-all | bytes 1179648 | tf_op jit(solution)/shard_map/all_to_all | solution.py:305
  90.9 7.2 %shard_map.67 = (f32[32,16,1152]{2,1,0:T(8,128)S(1)}, f32[32,16,1152]{2,1,0:T(8,128)S(1)}) custom-call(s32[1]{0:T(128)} %bitcast.place_ref, bf16[4,288,256]{2,1,0:T(8,128)(2,1)S(1)} %all_to_all.21.weights_ref, bf16[2,1152,2048]{2,1,0:T(8,128)(2,1)} %get-tuple-element.40.u0_ref.u1_ref.u2_ref.u3_ref, ...), custom_call_target="tpu_custom_call" | custom-call | flops 2415919104 | bytes 9437184 | tf_op jit(solution)/shard_map/pallas_call | solution.py:245
  98.3 8.0 %collective-permute-start.4 = (f16[32,16,1152]{2,1,0:T(8,128)(2,1)S(1)}, f16[32,16,1152]{2,1,0:T(8,128)(2,1)S(1)}, u32[]{:S(2)}, u32[]{:S(2)}) collective-permute-start(f16[32,16,1152]{2,1,0:T(8,128)(2,1)S(1)} %convert_element_type.52), channel_id=1, source_target_pairs={{0,16},{16,0},{1,17},{17,1},{2,18},{18,2},{3,19},{19,3},{4,20},{20... | collective-permute-start | bytes 3538952 | tf_op jit(solution)/shard_map/ppermute | solution.py:308
  106.3 2.5 %collective-permute-done.4 = f16[32,16,1152]{2,1,0:T(8,128)(2,1)S(1)} collective-permute-done((f16[32,16,1152]{2,1,0:T(8,128)(2,1)S(1)}, f16[32,16,1152]{2,1,0:T(8,128)(2,1)S(1)}, u32[]{:S(2)}, u32[]{:S(2)}) %collective-permute-start.4) | collective-permute-done | bytes 1179680 | tf_op jit(solution)/shard_map/ppermute | solution.py:308
  108.8 0.4 add_convert_fusion
  109.2 26.2 %all_to_all.22 = f16[32,16,1152]{2,1,0:T(8,128)(2,1)S(1)} all-to-all(f16[32,16,1152]{2,1,0:T(8,128)(2,1)S(1)} %add_convert_fusion), channel_id=1, replica_groups=mesh['col'=8,'core'=2,'yh'=2,'zq'=4,'zl'=2] {'col','yh','zl'}, dimensions={0} | all-to-all | bytes 2359296 | tf_op jit(solution)/shard_map/all_to_all | solution.py:310
  135.4 0.2 convert_reduce_fusion
  135.5 0.2 fusion.8
  135.8 0.7 reshape.200
  (28 shorter events, 1.2 us)
Async XLA Ops:
  2.3 8.0 %collective-permute-start = (bf16[128,512]{1,0:T(8,128)(2,1)}, bf16[128,512]{1,0:T(8,128)(2,1)S(1)}, u32[]{:S(2)}, u32[]{:S(2)}) collective-permute-start(bf16[128,512]{1,0:T(8,128)(2,1)} %get-tuple-element.26), channel_id=1, source_target_pairs={{0,1},{1,0},{8,9},{9,8},{2,3},{3,2},{10,11},{11,10},{4,5},{5,4},{1... | collective-permute-start | bytes 393224 | tf_op jit(solution)/shard_map/ppermute | solution.py:276
  4.8 8.1 %collective-permute-start.1 = (bf16[128,512]{1,0:T(8,128)(2,1)}, bf16[128,512]{1,0:T(8,128)(2,1)S(1)}, u32[]{:S(2)}, u32[]{:S(2)}) collective-permute-start(bf16[128,512]{1,0:T(8,128)(2,1)} %get-tuple-element.27), channel_id=1, source_target_pairs={{0,8},{1,9},{8,0},{9,1},{2,10},{3,11},{10,2},{11,3},{4,12},{5,13},... | collective-permute-start | bytes 393224 | tf_op jit(solution)/shard_map/ppermute | solution.py:276
  7.7 6.4 %collective-permute-start.2 = (bf16[128,512]{1,0:T(8,128)(2,1)}, bf16[128,512]{1,0:T(8,128)(2,1)S(1)}, u32[]{:S(2)}, u32[]{:S(2)}) collective-permute-start(bf16[128,512]{1,0:T(8,128)(2,1)} %get-tuple-element.28), channel_id=1, source_target_pairs={{0,9},{1,8},{8,1},{9,0},{2,11},{3,10},{10,3},{11,2},{4,13},{5,12},... | collective-permute-start | bytes 393224 | tf_op jit(solution)/shard_map/ppermute | solution.py:276
  10.3 10.4 %copy-start.1 = (bf16[128,512]{1,0:T(8,128)(2,1)}, bf16[128,512]{1,0:T(8,128)(2,1)S(1)}, u32[]{:S(2)}) copy-start(bf16[128,512]{1,0:T(8,128)(2,1)S(1)} %collective-permute-done.refs_1_) | copy-start | bytes 393220
  12.9 7.9 %copy-start.2 = (bf16[128,512]{1,0:T(8,128)(2,1)}, bf16[128,512]{1,0:T(8,128)(2,1)S(1)}, u32[]{:S(2)}) copy-start(bf16[128,512]{1,0:T(8,128)(2,1)S(1)} %collective-permute-done.1.refs_2_) | copy-start | bytes 393220
  14.1 6.7 %copy-start.3 = (bf16[128,512]{1,0:T(8,128)(2,1)}, bf16[128,512]{1,0:T(8,128)(2,1)S(1)}, u32[]{:S(2)}) copy-start(bf16[128,512]{1,0:T(8,128)(2,1)S(1)} %collective-permute-done.2.refs_3_) | copy-start | bytes 393220
  14.1 25.4 %all-to-all-start = ((bf16[32,32,512]{2,1,0:T(8,128)(2,1)}), bf16[32,32,512]{2,1,0:T(8,128)(2,1)S(1)}, u32[]{:S(2)}, u32[]{:S(2)}) async-start(bf16[32,32,512]{2,1,0:T(8,128)(2,1)} %get-tuple-element.29), calls=%async_computation | async-start | bytes 2097152 | tf_op jit(solution)/shard_map/all_to_all | solution.py:290
  39.5 4.1 %collective-permute-start.3 = (bf16[32,32,512]{2,1,0:T(8,128)(2,1)S(1)}, bf16[32,32,512]{2,1,0:T(8,128)(2,1)S(1)}, u32[]{:S(2)}, u32[]{:S(2)}) collective-permute-start(bf16[32,32,512]{2,1,0:T(8,128)(2,1)S(1)} %all-to-all-done.own_ref), channel_id=1, source_target_pairs={{0,16},{16,0},{1,17},{17,1},{2,18},{18,2},{3,19},{19,3},{4,20},{20... | collective-permute-start | bytes 3145736 | tf_op jit(solution)/shard_map/ppermute | solution.py:295
  43.7 1.0 copy-start
  98.3 10.5 %collective-permute-start.4 = (f16[32,16,1152]{2,1,0:T(8,128)(2,1)S(1)}, f16[32,16,1152]{2,1,0:T(8,128)(2,1)S(1)}, u32[]{:S(2)}, u32[]{:S(2)}) collective-permute-start(f16[32,16,1152]{2,1,0:T(8,128)(2,1)S(1)} %convert_element_type.52), channel_id=1, source_target_pairs={{0,16},{16,0},{1,17},{17,1},{2,18},{18,2},{3,19},{19,3},{4,20},{20... | collective-permute-start | bytes 3538952 | tf_op jit(solution)/shard_map/ppermute | solution.py:308

commit v8 on v7

--- a/solution.py
+++ b/solution.py
@@ -205,7 +205,7 @@
     step = pl.program_id(0)
     peers, mine, classes = weights_ref.shape
     picked = [weights_ref[p, q * 16 : (q + 1) * 16, :] for q in range(mine // 16) for p in range(peers)]
-    turned = jnp.concatenate(picked).astype(F32).T.astype(BF16)
+    turned = jnp.concatenate(picked).T
     count = jnp.dot(turned, jnp.ones((turned.shape[1], 128), BF16), preferred_element_type=F32)
 
     @pl.when(step == 0)

time: 137 us -> 137 us (level)
  no operation moved by 1% of the time
where the time goes in v8:
time: 137 us; the launch traced here: 136 us
  blocking collectives  64.4 us (47%)
  Pallas kernels  35.1 us (26%)
  starting transfers between devices  21.9 us (16%)
  waiting for transfers between devices  8.56 us (6%)
  other arithmetic  4.31 us (3%)
  local copies, waits for them, and re-layouts  2.09 us (2%)
    all_to_all x1, blocking collectives, shards(): message = lax.all_to_all(message, ('col', 'yh', 'zl'), 0, 0)  26.2 us
    all_to_all x1, blocking collectives, shards(): lax.all_to_all(partial, 'zq', 0, 0).astype(F32)  21.8 us
    pallas_call x1, Pallas kernels, unrotate(): pl.pallas_call(functools.partial(unrotate_kernel, peers), grid=(steps,),...  18.7 us
    all_to_all x1, blocking collectives, shards(): weights = lax.all_to_all(spread, 'zq', 0, 0)  16.4 us
    ppermute x1, starting transfers between devices, shards(): other = lax.ppermute(other.astype(F16), 'core', [(0, 1), (1, 0)])  8.01 us
    pallas_call x1, Pallas kernels, class_sums(): pl.pallas_call(functools.partial(sums_kernel, steps, block, k_dev), grid=...  7.19 us
    pallas_call x1, Pallas kernels, score(): pl.pallas_call(functools.partial(score_kernel, peers, per_step), grid=(st...  6.88 us
    all_to_all x1, starting transfers between devices, shards(): refs = lax.all_to_all(mine, ('col', 'yh', 'zl'), 0, 0)  6.63 us
  transfers between devices with their start and end apart: 6, of which 4 were waited for; matrix products, arithmetic and copies ran while one was open for 2% of the time, Pallas kernels for 14%

profile of v8, /device:TPU:1, one launch (start us, length us, event | category | flops | bytes accessed | tf_op | source)
XLA Modules:
  0.0 136.5 jit_solution(13177955150500196705)
XLA Ops:
  0.0 2.3 %shard_map.64 = (bf16[128,512]{1,0:T(8,128)(2,1)}, bf16[128,512]{1,0:T(8,128)(2,1)}, bf16[128,512]{1,0:T(8,128)(2,1)}, bf16[128,512]{1,0:T(8,128)(2,1)}, bf16[32,32,512]{2,1,0:T(8,128)(2,1)}) custom-call(f32[64]{0:T(128)} %sigma_ref.1, bf16[2,128,512]{2,1,0:T(8,128)(2,1)} %particles_ref.1, s32[36,512]{1,0:T(8,128)} %rot_ref.1, s32[1,512]{1,0:T(1,128)} %bitcast.2, ...), custom_call_target="tpu_custom_call" | custom-call | tf_op jit(solution)/shard_map/pallas_call | solution.py:57
  2.3 2.5 %collective-permute-start = (bf16[128,512]{1,0:T(8,128)(2,1)}, bf16[128,512]{1,0:T(8,128)(2,1)S(1)}, u32[]{:S(2)}, u32[]{:S(2)}) collective-permute-start(bf16[128,512]{1,0:T(8,128)(2,1)} %get-tuple-element.26), channel_id=1, source_target_pairs={{0,1},{1,0},{8,9},{9,8},{2,3},{3,2},{10,11},{11,10},{4,5},{5,4},{1... | collective-permute-start | bytes 393224 | tf_op jit(solution)/shard_map/ppermute | solution.py:276
  4.8 2.9 %collective-permute-start.1 = (bf16[128,512]{1,0:T(8,128)(2,1)}, bf16[128,512]{1,0:T(8,128)(2,1)S(1)}, u32[]{:S(2)}, u32[]{:S(2)}) collective-permute-start(bf16[128,512]{1,0:T(8,128)(2,1)} %get-tuple-element.27), channel_id=1, source_target_pairs={{0,8},{1,9},{8,0},{9,1},{2,10},{3,11},{10,2},{11,3},{4,12},{5,13},... | collective-permute-start | bytes 393224 | tf_op jit(solution)/shard_map/ppermute | solution.py:276
  7.7 0.7 fusion.12
  8.5 1.8 %fusion = (f32[32,2048]{1,0:T(8,128)}, f32[32,2048]{1,0:T(8,128)}) fusion(f32[2048]{0:T(1024)S(1)} %get-tuple-element.46, f32[32]{0:T(128)S(1)} %get-tuple-element.48, f32[2048]{0:T(1024)S(1)} %get-tuple-element.45, f32[32]{0:T(128)S(1)} %get-tuple-element.47), kind=kLoop, calls=%fused_computation.6 | loop fusion | flops 262144 | bytes 540928 | tf_op jit(solution)/shard_map/sin | solution.py:287
  10.3 2.6 %collective-permute-done.1.refs_2_ = bf16[128,512]{1,0:T(8,128)(2,1)S(1)} collective-permute-done((bf16[128,512]{1,0:T(8,128)(2,1)}, bf16[128,512]{1,0:T(8,128)(2,1)S(1)}, u32[]{:S(2)}, u32[]{:S(2)}) %collective-permute-start.1) | collective-permute-done | bytes 131104 | tf_op jit(solution)/shard_map/ppermute | solution.py:276
  12.9 1.2 collective-permute-done.2.refs_3_
  14.1 6.6 %all-to-all-start = ((bf16[32,32,512]{2,1,0:T(8,128)(2,1)}), bf16[32,32,512]{2,1,0:T(8,128)(2,1)S(1)}, u32[]{:S(2)}, u32[]{:S(2)}) async-start(bf16[32,32,512]{2,1,0:T(8,128)(2,1)} %get-tuple-element.29), calls=%async_computation | async-start | bytes 2097152 | tf_op jit(solution)/shard_map/all_to_all | solution.py:290
  20.8 18.7 %shard_map.65 = (bf16[2,1152,2048]{2,1,0:T(8,128)(2,1)}, bf16[2,1152,2048]{2,1,0:T(8,128)(2,1)}, f32[6,8,2048]{2,1,0:T(8,128)}) custom-call(f32[32,2048]{1,0:T(8,128)} %get-tuple-element.30.cos_ref, f32[32,2048]{1,0:T(8,128)} %get-tuple-element.31.sin_ref, bf16[128,512]{1,0:T(8,128)(2,1)} %get-tuple-element.32.refs_0_, bf16[128,512]{1,0:T(8,128)(2,1)} %copy-done.1, ...), custom_call_target="tpu_custom_call" | custom-call | flops 6039797760 | bytes 18874368 | tf_op jit(solution)/shard_map/pallas_call | solution.py:118
  39.5 1.9 %collective-permute-start.3 = (bf16[32,32,512]{2,1,0:T(8,128)(2,1)S(1)}, bf16[32,32,512]{2,1,0:T(8,128)(2,1)S(1)}, u32[]{:S(2)}, u32[]{:S(2)}) collective-permute-start(bf16[32,32,512]{2,1,0:T(8,128)(2,1)S(1)} %all-to-all-done.own_ref), channel_id=1, source_target_pairs={{0,16},{16,0},{1,17},{17,1},{2,18},{18,2},{3,19},{19,3},{4,20},{20... | collective-permute-start | bytes 3145736 | tf_op jit(solution)/shard_map/ppermute | solution.py:295
  41.4 2.3 %collective-permute-done.3.other_ref = bf16[32,32,512]{2,1,0:T(8,128)(2,1)S(1)} collective-permute-done((bf16[32,32,512]{2,1,0:T(8,128)(2,1)S(1)}, bf16[32,32,512]{2,1,0:T(8,128)(2,1)S(1)}, u32[]{:S(2)}, u32[]{:S(2)}) %collective-permute-start.3) | collective-permute-done | bytes 1048608 | tf_op jit(solution)/shard_map/ppermute | solution.py:295
  43.7 1.0 copy-done
  44.7 6.9 %shard_map.66 = f32[4,288,256]{2,1,0:T(8,128)S(1)} custom-call(s32[1]{0:T(128)} %bitcast.place_ref, bf16[2,1152,2048]{2,1,0:T(8,128)(2,1)} %get-tuple-element.37.w0_ref.w1_ref.w2_ref.w3_ref, bf16[2,1152,2048]{2,1,0:T(8,128)(2,1)} %get-tuple-element.37.w0_ref.w1_ref.w2_ref.w3_ref, bf16[2,1152,2048]{2,1,0:T(8,128)(2,1)} %get-tuple-element.37.w0_ref.w1_ref.w2_ref.w3_ref, ...), custom_call_target="tpu_custom_call" | custom-call | tf_op jit(solution)/shard_map/pallas_call | solution.py:187
  51.6 21.8 %all_to_all.20 = f16[4,288,256]{2,1,0:T(8,128)(2,1)S(1)} all-to-all(f16[4,288,256]{2,1,0:T(8,128)(2,1)S(1)} %convert_element_type.49), channel_id=1, replica_groups=mesh['col'=8,'core'=2,'yh'=2,'zq'=4,'zl'=2] {'zq'}, dimensions={0} | all-to-all | bytes 1179648 | tf_op jit(solution)/shard_map/all_to_all | solution.py:300
  73.9 0.2 fusion.2
  74.5 16.4 %all_to_all.21.weights_ref = bf16[4,288,256]{2,1,0:T(8,128)(2,1)S(1)} all-to-all(bf16[4,288,256]{2,1,0:T(8,128)(2,1)S(1)} %broadcast_in_dim.5), channel_id=1, replica_groups=mesh['col'=8,'core'=2,'yh'=2,'zq'=4,'zl'=2] {'zq'}, dimensions={0} | all-to-all | bytes 1179648 | tf_op jit(solution)/shard_map/all_to_all | solution.py:305
  90.9 7.2 %shard_map.67 = (f32[32,16,1152]{2,1,0:T(8,128)S(1)}, f32[32,16,1152]{2,1,0:T(8,128)S(1)}) custom-call(s32[1]{0:T(128)} %bitcast.place_ref, bf16[4,288,256]{2,1,0:T(8,128)(2,1)S(1)} %all_to_all.21.weights_ref, bf16[2,1152,2048]{2,1,0:T(8,128)(2,1)} %get-tuple-element.40.u0_ref.u1_ref.u2_ref.u3_ref, ...), custom_call_target="tpu_custom_call" | custom-call | flops 2415919104 | bytes 9437184 | tf_op jit(solution)/shard_map/pallas_call | solution.py:245
  98.2 8.0 %collective-permute-start.4 = (f16[32,16,1152]{2,1,0:T(8,128)(2,1)S(1)}, f16[32,16,1152]{2,1,0:T(8,128)(2,1)S(1)}, u32[]{:S(2)}, u32[]{:S(2)}) collective-permute-start(f16[32,16,1152]{2,1,0:T(8,128)(2,1)S(1)} %convert_element_type.52), channel_id=1, source_target_pairs={{0,16},{16,0},{1,17},{17,1},{2,18},{18,2},{3,19},{19,3},{4,20},{20... | collective-permute-start | bytes 3538952 | tf_op jit(solution)/shard_map/ppermute | solution.py:308
  106.3 2.5 %collective-permute-done.4 = f16[32,16,1152]{2,1,0:T(8,128)(2,1)S(1)} collective-permute-done((f16[32,16,1152]{2,1,0:T(8,128)(2,1)S(1)}, f16[32,16,1152]{2,1,0:T(8,128)(2,1)S(1)}, u32[]{:S(2)}, u32[]{:S(2)}) %collective-permute-start.4) | collective-permute-done | bytes 1179680 | tf_op jit(solution)/shard_map/ppermute | solution.py:308
  108.7 0.4 add_convert_fusion
  109.1 26.2 %all_to_all.22 = f16[32,16,1152]{2,1,0:T(8,128)(2,1)S(1)} all-to-all(f16[32,16,1152]{2,1,0:T(8,128)(2,1)S(1)} %add_convert_fusion), channel_id=1, replica_groups=mesh['col'=8,'core'=2,'yh'=2,'zq'=4,'zl'=2] {'col','yh','zl'}, dimensions={0} | all-to-all | bytes 2359296 | tf_op jit(solution)/shard_map/all_to_all | solution.py:310
  135.3 0.2 convert_reduce_fusion
  135.5 0.2 fusion.8
  135.8 0.7 reshape.200
  (28 shorter events, 1.2 us)
Async XLA Ops:
  2.3 8.0 %collective-permute-start = (bf16[128,512]{1,0:T(8,128)(2,1)}, bf16[128,512]{1,0:T(8,128)(2,1)S(1)}, u32[]{:S(2)}, u32[]{:S(2)}) collective-permute-start(bf16[128,512]{1,0:T(8,128)(2,1)} %get-tuple-element.26), channel_id=1, source_target_pairs={{0,1},{1,0},{8,9},{9,8},{2,3},{3,2},{10,11},{11,10},{4,5},{5,4},{1... | collective-permute-start | bytes 393224 | tf_op jit(solution)/shard_map/ppermute | solution.py:276
  4.8 8.1 %collective-permute-start.1 = (bf16[128,512]{1,0:T(8,128)(2,1)}, bf16[128,512]{1,0:T(8,128)(2,1)S(1)}, u32[]{:S(2)}, u32[]{:S(2)}) collective-permute-start(bf16[128,512]{1,0:T(8,128)(2,1)} %get-tuple-element.27), channel_id=1, source_target_pairs={{0,8},{1,9},{8,0},{9,1},{2,10},{3,11},{10,2},{11,3},{4,12},{5,13},... | collective-permute-start | bytes 393224 | tf_op jit(solution)/shard_map/ppermute | solution.py:276
  7.7 6.4 %collective-permute-start.2 = (bf16[128,512]{1,0:T(8,128)(2,1)}, bf16[128,512]{1,0:T(8,128)(2,1)S(1)}, u32[]{:S(2)}, u32[]{:S(2)}) collective-permute-start(bf16[128,512]{1,0:T(8,128)(2,1)} %get-tuple-element.28), channel_id=1, source_target_pairs={{0,9},{1,8},{8,1},{9,0},{2,11},{3,10},{10,3},{11,2},{4,13},{5,12},... | collective-permute-start | bytes 393224 | tf_op jit(solution)/shard_map/ppermute | solution.py:276
  10.3 10.4 %copy-start.1 = (bf16[128,512]{1,0:T(8,128)(2,1)}, bf16[128,512]{1,0:T(8,128)(2,1)S(1)}, u32[]{:S(2)}) copy-start(bf16[128,512]{1,0:T(8,128)(2,1)S(1)} %collective-permute-done.refs_1_) | copy-start | bytes 393220
  12.9 7.9 %copy-start.2 = (bf16[128,512]{1,0:T(8,128)(2,1)}, bf16[128,512]{1,0:T(8,128)(2,1)S(1)}, u32[]{:S(2)}) copy-start(bf16[128,512]{1,0:T(8,128)(2,1)S(1)} %collective-permute-done.1.refs_2_) | copy-start | bytes 393220
  14.1 6.7 %copy-start.3 = (bf16[128,512]{1,0:T(8,128)(2,1)}, bf16[128,512]{1,0:T(8,128)(2,1)S(1)}, u32[]{:S(2)}) copy-start(bf16[128,512]{1,0:T(8,128)(2,1)S(1)} %collective-permute-done.2.refs_3_) | copy-start | bytes 393220
  14.1 25.4 %all-to-all-start = ((bf16[32,32,512]{2,1,0:T(8,128)(2,1)}), bf16[32,32,512]{2,1,0:T(8,128)(2,1)S(1)}, u32[]{:S(2)}, u32[]{:S(2)}) async-start(bf16[32,32,512]{2,1,0:T(8,128)(2,1)} %get-tuple-element.29), calls=%async_computation | async-start | bytes 2097152 | tf_op jit(solution)/shard_map/all_to_all | solution.py:290
  39.5 4.1 %collective-permute-start.3 = (bf16[32,32,512]{2,1,0:T(8,128)(2,1)S(1)}, bf16[32,32,512]{2,1,0:T(8,128)(2,1)S(1)}, u32[]{:S(2)}, u32[]{:S(2)}) collective-permute-start(bf16[32,32,512]{2,1,0:T(8,128)(2,1)S(1)} %all-to-all-done.own_ref), channel_id=1, source_target_pairs={{0,16},{16,0},{1,17},{17,1},{2,18},{18,2},{3,19},{19,3},{4,20},{20... | collective-permute-start | bytes 3145736 | tf_op jit(solution)/shard_map/ppermute | solution.py:295
  43.7 1.0 copy-start
  98.2 10.5 %collective-permute-start.4 = (f16[32,16,1152]{2,1,0:T(8,128)(2,1)S(1)}, f16[32,16,1152]{2,1,0:T(8,128)(2,1)S(1)}, u32[]{:S(2)}, u32[]{:S(2)}) collective-permute-start(f16[32,16,1152]{2,1,0:T(8,128)(2,1)S(1)} %convert_element_type.52), channel_id=1, source_target_pairs={{0,16},{16,0},{1,17},{17,1},{2,18},{18,2},{3,19},{19,3},{4,20},{20... | collective-permute-start | bytes 3538952 | tf_op jit(solution)/shard_map/ppermute | solution.py:308
